TPU v7x, 256 devices: a whole 4x4x8 slice. The times are simulated.
256 devices in a mesh: gx: 8 (over y, core), gy: 32 (over x, z).
Axes of the slice: x: 4, y: 4, z: 8, core: 2. Of those that a mesh axis runs over, the one named last changes fastest.
Arguments:
- right_side: float32 [2048, 8, 64], P(('gx', 'gy')), may hold values from -6 to 6
- operator_top: float32 [2048, 27, 64, 64], P(('gx', 'gy')), may hold values from -0.078125 to 0.078125
- columns_top: int32 [2048, 27], P(('gx', 'gy')), may hold values from 0 to 2047, as said below
- aggregate_top: int32 [2048], P(('gx', 'gy')), may hold values from 0 to 1023, as said below
- prolong_top: float32 [2048, 64, 64], P(('gx', 'gy')), may hold values from -0.75 to 0.75
- operator_mid: float32 [1024, 27, 64, 64], P(('gx', 'gy')), may hold values from -0.078125 to 0.078125
- columns_mid: int32 [1024, 27], P(('gx', 'gy')), may hold values from 0 to 1023, as said below
- aggregate_mid: int32 [1024], P(('gx', 'gy')), may hold values from 0 to 511, as said below
- prolong_mid: float32 [1024, 64, 64], P(('gx', 'gy')), may hold values from -0.75 to 0.75
- operator_low: float32 [512, 27, 64, 64], P(('gx', 'gy')), may hold values from -0.078125 to 0.078125
- columns_low: int32 [512, 27], P(('gx', 'gy')), may hold values from 0 to 511, as said below
Outputs:
- correction: float32 [2048, 8, 64], P(('gx', 'gy'))
- smoothed_residual: float32 [2048, 8, 64], P(('gx', 'gy'))
Inputs may be any that keep to these rules, and one draw needn't show every extreme that they name: `columns_top`: slot 0 of block row b names b itself; every column of block row b lies on the device of b or on its first level partner. `columns_mid`: slot 0 of block row b names b itself; every column of block row b lies on the device of b or on its second level partner. `columns_low`: slot 0 of block row b names b itself; every column of block row b lies on the device of b or on its third level partner. `aggregate_top`: block row b joins a second level block of the device of b or of its first level partner; counts per block are uneven. `aggregate_mid`: block row b joins a third level block of the device of b or of its second level partner; counts per block are uneven.
All inputs are finite; a program needn't handle non-finite values.
Results may differ from a plain program's by a relative error of at most 0.0001.
Values sent between devices are 32-bit elements; how exact they have to be, the bound alone decides.
No kernel may reach another device: no remote copies, remote signals or barrier semaphores. Data moves between devices by JAX's collectives and lax.ppermute only.
A program may use at most 64 MiB of HBM per device.

v0:
```python
import jax
import jax.numpy as jnp
from jax import lax
from jax.sharding import PartitionSpec as P

center = 1.0
half_width = 0.6


def partner(value, axis, stride):
    mask = 2**stride
    pairs = [(source, source ^ mask) for source in range(lax.axis_size(axis))]
    return lax.ppermute(value, axis, pairs)


def local_index(glob, rows, device):
    owner = glob // rows
    return jnp.where(owner == device, glob % rows, rows + glob % rows)


def apply_rows(operator, local_cols, whole, own):
    gathered = whole[local_cols]
    return own + jnp.einsum("bjik,bjsk->bsi", operator, gathered, precision=lax.Precision.HIGHEST)


def pair_vector(vector, on_y, bit):
    if on_y:
        other = partner(vector, "gy", bit)
    else:
        other = partner(vector, "gx", bit)
    return jnp.concatenate([vector, other], axis=0)


def chebyshev(residual, product):
    sigma = center / half_width
    rho = half_width / center
    solution = jnp.zeros_like(residual)
    direction = residual / center
    for step in range(3):
        solution = solution + direction
        residual = residual - product(direction)
        rho_next = 1.0 / (2.0 * sigma - rho)
        direction = rho_next * rho * direction + 2.0 * rho_next / half_width * residual
        rho = rho_next
    return (solution, residual)


def split_smooth(operator, columns, residual, device, on_y, bit):
    rows = residual.shape[0]
    local_cols = local_index(columns, rows, device)

    def product(direction):
        return apply_rows(operator, local_cols, pair_vector(direction, on_y, bit), direction)

    return chebyshev(residual, product)


def restrict(prolong, aggregate, residual, device, on_y, bit):
    half_rows = residual.shape[0] // 2
    terms = jnp.einsum("bki,bsk->bsi", prolong, residual, precision=lax.Precision.HIGHEST)
    slots = local_index(aggregate, half_rows, device)
    picker = (jnp.arange(2 * half_rows, dtype=jnp.int32)[:, None] == slots[None, :]).astype(
        jnp.float32
    )
    partial_sums = jnp.einsum("cb,bsi->csi", picker, terms, precision=lax.Precision.HIGHEST)
    if on_y:
        arrived = partner(partial_sums[half_rows:], "gy", bit)
    else:
        arrived = partner(partial_sums[half_rows:], "gx", bit)
    return partial_sums[:half_rows] + arrived


def prolongate(prolong, aggregate, fine, coarse_values, device, on_y, bit):
    half_rows = coarse_values.shape[0]
    if on_y:
        other = partner(coarse_values, "gy", bit)
    else:
        other = partner(coarse_values, "gx", bit)
    whole = jnp.concatenate([coarse_values, other], axis=0)
    picked = whole[local_index(aggregate, half_rows, device)]
    return fine + jnp.einsum("bik,bsk->bsi", prolong, picked, precision=lax.Precision.HIGHEST)


def per_device(
    right_side,
    operator_top,
    columns_top,
    aggregate_top,
    prolong_top,
    operator_mid,
    columns_mid,
    aggregate_mid,
    prolong_mid,
    operator_low,
    columns_low,
):
    device = lax.axis_index("gx") * lax.axis_size("gy") + lax.axis_index("gy")
    width_y = lax.axis_size("gy").bit_length() - 1
    width_x = lax.axis_size("gx").bit_length() - 1
    top_bit = width_y - 1
    mid_bit = width_x - 1
    low_bit = width_y - 2
    x_top, smoothed = split_smooth(operator_top, columns_top, right_side, device, True, top_bit)
    mid_side = restrict(prolong_top, aggregate_top, smoothed, device, True, top_bit)
    x_mid, r_mid = split_smooth(operator_mid, columns_mid, mid_side, device, False, mid_bit)
    low_side = restrict(prolong_mid, aggregate_mid, r_mid, device, False, mid_bit)
    x_low, r_low = split_smooth(operator_low, columns_low, low_side, device, True, low_bit)
    mid_fixed = prolongate(prolong_mid, aggregate_mid, x_mid, x_low, device, False, mid_bit)
    correction = prolongate(prolong_top, aggregate_top, x_top, mid_fixed, device, True, top_bit)
    return (correction, smoothed)


def solution(mesh):
    in_specs = (
        P(("gx", "gy"), None, None),
        P(("gx", "gy"), None, None, None),
        P(("gx", "gy"), None),
        P(("gx", "gy")),
        P(("gx", "gy"), None, None),
        P(("gx", "gy"), None, None, None),
        P(("gx", "gy"), None),
        P(("gx", "gy")),
        P(("gx", "gy"), None, None),
        P(("gx", "gy"), None, None, None),
        P(("gx", "gy"), None),
    )
    out_specs = (P(("gx", "gy"), None, None), P(("gx", "gy"), None, None))
    return jax.shard_map(
        per_device, mesh=mesh, in_specs=in_specs, out_specs=out_specs, check_vma=False
    )
```

profile of v0, /device:TPU:128, one launch (start us, length us, event | category | flops | bytes accessed | tf_op | source)
XLA Modules:
  0.0 141.4 jit_solution(17958121827125799560)
XLA Ops:
  0.6 3.1 %collective-permute-start = (f32[8,8,64]{2,1,0:T(8,128)}, f32[8,8,64]{2,1,0:T(8,128)}, u32[]{:S(2)}, u32[]{:S(2)}) collective-permute-start(f32[8,8,64]{2,1,0:T(8,128)} %param.11), channel_id=1, source_target_pairs={{0,16},{1,17},{2,18},{3,19},{4,20},{5,21},{6,22},{7,23},{8,24},{9,... | collective-permute-start | bytes 49160 | tf_op jit(solution)/shard_map/ppermute | solution.py:13
  4.5 1.9 %collective-permute-done = f32[8,8,64]{2,1,0:T(8,128)} collective-permute-done((f32[8,8,64]{2,1,0:T(8,128)}, f32[8,8,64]{2,1,0:T(8,128)}, u32[]{:S(2)}, u32[]{:S(2)}) %collective-permute-start) | collective-permute-done | bytes 16416 | tf_op jit(solution)/shard_map/ppermute | solution.py:13
  7.9 2.5 %gather_fusion = f32[216,8,64]{2,1,0:T(8,128)} fusion(f32[16,8,64]{2,1,0:T(8,128)} %pad_maximum_fusion, s32[1024]{0:T(1024)S(1)} %pad_clamp_fusion.4), kind=kCustom, calls=%fused_computation | custom fusion | bytes 885600 | tf_op jit(solution)/shard_map/gather | solution.py:22
  10.3 8.8 %multiply_add_fusion.1 = (f32[8,8,64]{2,1,0:T(8,128)S(1)}, f32[8,8,64]{2,1,0:T(8,128)}) fusion(f32[8,8,64]{2,1,0:T(8,128)} %param.11, f32[8,27,8,64]{3,2,1,0:T(8,128)} %bitcast.86, f32[8,27,64,64]{3,2,1,0:T(8,128)} %param.12), kind=kOutput, calls=%fused_computation.40 | convolution fusion | flops 84955136 | bytes 4030464 | tf_op jit(solution)/shard_map/bjik,bjsk->bsi/dot_general | solution.py:23
  19.2 3.0 %collective-permute-start.1 = (f32[8,8,64]{2,1,0:T(8,128)S(1)}, f32[8,8,64]{2,1,0:T(8,128)S(1)}, u32[]{:S(2)}, u32[]{:S(2)}) collective-permute-start(f32[8,8,64]{2,1,0:T(8,128)S(1)} %get-tuple-element.8), channel_id=1, source_target_pairs={{0,16},{1,17},{2,18},{3,19},{4,20},{5,21},{6,22},{7,23},{8,24},{9,... | collective-permute-start | bytes 49160 | tf_op jit(solution)/shard_map/ppermute | solution.py:13
  22.2 2.4 %collective-permute-done.1 = f32[8,8,64]{2,1,0:T(8,128)S(1)} collective-permute-done((f32[8,8,64]{2,1,0:T(8,128)S(1)}, f32[8,8,64]{2,1,0:T(8,128)S(1)}, u32[]{:S(2)}, u32[]{:S(2)}) %collective-permute-start.1) | collective-permute-done | bytes 16416 | tf_op jit(solution)/shard_map/ppermute | solution.py:13
  25.2 2.5 %gather_fusion.1 = f32[216,8,64]{2,1,0:T(8,128)} fusion(f32[16,8,64]{2,1,0:T(8,128)} %pad_maximum_fusion.1, s32[1024]{0:T(1024)S(1)} %pad_clamp_fusion.4), kind=kCustom, calls=%fused_computation.1 | custom fusion | bytes 885600 | tf_op jit(solution)/shard_map/gather | solution.py:22
  27.7 8.8 %multiply_add_fusion = (f32[8,8,64]{2,1,0:T(8,128)S(1)}, f32[8,8,64]{2,1,0:T(8,128)}) fusion(f32[8,8,64]{2,1,0:T(8,128)} %copy-done.2, f32[8,8,64]{2,1,0:T(8,128)} %get-tuple-element.9, f32[8,27,8,64]{3,2,1,0:T(8,128)} %bitcast.85, f32[8,27,64,64]{3,2,1,0:T(8,128)} %param.12), kind=kOutput, calls=%fused_computation.39 | convolution fusion | flops 84955136 | bytes 4046848 | tf_op jit(solution)/shard_map/bjik,bjsk->bsi/dot_general | solution.py:23
  36.5 3.0 %collective-permute-start.2 = (f32[8,8,64]{2,1,0:T(8,128)S(1)}, f32[8,8,64]{2,1,0:T(8,128)S(1)}, u32[]{:S(2)}, u32[]{:S(2)}) collective-permute-start(f32[8,8,64]{2,1,0:T(8,128)S(1)} %get-tuple-element.10), channel_id=1, source_target_pairs={{0,16},{1,17},{2,18},{3,19},{4,20},{5,21},{6,22},{7,23},{8,24},{9,... | collective-permute-start | bytes 49160 | tf_op jit(solution)/shard_map/ppermute | solution.py:13
  40.1 1.8 %collective-permute-done.2 = f32[8,8,64]{2,1,0:T(8,128)S(1)} collective-permute-done((f32[8,8,64]{2,1,0:T(8,128)S(1)}, f32[8,8,64]{2,1,0:T(8,128)S(1)}, u32[]{:S(2)}, u32[]{:S(2)}) %collective-permute-start.2) | collective-permute-done | bytes 16416 | tf_op jit(solution)/shard_map/ppermute | solution.py:13
  42.6 2.5 %gather_fusion.2 = f32[216,8,64]{2,1,0:T(8,128)} fusion(f32[16,8,64]{2,1,0:T(8,128)} %pad_maximum_fusion.2, s32[1024]{0:T(1024)S(1)} %pad_clamp_fusion.4), kind=kCustom, calls=%fused_computation.2 | custom fusion | bytes 885600 | tf_op jit(solution)/shard_map/gather | solution.py:22
  45.1 8.2 %fusion.1 = f32[8,8,64]{2,1,0:T(8,128)S(1)} fusion(f32[8,8,64]{2,1,0:T(8,128)} %get-tuple-element.11, f32[8,27,8,64]{3,2,1,0:T(8,128)} %bitcast.87, f32[8,27,64,64]{3,2,1,0:T(8,128)} %param.12, f32[8,8,64]{2,1,0:T(8,128)} %copy-done.2), kind=kOutput, calls=%fused_computation.13 | convolution fusion | flops 84955136 | bytes 4030464 | tf_op jit(solution)/shard_map/bjik,bjsk->bsi/dot_general | solution.py:23
  54.7 3.0 %collective-permute-start.3 = (f32[4,8,64]{2,0,1:T(4,128)S(1)}, f32[4,8,64]{2,0,1:T(4,128)}, u32[]{:S(2)}, u32[]{:S(2)}) collective-permute-start(f32[4,8,64]{2,0,1:T(4,128)S(1)} %slice.37), channel_id=1, source_target_pairs={{0,16},{1,17},{2,18},{3,19},{4,20},{5,21},{6,22},{7,23},{8,24},{9,... | collective-permute-start | bytes 24584 | tf_op jit(solution)/shard_map/ppermute | solution.py:13
  60.8 3.4 %collective-permute-start.4 = (f32[4,8,64]{2,0,1:T(4,128)S(1)}, f32[4,8,64]{2,0,1:T(4,128)S(1)}, u32[]{:S(2)}, u32[]{:S(2)}) collective-permute-start(f32[4,8,64]{2,0,1:T(4,128)S(1)} %slice_add_fusion), channel_id=1, source_target_pairs={{0,128},{32,160},{64,192},{96,224},{128,0},{160,32},{192,64},{224,... | collective-permute-start | bytes 24584 | tf_op jit(solution)/shard_map/ppermute | solution.py:13
  66.9 2.3 %gather_fusion.3 = f32[108,8,64]{2,1,0:T(8,128)} fusion(f32[8,8,64]{2,1,0:T(8,128)} %copy.37, s32[1024]{0:T(1024)} %pad_clamp_fusion.3), kind=kCustom, calls=%fused_computation.3 | custom fusion | bytes 442800 | tf_op jit(solution)/shard_map/gather | solution.py:22
  69.2 4.0 %convolution_bitcast_fusion.5 = f32[4,8,64]{2,1,0:T(8,128)S(1)} fusion(f32[4,27,8,64]{3,2,1,0:T(8,128)} %bitcast.89, f32[4,27,64,64]{3,2,1,0:T(8,128)S(1)} %copy-done), kind=kOutput, calls=%fused_computation.22 | convolution fusion | flops 42467328 | bytes 1998848 | tf_op jit(solution)/shard_map/bjik,bjsk->bsi/dot_general | solution.py:23
  73.8 3.3 %collective-permute-start.5 = (f32[4,8,64]{2,0,1:T(4,128)S(1)}, f32[4,8,64]{2,0,1:T(4,128)S(1)}, u32[]{:S(2)}, u32[]{:S(2)}) collective-permute-start(f32[4,8,64]{2,0,1:T(4,128)S(1)} %multiply_add_fusion.3), channel_id=1, source_target_pairs={{0,128},{32,160},{64,192},{96,224},{128,0},{160,32},{192,64},{224,... | collective-permute-start | bytes 24584 | tf_op jit(solution)/shard_map/ppermute | solution.py:13
  77.1 2.0 %collective-permute-done.5 = f32[4,8,64]{2,0,1:T(4,128)S(1)} collective-permute-done((f32[4,8,64]{2,0,1:T(4,128)S(1)}, f32[4,8,64]{2,0,1:T(4,128)S(1)}, u32[]{:S(2)}, u32[]{:S(2)}) %collective-permute-start.5) | collective-permute-done | bytes 8224 | tf_op jit(solution)/shard_map/ppermute | solution.py:13
  79.8 2.3 %gather_fusion.4 = f32[108,8,64]{2,1,0:T(8,128)} fusion(f32[8,8,64]{2,1,0:T(8,128)} %copy.39, s32[1024]{0:T(1024)} %pad_clamp_fusion.3), kind=kCustom, calls=%fused_computation.4 | custom fusion | bytes 442800 | tf_op jit(solution)/shard_map/gather | solution.py:22
  82.1 4.0 %convolution_bitcast_fusion.4 = f32[4,8,64]{2,1,0:T(8,128)S(1)} fusion(f32[4,27,8,64]{3,2,1,0:T(8,128)} %bitcast.90, f32[4,27,64,64]{3,2,1,0:T(8,128)S(1)} %copy-done), kind=kOutput, calls=%fused_computation.21 | convolution fusion | flops 42467328 | bytes 1998848 | tf_op jit(solution)/shard_map/bjik,bjsk->bsi/dot_general | solution.py:23
  86.7 3.2 %collective-permute-start.6 = (f32[4,8,64]{2,0,1:T(4,128)S(1)}, f32[4,8,64]{2,0,1:T(4,128)S(1)}, u32[]{:S(2)}, u32[]{:S(2)}) collective-permute-start(f32[4,8,64]{2,0,1:T(4,128)S(1)} %multiply_add_fusion.2), channel_id=1, source_target_pairs={{0,128},{32,160},{64,192},{96,224},{128,0},{160,32},{192,64},{224,... | collective-permute-start | bytes 24584 | tf_op jit(solution)/shard_map/ppermute | solution.py:13
  92.6 2.3 %gather_fusion.5 = f32[108,8,64]{2,1,0:T(8,128)} fusion(f32[8,8,64]{2,1,0:T(8,128)} %copy.41, s32[1024]{0:T(1024)} %pad_clamp_fusion.3), kind=kCustom, calls=%fused_computation.5 | custom fusion | bytes 442800 | tf_op jit(solution)/shard_map/gather | solution.py:22
  94.9 4.0 %convolution_bitcast_fusion.3 = f32[4,8,64]{2,1,0:T(8,128)S(1)} fusion(f32[4,27,8,64]{3,2,1,0:T(8,128)} %bitcast.88, f32[4,27,64,64]{3,2,1,0:T(8,128)S(1)} %copy-done), kind=kOutput, calls=%fused_computation.20 | convolution fusion | flops 42467328 | bytes 1998848 | tf_op jit(solution)/shard_map/bjik,bjsk->bsi/dot_general | solution.py:23
  100.0 3.2 %collective-permute-start.7 = (f32[2,8,64]{2,1,0:T(8,128)}, f32[2,8,64]{2,1,0:T(8,128)S(1)}, u32[]{:S(2)}, u32[]{:S(2)}) collective-permute-start(f32[2,8,64]{2,1,0:T(8,128)} %copy.58), channel_id=1, source_target_pairs={{0,128},{32,160},{64,192},{96,224},{128,0},{160,32},{192,64},{224,... | collective-permute-start | bytes 12296 | tf_op jit(solution)/shard_map/ppermute | solution.py:13
  110.4 3.6 %multiply_add_fusion.4 = (f32[2,8,64]{2,1,0:T(8,128)S(1)}, f32[2,8,64]{2,1,0:T(8,128)}) fusion(f32[2,8,64]{2,1,0:T(8,128)} %copy-done.11, f32[2,27,8,64]{3,2,1,0:T(8,128)} %bitcast.92, f32[2,27,64,64]{3,2,1,0:T(8,128)} %param.20), kind=kOutput, calls=%fused_computation.60 | convolution fusion | flops 21238784 | bytes 1007616 | tf_op jit(solution)/shard_map/bjik,bjsk->bsi/dot_general | solution.py:23
  115.6 2.2 %collective-permute-done.9 = f32[2,8,64]{2,1,0:T(8,128)S(1)} collective-permute-done((f32[2,8,64]{2,1,0:T(8,128)S(1)}, f32[2,8,64]{2,1,0:T(8,128)S(1)}, u32[]{:S(2)}, u32[]{:S(2)}) %collective-permute-start.9) | collective-permute-done | bytes 4128 | tf_op jit(solution)/shard_map/ppermute | solution.py:13
  119.1 3.0 %add_add_fusion = f32[2,8,64]{2,1,0:T(8,128)S(1)} fusion(f32[2,8,64]{2,1,0:T(8,128)} %copy-done.11, f32[2,8,64]{2,1,0:T(8,128)} %get-tuple-element.13, f32[2,27,8,64]{3,2,1,0:T(8,128)} %bitcast.91, f32[2,27,64,64]{3,2,1,0:T(8,128)} %param.20), kind=kOutput, calls=%fused_computation.59 | convolution fusion | flops 21243904 | bytes 1007616 | tf_op jit(solution)/shard_map/bjik,bjsk->bsi/dot_general | solution.py:23
  122.2 3.3 %collective-permute-start.10 = (f32[2,8,64]{2,1,0:T(8,128)S(1)}, f32[2,8,64]{2,1,0:T(8,128)S(1)}, u32[]{:S(2)}, u32[]{:S(2)}) collective-permute-start(f32[2,8,64]{2,1,0:T(8,128)S(1)} %add_add_fusion), channel_id=1, source_target_pairs={{0,128},{32,160},{64,192},{96,224},{128,0},{160,32},{192,64},{224,... | collective-permute-start | bytes 12296 | tf_op jit(solution)/shard_map/ppermute | solution.py:13
  131.4 3.1 %collective-permute-start.11 = (f32[4,8,64]{2,0,1:T(4,128)S(1)}, f32[4,8,64]{2,0,1:T(4,128)S(1)}, u32[]{:S(2)}, u32[]{:S(2)}) collective-permute-start(f32[4,8,64]{2,0,1:T(4,128)S(1)} %copy_add_fusion), channel_id=1, source_target_pairs={{0,16},{1,17},{2,18},{3,19},{4,20},{5,21},{6,22},{7,23},{8,24},{9,... | collective-permute-start | bytes 24584 | tf_op jit(solution)/shard_map/ppermute | solution.py:13
  135.2 1.6 %collective-permute-done.11 = f32[4,8,64]{2,0,1:T(4,128)S(1)} collective-permute-done((f32[4,8,64]{2,0,1:T(4,128)S(1)}, f32[4,8,64]{2,0,1:T(4,128)S(1)}, u32[]{:S(2)}, u32[]{:S(2)}) %collective-permute-start.11) | collective-permute-done | bytes 8224 | tf_op jit(solution)/shard_map/ppermute | solution.py:13
  137.4 1.9 %gather_fusion.9 = f32[8,8,64]{2,1,0:T(8,128)} fusion(f32[8,8,64]{2,1,0:T(8,128)} %copy.48, s32[1024]{0:T(1024)S(1)} %pad_clamp_fusion), kind=kCustom, calls=%fused_computation.9 | custom fusion | bytes 32800 | tf_op jit(solution)/shard_map/gather | solution.py:80
  139.3 2.1 %convolution_add_fusion = f32[8,8,64]{2,1,0:T(8,128)} fusion(f32[8,8,64]{2,1,0:T(8,128)} %gather_fusion.9, f32[8,64,64]{2,1,0:T(8,128)} %param.15, f32[8,8,64]{2,1,0:T(8,128)} %param.11, f32[8,8,64]{2,1,0:T(8,128)} %copy-done.2, f32[8,8,64]{2,1,0:T(8,128)} %get-tuple-element.11), kind=kOutput, calls=%fused_computation.10 | convolution fusion | flops 3170304 | bytes 212992 | tf_op jit(solution)/shard_map/bik,bsk->bsi/dot_general | solution.py:81
  (88 shorter events, 34.1 us)
Async XLA Ops:
  0.6 68.6 %copy-start = (f32[4,27,64,64]{3,2,1,0:T(8,128)S(1)}, f32[4,27,64,64]{3,2,1,0:T(8,128)}, u32[]{:S(2)}) copy-start(f32[4,27,64,64]{3,2,1,0:T(8,128)} %param.16) | copy-start | bytes 5308420
  0.6 5.8 %collective-permute-start = (f32[8,8,64]{2,1,0:T(8,128)}, f32[8,8,64]{2,1,0:T(8,128)}, u32[]{:S(2)}, u32[]{:S(2)}) collective-permute-start(f32[8,8,64]{2,1,0:T(8,128)} %param.11), channel_id=1, source_target_pairs={{0,16},{1,17},{2,18},{3,19},{4,20},{5,21},{6,22},{7,23},{8,24},{9,... | collective-permute-start | bytes 49160 | tf_op jit(solution)/shard_map/ppermute | solution.py:13
  19.2 5.4 %copy-start.2 = (f32[8,8,64]{2,1,0:T(8,128)}, f32[8,8,64]{2,1,0:T(8,128)S(1)}, u32[]{:S(2)}) copy-start(f32[8,8,64]{2,1,0:T(8,128)S(1)} %get-tuple-element.8) | copy-start | bytes 49156
  19.2 5.4 %collective-permute-start.1 = (f32[8,8,64]{2,1,0:T(8,128)S(1)}, f32[8,8,64]{2,1,0:T(8,128)S(1)}, u32[]{:S(2)}, u32[]{:S(2)}) collective-permute-start(f32[8,8,64]{2,1,0:T(8,128)S(1)} %get-tuple-element.8), channel_id=1, source_target_pairs={{0,16},{1,17},{2,18},{3,19},{4,20},{5,21},{6,22},{7,23},{8,24},{9,... | collective-permute-start | bytes 49160 | tf_op jit(solution)/shard_map/ppermute | solution.py:13
  27.7 11.9 %copy-start.16 = (s32[8]{0:T(128)S(1)}, s32[8]{0:T(128)}, u32[]{:S(2)}) copy-start(s32[8]{0:T(128)} %param.14) | copy-start | bytes 100
  36.5 5.4 %collective-permute-start.2 = (f32[8,8,64]{2,1,0:T(8,128)S(1)}, f32[8,8,64]{2,1,0:T(8,128)S(1)}, u32[]{:S(2)}, u32[]{:S(2)}) collective-permute-start(f32[8,8,64]{2,1,0:T(8,128)S(1)} %get-tuple-element.10), channel_id=1, source_target_pairs={{0,16},{1,17},{2,18},{3,19},{4,20},{5,21},{6,22},{7,23},{8,24},{9,... | collective-permute-start | bytes 49160 | tf_op jit(solution)/shard_map/ppermute | solution.py:13
  45.1 8.3 %copy-start.1 = (f32[8,64,64]{2,1,0:T(8,128)S(1)}, f32[8,64,64]{2,1,0:T(8,128)}, u32[]{:S(2)}) copy-start(f32[8,64,64]{2,1,0:T(8,128)} %param.15) | copy-start | bytes 393220
  45.1 12.7 %copy-start.14 = (s32[4,27]{1,0:T(4,128)S(1)}, s32[4,27]{1,0:T(4,128)}, u32[]{:S(2)}) copy-start(s32[4,27]{1,0:T(4,128)} %param.17) | copy-start | bytes 1300
  53.3 0.6 copy-start.10
  54.1 0.6 copy-start.12
  54.7 5.3 %collective-permute-start.3 = (f32[4,8,64]{2,0,1:T(4,128)S(1)}, f32[4,8,64]{2,0,1:T(4,128)}, u32[]{:S(2)}, u32[]{:S(2)}) collective-permute-start(f32[4,8,64]{2,0,1:T(4,128)S(1)} %slice.37), channel_id=1, source_target_pairs={{0,16},{1,17},{2,18},{3,19},{4,20},{5,21},{6,22},{7,23},{8,24},{9,... | collective-permute-start | bytes 24584 | tf_op jit(solution)/shard_map/ppermute | solution.py:13
  60.8 38.1 %copy-start.3 = (f32[4,8,64]{2,0,1:T(4,128)}, f32[4,8,64]{2,0,1:T(4,128)S(1)}, u32[]{:S(2)}) copy-start(f32[4,8,64]{2,0,1:T(4,128)S(1)} %slice_add_fusion) | copy-start | bytes 24580
  60.8 5.5 %collective-permute-start.4 = (f32[4,8,64]{2,0,1:T(4,128)S(1)}, f32[4,8,64]{2,0,1:T(4,128)S(1)}, u32[]{:S(2)}, u32[]{:S(2)}) collective-permute-start(f32[4,8,64]{2,0,1:T(4,128)S(1)} %slice_add_fusion), channel_id=1, source_target_pairs={{0,128},{32,160},{64,192},{96,224},{128,0},{160,32},{192,64},{224,... | collective-permute-start | bytes 24584 | tf_op jit(solution)/shard_map/ppermute | solution.py:13
  73.2 0.6 copy-start.5
  73.8 5.3 %collective-permute-start.5 = (f32[4,8,64]{2,0,1:T(4,128)S(1)}, f32[4,8,64]{2,0,1:T(4,128)S(1)}, u32[]{:S(2)}, u32[]{:S(2)}) collective-permute-start(f32[4,8,64]{2,0,1:T(4,128)S(1)} %multiply_add_fusion.3), channel_id=1, source_target_pairs={{0,128},{32,160},{64,192},{96,224},{128,0},{160,32},{192,64},{224,... | collective-permute-start | bytes 24584 | tf_op jit(solution)/shard_map/ppermute | solution.py:13
  82.1 4.0 %copy-start.6 = (f32[4,8,64]{2,1,0:T(8,128)S(1)}, f32[4,8,64]{2,1,0:T(8,128)}, u32[]{:S(2)}) copy-start(f32[4,8,64]{2,1,0:T(8,128)} %copy-done.5) | copy-start | bytes 24580
  82.1 7.8 %copy-start.17 = (s32[4]{0:T(128)S(1)}, s32[4]{0:T(128)}, u32[]{:S(2)}) copy-start(s32[4]{0:T(128)} %param.18) | copy-start | bytes 52
  86.1 0.6 copy-start.8
  86.7 5.2 %collective-permute-start.6 = (f32[4,8,64]{2,0,1:T(4,128)S(1)}, f32[4,8,64]{2,0,1:T(4,128)S(1)}, u32[]{:S(2)}, u32[]{:S(2)}) collective-permute-start(f32[4,8,64]{2,0,1:T(4,128)S(1)} %multiply_add_fusion.2), channel_id=1, source_target_pairs={{0,128},{32,160},{64,192},{96,224},{128,0},{160,32},{192,64},{224,... | collective-permute-start | bytes 24584 | tf_op jit(solution)/shard_map/ppermute | solution.py:13
  94.9 4.1 %copy-start.7 = (f32[4,8,64]{2,1,0:T(8,128)S(1)}, f32[4,8,64]{2,1,0:T(8,128)}, u32[]{:S(2)}) copy-start(f32[4,8,64]{2,1,0:T(8,128)} %copy-done.5) | copy-start | bytes 24580
  94.9 4.1 %copy-start.9 = (f32[4,8,64]{2,1,0:T(8,128)S(1)}, f32[4,8,64]{2,1,0:T(8,128)}, u32[]{:S(2)}) copy-start(f32[4,8,64]{2,1,0:T(8,128)} %copy-done.8) | copy-start | bytes 24580
  94.9 4.1 %copy-start.4 = (f32[4,64,64]{2,1,0:T(8,128)S(1)}, f32[4,64,64]{2,1,0:T(8,128)}, u32[]{:S(2)}) copy-start(f32[4,64,64]{2,1,0:T(8,128)} %param.19) | copy-start | bytes 196612
  94.9 4.3 %copy-start.13 = (s32[4]{0:T(128)S(1)}, s32[4]{0:T(128)}, u32[]{:S(2)}) copy-start(s32[4]{0:T(128)} %get-tuple-element.5) | copy-start | bytes 52
  94.9 8.3 %copy-start.15 = (s32[2,27]{1,0:T(2,128)S(1)}, s32[2,27]{1,0:T(2,128)}, u32[]{:S(2)}) copy-start(s32[2,27]{1,0:T(2,128)} %param.21) | copy-start | bytes 652
  100.0 5.4 %collective-permute-start.7 = (f32[2,8,64]{2,1,0:T(8,128)}, f32[2,8,64]{2,1,0:T(8,128)S(1)}, u32[]{:S(2)}, u32[]{:S(2)}) collective-permute-start(f32[2,8,64]{2,1,0:T(8,128)} %copy.58), channel_id=1, source_target_pairs={{0,128},{32,160},{64,192},{96,224},{128,0},{160,32},{192,64},{224,... | collective-permute-start | bytes 12296 | tf_op jit(solution)/shard_map/ppermute | solution.py:13
  105.4 3.7 %copy-start.11 = (f32[2,8,64]{2,1,0:T(8,128)}, f32[2,8,64]{2,1,0:T(8,128)S(1)}, u32[]{:S(2)}) copy-start(f32[2,8,64]{2,1,0:T(8,128)S(1)} %copy_add_fusion.3) | copy-start | bytes 12292
  105.4 3.7 %collective-permute-start.8 = (f32[2,8,64]{2,1,0:T(8,128)S(1)}, f32[2,8,64]{2,1,0:T(8,128)S(1)}, u32[]{:S(2)}, u32[]{:S(2)}) collective-permute-start(f32[2,8,64]{2,1,0:T(8,128)S(1)} %copy_add_fusion.3), channel_id=1, source_target_pairs={{0,8},{1,9},{2,10},{3,11},{4,12},{5,13},{6,14},{7,15},{8,0},{9,1},... | collective-permute-start | bytes 12296 | tf_op jit(solution)/shard_map/ppermute | solution.py:13
  114.1 3.7 %collective-permute-start.9 = (f32[2,8,64]{2,1,0:T(8,128)S(1)}, f32[2,8,64]{2,1,0:T(8,128)S(1)}, u32[]{:S(2)}, u32[]{:S(2)}) collective-permute-start(f32[2,8,64]{2,1,0:T(8,128)S(1)} %get-tuple-element.12), channel_id=1, source_target_pairs={{0,8},{1,9},{2,10},{3,11},{4,12},{5,13},{6,14},{7,15},{8,0},{9,1},... | collective-permute-start | bytes 12296 | tf_op jit(solution)/shard_map/ppermute | solution.py:13
  122.2 5.2 %collective-permute-start.10 = (f32[2,8,64]{2,1,0:T(8,128)S(1)}, f32[2,8,64]{2,1,0:T(8,128)S(1)}, u32[]{:S(2)}, u32[]{:S(2)}) collective-permute-start(f32[2,8,64]{2,1,0:T(8,128)S(1)} %add_add_fusion), channel_id=1, source_target_pairs={{0,128},{32,160},{64,192},{96,224},{128,0},{160,32},{192,64},{224,... | collective-permute-start | bytes 12296 | tf_op jit(solution)/shard_map/ppermute | solution.py:13
  131.4 5.3 %collective-permute-start.11 = (f32[4,8,64]{2,0,1:T(4,128)S(1)}, f32[4,8,64]{2,0,1:T(4,128)S(1)}, u32[]{:S(2)}, u32[]{:S(2)}) collective-permute-start(f32[4,8,64]{2,0,1:T(4,128)S(1)} %copy_add_fusion), channel_id=1, source_target_pairs={{0,16},{1,17},{2,18},{3,19},{4,20},{5,21},{6,22},{7,23},{8,24},{9,... | collective-permute-start | bytes 24584 | tf_op jit(solution)/shard_map/ppermute | solution.py:13
where the time goes:
time: 143 us; the launch traced here: 141 us
  matrix products  48.7 us (34%)
  starting transfers between devices  34.7 us (24%)
  local copies, waits for them, and re-layouts  28.3 us (20%)
  waiting for transfers between devices  16.5 us (12%)
  other arithmetic  12.4 us (9%)
    dot_general x8, matrix products, apply_rows(): jnp.einsum('bjik,bjsk->bsi', operator, gathered, precision=lax.Precision....  44.6 us
    ppermute x12, starting transfers between devices, partner(): return lax.ppermute(value, axis, pairs)  34.7 us
    gather x8, local copies, waits for them, and re-layouts, apply_rows(): gathered = whole[local_cols]  17.1 us
    ppermute x12, waiting for transfers between devices, partner(): return lax.ppermute(value, axis, pairs)  16.5 us
    dot_general x2, matrix products, prolongate(): jnp.einsum('bik,bsk->bsi', prolong, picked, precision=lax.Precision.HIGHEST)  3.29 us
    gather x2, local copies, waits for them, and re-layouts, prolongate(): picked = whole[local_index(aggregate, half_rows, device)]  3.29 us
  transfers between devices with their start and end apart: 12, of which 12 were waited for; matrix products, arithmetic and copies ran while one was open for 7% of the time, Pallas kernels for 0%

commit v1 on v0

v1 whole, which is shorter than its diff:
```python
import functools

import jax
import jax.numpy as jnp
from jax import lax
from jax.experimental import pallas as pl
from jax.experimental.pallas import tpu as pltpu
from jax.sharding import PartitionSpec as P

center = 1.0
half_width = 0.6
F32 = jnp.float32
BF16 = jnp.bfloat16
N = 64
S = 8
J = 27


def chebyshev_weights():
    sigma = center / half_width
    rho = half_width / center
    weights = []
    for step in range(3):
        rho_next = 1.0 / (2.0 * sigma - rho)
        weights.append((rho_next * rho, 2.0 * rho_next / half_width))
        rho = rho_next
    return weights


W = chebyshev_weights()
COST = {"pack_side": 20000, "prepare_top": 4000, "step_second": 100000, "step_third": 6000, "add_mid": 6000}


def call(name, body, outs, *args, scalars=0):
    spaces = [pltpu.SMEM] * scalars + [pltpu.VMEM] * (len(args) - scalars)
    args = [pltpu.with_memory_space_constraint(a, m) for a, m in zip(args, spaces)]
    return pl.pallas_call(
        body,
        name=name,
        out_shape=[pltpu.VMEM(shape, dtype) for shape, dtype in outs],
        in_specs=[pl.BlockSpec(memory_space=m) for m in spaces],
        out_specs=[pl.BlockSpec(memory_space=pltpu.VMEM)] * len(outs),
        cost_estimate=pl.CostEstimate(flops=COST.get(name, 200) * 1000000, bytes_accessed=0, transcendentals=0),
        compiler_params=pltpu.CompilerParams(vmem_limit_bytes=8 * 1024 * 1024),
    )(*args)


def split(value):
    high = value.astype(BF16)
    return high, (value - high.astype(F32)).astype(BF16)


def stack(value):
    return jnp.concatenate(split(value), axis=0)


def fold(value):
    return value[:S] + value[S:]


def apply_t(vector, matrix):
    both = stack(vector)
    both = jnp.concatenate([both, both], axis=1)
    out = lax.dot_general(both, matrix, (((1,), (1,)), ((), ())), preferred_element_type=F32)
    return fold(out)


def apply_n(vector, matrix):
    out = fold(lax.dot_general(stack(vector), matrix, (((1,), (0,)), ((), ())), preferred_element_type=F32))
    half = out.shape[1] // 2
    return out[:, :half] + out[:, half:]


def pack(ref):
    return jnp.concatenate([ref[b] for b in range(ref.shape[0])], axis=1)


def unpack(value, ref):
    for b in range(ref.shape[0]):
        ref[b] = value[:, b * N : (b + 1) * N]


def local(index, rows, device):
    return (index % rows) + jnp.where(index // rows == device, 0, rows)


def collapse_rows(cols, b, rows, device, blocks, sums):
    for part in sums:
        part[...] = jnp.zeros(part.shape, F32)
    for j in range(J):
        for n, part in enumerate(sums):
            at = local(cols[b + n, j], rows, device)
            part[at] = part[at] + blocks[b + n, j]


def pair_of(sums, at):
    return jnp.concatenate([sums[at], sums[at + 1]], axis=1)


def spread_row(agg, b, rows, device, prolong):
    at = local(agg[b], rows, device)
    block = prolong[b]
    twice = jnp.concatenate([block, block], axis=1)
    lane = lax.broadcasted_iota(jnp.int32, (N, 2 * N), 1) // N
    return [jnp.where(lane + 2 * piece == at, twice, 0.0) for piece in range(rows)]


def put_halves(ref, rows_at, pieces):
    half = len(pieces) // 2
    width = half * 2 * N
    for p, piece in enumerate(pieces):
        high, low = split(piece)
        base = (p // half) * 2 * width + (p % half) * 2 * N
        ref[rows_at, pl.ds(base, 2 * N)] = high
        ref[rows_at, pl.ds(base + width, 2 * N)] = low


def pack_side(side, out):
    out[...] = pack(side)


def lanes_of(b):
    return pl.ds(pl.multiple_of(b * N, N), N)


def prepare_top(cols, blocks, first, matrix, product, *sums):
    rows = blocks.shape[0]
    device = cols[0, 0] // rows

    def some(step, carry):
        b = step * len(sums)
        collapse_rows(cols, b, rows, device, blocks, sums)
        for n, part in enumerate(sums):
            put_halves(matrix, lanes_of(b + n), [pair_of(part, 2 * c) for c in range(rows)])
        return carry

    lax.fori_loop(0, rows // len(sums), some, 0)
    product[...] = apply_t(first[...], matrix[:, : 2 * rows * N])


def collapse_out(cols, blocks, out, sums):
    rows = blocks.shape[0]
    device = cols[0, 0] // rows
    sums = [part.at[: 2 * rows] for part in sums]

    def some(step, carry):
        b = step * len(sums)
        collapse_rows(cols, b, rows, device, blocks, sums)
        for n, part in enumerate(sums):
            for c in range(rows):
                out[lanes_of(b + n), pl.ds(c * 2 * N, 2 * N)] = pair_of(part, 2 * c)
        return carry

    lax.fori_loop(0, rows // len(sums), some, 0)
    return device


def shadow_second(cols, agg, blocks, prolong, direction, matrix, product, send, *sums):
    own_product(direction, matrix, product)
    rows = blocks.shape[0]
    device = collapse_out(cols, blocks, send, sums)
    for b in range(rows):
        for p, piece in enumerate(spread_row(agg, b, rows // 2, device, prolong)):
            send[b * N : (b + 1) * N, (rows + p) * 2 * N : (rows + p + 1) * 2 * N] = piece


def shadow_third(cols, cols_top, agg_top, blocks, prolong_top, direction, matrix, product, send, transfer, *sums):
    own_product(direction, matrix, product)
    collapse_out(cols, blocks, send, sums)
    rows = prolong_top.shape[0]
    device = cols_top[0, 0] // rows
    for b in range(rows):
        put_halves(transfer, slice(b * N, (b + 1) * N), spread_row(agg_top, b, rows // 2, device, prolong_top))


def own_product(vector, matrix, product):
    product[...] = apply_t(vector[...], matrix[:, : matrix.shape[1] // 2])


def other_product(product, other, matrix):
    return product[...] + apply_t(other, matrix[:, matrix.shape[1] // 2 :])


def step_first(first, product, other, matrix, direction, residual):
    d = first[...]
    r = d - (d + other_product(product, other[...], matrix))
    residual[...] = r
    direction[...] = W[0][0] * d + W[0][1] * r


def step_second(first, old, residual, product, other, matrix, direction, new_residual, total):
    d = old[...]
    r = residual[...] - (d + other_product(product, other[...], matrix))
    new_residual[...] = r
    new = W[1][0] * d + W[1][1] * r
    direction[...] = new
    total[...] = first[...] + d + new


def step_third(old, residual, product, other, matrix, transfer, new_residual, own_part, other_part):
    r = residual[...] - (old[...] + other_product(product, other[...], matrix))
    new_residual[...] = r
    half = transfer.shape[1] // 2
    other_part[...] = apply_n(r, transfer[:, half:])
    own_part[...] = apply_n(r, transfer[:, :half])


def add(a, b, out):
    out[...] = a[...] + b[...]


def write_blocks(value, out):
    unpack(value[...], out)


def swapped(value):
    half = value.shape[1] // 2
    return jnp.concatenate([value[:, half:], value[:, :half]], axis=1)


def join_mid(own, other, matrix, transfer):
    rows = own.shape[0]
    width = 2 * rows
    for at, source, turn in ((0, own, False), (1, other, True)):
        value = source[:, :width]
        shift = source[:, width:]
        if turn:
            value, shift = swapped(value), swapped(shift)
        here = pl.ds(at * rows, rows)
        for side in range(2):
            high, low = split(value[:, side * rows : (side + 1) * rows])
            matrix[here, pl.ds(2 * side * rows, rows)] = high
            matrix[here, pl.ds((2 * side + 1) * rows, rows)] = low
        high, low = split(shift)
        transfer[here, pl.ds(0, rows)] = high
        transfer[here, pl.ds(rows, rows)] = low


def join_low(own, other, out):
    rows = own.shape[0]
    out[:rows] = own[...]
    out[rows:] = swapped(other[...])


def split_low(own, other, out_own, out_other):
    width = own.shape[1]
    for source, out in ((own, out_own), (other, out_other)):
        high, low = split(source[...])
        out[:, :width] = high
        out[:, width:] = low


def solve_mid(product, own, other, matrix, transfer, low_pair, solution):
    half = own.shape[1]
    d = jnp.concatenate([own[...], other[...]], axis=1)
    r = d - (d + other_product(product, other[...], matrix))
    x = d[:, :half]
    for step in range(2):
        d = W[step][0] * d + W[step][1] * r
        x = x + d[:, :half]
        mid = matrix.shape[1] // 2
        r = r - (d + apply_t(d[:, :half], matrix[:, :mid]) + apply_t(d[:, half:], matrix[:, mid:]))
    solution[...] = x
    low_pair[...] = apply_n(r, transfer[...])


def solve_low(own, other, matrix_own, matrix_other, fine, transfer, fixed):
    half = own.shape[1] // 2
    found = []
    for at, matrix in ((0, matrix_own), (1, matrix_other)):
        here = slice(at * half, (at + 1) * half)
        d = jnp.concatenate([own[:, here], other[:, here]], axis=1)
        r = d
        x = d
        for step in range(2):
            r = r - (d + apply_t(d, matrix[...]))
            d = W[step][0] * d + W[step][1] * r
            x = x + d
        found.append(x[:, :half])
    fixed[...] = fine[...] + apply_t(jnp.concatenate(found, axis=1), transfer[: fixed.shape[1]])


def start_correction(total, fixed, transfer, out):
    out[...] = total[...] + apply_t(fixed[...], transfer[:, : transfer.shape[1] // 2])


def end_correction(partial, other, transfer, out):
    unpack(other_product(partial, other[...], transfer), out)


def per_device(
    flips,
    right_side,
    operator_top,
    columns_top,
    aggregate_top,
    prolong_top,
    operator_mid,
    columns_mid,
    aggregate_mid,
    prolong_mid,
    operator_low,
    columns_low,
):
    def flip(value, level):
        return lax.ppermute(value, ("gx", "gy"), flips[level])

    rows = operator_top.shape[0]
    n_top = rows * N
    n_mid = n_top // 2
    n_low = n_mid // 2
    vec_top = ((S, n_top), F32)
    vec_mid = ((S, n_mid), F32)
    sums = [pltpu.VMEM((2 * rows, N, N), F32)] * 2

    (first,) = call("pack_side", pack_side, [vec_top], right_side)
    other = flip(first, 0)
    matrix, product = prepare(
        "prepare_top",
        prepare_top,
        [((n_top, 4 * n_top), BF16), vec_top],
        sums,
        1,
        columns_top,
        operator_top,
        first,
    )
    d1, r1 = call("step_first", step_first, [vec_top, vec_top], first, product, other, matrix)
    other = flip(d1, 0)
    product, send_mid = prepare(
        "shadow_second",
        shadow_second,
        [vec_top, ((n_mid, 3 * n_mid), F32)],
        sums,
        2,
        columns_mid,
        aggregate_mid,
        operator_mid,
        prolong_mid,
        d1,
        matrix,
    )
    mid_other = flip(send_mid, 1)
    d2, r2, total = call("step_second", step_second, [vec_top] * 3, first, d1, r1, product, other, matrix)
    other = flip(d2, 0)
    product, send_low, transfer = prepare(
        "shadow_third",
        shadow_third,
        [vec_top, ((n_low, 2 * n_low), F32), ((n_top, 4 * n_mid), BF16)],
        sums,
        3,
        columns_low,
        columns_top,
        aggregate_top,
        operator_low,
        prolong_top,
        d2,
        matrix,
    )
    low_other = flip(send_low, 2)
    smoothed, own_part, other_part = call(
        "step_third", step_third, [vec_top, vec_mid, vec_mid], d2, r2, product, other, matrix, transfer
    )
    arrived = flip(other_part, 0)
    (low_matrix,) = call("join_low", join_low, [((2 * n_low, 2 * n_low), F32)], send_low, low_other)
    low_matrix_other = flip(low_matrix, 1)
    (smoothed_blocks,) = call("write_smoothed", write_blocks, [((rows, S, N), F32)], smoothed)
    (mid_side,) = call("add_mid", add, [vec_mid], own_part, arrived)
    other = flip(mid_side, 1)
    mid_matrix, mid_transfer = call(
        "join_mid", join_mid, [((2 * n_mid, 4 * n_mid), BF16), ((2 * n_mid, 4 * n_low), BF16)], send_mid, mid_other
    )
    (product,) = call("own_mid", own_product, [vec_top], mid_side, mid_matrix)
    low_pair, x_mid = call(
        "solve_mid", solve_mid, [((S, 2 * n_low), F32), vec_mid], product, mid_side, other, mid_matrix, mid_transfer
    )
    other = flip(low_pair, 2)
    low_own, low_far = call(
        "split_low", split_low, [((2 * n_low, 4 * n_low), BF16)] * 2, low_matrix, low_matrix_other
    )
    (mid_fixed,) = call("solve_low", solve_low, [vec_mid], low_pair, other, low_own, low_far, x_mid, mid_transfer)
    other = flip(mid_fixed, 0)
    (partial,) = call("start_correction", start_correction, [vec_top], total, mid_fixed, transfer)
    (correction,) = call("end_correction", end_correction, [((rows, S, N), F32)], partial, other, transfer)
    return correction, smoothed_blocks


def prepare(name, body, outs, scratch, scalars, *args):
    spaces = [pltpu.SMEM] * scalars + [pltpu.VMEM] * (len(args) - scalars)
    args = [pltpu.with_memory_space_constraint(a, m) for a, m in zip(args, spaces)]
    return pl.pallas_call(
        body,
        name=name,
        out_shape=[pltpu.VMEM(shape, dtype) for shape, dtype in outs],
        in_specs=[pl.BlockSpec(memory_space=m) for m in spaces],
        out_specs=[pl.BlockSpec(memory_space=pltpu.VMEM)] * len(outs),
        scratch_shapes=scratch,
        cost_estimate=pl.CostEstimate(flops=COST.get(name, 200) * 1000000, bytes_accessed=0, transcendentals=0),
        compiler_params=pltpu.CompilerParams(vmem_limit_bytes=8 * 1024 * 1024),
    )(*args)


def solution(mesh):
    n_gx, n_gy = mesh.shape["gx"], mesh.shape["gy"]
    masks = (n_gy // 2, n_gx // 2 * n_gy, n_gy // 4)
    flips = [[(source, source ^ mask) for source in range(n_gx * n_gy)] for mask in masks]
    lead = ("gx", "gy")
    in_specs = (
        P(lead, None, None),
        P(lead, None, None, None),
        P(lead, None),
        P(lead),
        P(lead, None, None),
        P(lead, None, None, None),
        P(lead, None),
        P(lead),
        P(lead, None, None),
        P(lead, None, None, None),
        P(lead, None),
    )
    out_specs = (P(lead, None, None), P(lead, None, None))
    return jax.shard_map(
        functools.partial(per_device, flips), mesh=mesh, in_specs=in_specs, out_specs=out_specs, check_vma=False
    )
```

time: 143 us -> 50.6 us (0.35); the launches traced: 141 us -> 50.5 us
  matrix products: 48.7 us -> 0 us
  local copies, waits for them, and re-layouts: 28.3 us -> 2.19 us
  starting transfers between devices: 34.7 us -> 17.3 us
  other arithmetic: 12.4 us -> 0 us
  Pallas kernels: 0 us -> 11.1 us
  waiting for transfers between devices: 16.5 us -> 19.1 us
    dot_general x14 -> x0, matrix products: 48.7 us -> none  [the longest x8 44.6 us: apply_rows(): jnp.einsum('bjik,bjsk->bsi', operator, gathered, precision=lax.Precision....]
    gather x10 -> x0, local copies, waits for them, and re-layouts: 20.4 us -> none  [the longest x8 17.1 us: apply_rows(): gathered = whole[local_cols]]
    ppermute x12 -> x10, starting transfers between devices: 34.7 us -> 17.3 us  [flip(): return lax.ppermute(value, ('gx', 'gy'), flips[level])]
    pallas_call x0 -> x17, Pallas kernels: none -> 11.1 us  [the longest x3 6.7 us: prepare(): pl.pallas_call(body, name=name, out_shape=[pltpu.VMEM(shape, dtype) for s...]
    gather x5 -> x0, other arithmetic: 4.38 us -> none  [the longest x3 2.48 us: apply_rows(): gathered = whole[local_cols]]
    concatenate x10 -> x0, other arithmetic: 3.33 us -> none  [the longest x8 2.7 us: pair_vector(): return jnp.concatenate([vector, other], axis=0)]
    select_n x5 -> x0, other arithmetic: 3.03 us -> none  [the longest x3 1.89 us: apply_rows(): gathered = whole[local_cols]]
    broadcast_in_dim x3 -> x0, local copies, waits for them, and re-layouts: 2.69 us -> none  [apply_rows(): gathered = whole[local_cols]]
  transfers between devices with their start and end apart: 12 -> 10, of which waited for: 12 -> 6; matrix products, arithmetic and copies ran while one was open for 7% -> 1% of each run, Pallas kernels for 0% -> 19%
where the time goes in v1:
time: 50.6 us; the launch traced here: 50.5 us
  waiting for transfers between devices  19.1 us (38%)
  starting transfers between devices  17.3 us (34%)
  Pallas kernels  11.1 us (22%)
  local copies, waits for them, and re-layouts  2.19 us (4%)
  between operations  0.74 us (1%)
    ppermute x10, waiting for transfers between devices, flip(): return lax.ppermute(value, ('gx', 'gy'), flips[level])  19.1 us
    ppermute x10, starting transfers between devices, flip(): return lax.ppermute(value, ('gx', 'gy'), flips[level])  17.3 us
    pallas_call x3, Pallas kernels, prepare(): pl.pallas_call(body, name=name, out_shape=[pltpu.VMEM(shape, dtype) for s...  6.7 us
    pallas_call x14, Pallas kernels, call(): pl.pallas_call(body, name=name, out_shape=[pltpu.VMEM(shape, dtype) for s...  4.44 us
    unnamed x24, local copies, waits for them, and re-layouts  2.19 us
  transfers between devices with their start and end apart: 10, of which 6 were waited for; matrix products, arithmetic and copies ran while one was open for 1% of the time, Pallas kernels for 19%

profile of v1, /device:TPU:128, one launch (start us, length us, event | category | flops | bytes accessed | tf_op | source)
XLA Modules:
  0.0 50.5 jit_solution(12333090472095193450)
XLA Ops:
  0.7 0.9 %copy-done.10 = f32[8,8,64]{2,1,0:T(8,128)S(1)} copy-done((f32[8,8,64]{2,1,0:T(8,128)S(1)}, f32[8,8,64]{2,1,0:T(8,128)}, u32[]{:S(2)}) %copy-start.10) | copy-done | bytes 16408
  1.6 3.1 %collective-permute-start = (f32[8,512]{1,0:T(8,128)S(1)}, f32[8,512]{1,0:T(8,128)S(1)}, u32[]{:S(2)}, u32[]{:S(2)}) collective-permute-start(f32[8,512]{1,0:T(8,128)S(1)} %pack_side.1.first), channel_id=1, source_target_pairs={{0,16},{1,17},{2,18},{3,19},{4,20},{5,21},{6,22},{7,23},{8,24},{9,... | collective-permute-start | bytes 49160 | tf_op jit(solution)/shard_map/ppermute | solution.py:306
  4.8 3.3 %prepare_top.1 = (bf16[512,2048]{1,0:T(8,128)(2,1)S(1)}, f32[8,512]{1,0:T(8,128)S(1)}) custom-call(s32[8,27]{1,0:T(8,128)S(1)} %copy-done.4, f32[8,27,64,64]{3,2,1,0:T(8,128)S(1)} %copy-done.9, f32[8,512]{1,0:T(8,128)S(1)} %pack_side.1.first), custom_call_target="tpu_custom_call" | custom-call | flops 4000000000 | tf_op jit(solution)/shard_map/prepare_top/pallas_call | solution.py:391
  8.1 0.4 step_first.1
  8.5 2.0 %collective-permute-start.1 = (f32[8,512]{1,0:T(8,128)S(1)}, f32[8,512]{1,0:T(8,128)S(1)}, u32[]{:S(2)}, u32[]{:S(2)}) collective-permute-start(f32[8,512]{1,0:T(8,128)S(1)} %get-tuple-element.25.direction.old), channel_id=1, source_target_pairs={{0,16},{1,17},{2,18},{3,19},{4,20},{5,21},{6,22},{7,23},{8,24},{9,... | collective-permute-start | bytes 49160 | tf_op jit(solution)/shard_map/ppermute | solution.py:306
  10.5 2.1 %shadow_second.1 = (f32[8,512]{1,0:T(8,128)S(1)}, f32[256,768]{1,0:T(8,128)S(1)}) custom-call(s32[4,27]{1,0:T(4,128)S(1)} %copy-done.5, s32[4]{0:T(128)S(1)} %copy-done.7, f32[4,27,64,64]{3,2,1,0:T(8,128)S(1)} %copy-done, f32[4,64,64]{2,1,0:T(8,128)S(1)} %copy-done.3, f32[8,512]{1,0:T(8,128)S(1)} %get-tuple-element.25.direction.old, ...), custom_call_target="tpu_custom_call" | custom-call | flops 200000000 | tf_op jit(solution)/shard_map/shadow_second/pallas_call | solution.py:391
  12.6 3.3 %collective-permute-start.4 = (f32[256,768]{1,0:T(8,128)S(1)}, f32[256,768]{1,0:T(8,128)S(1)}, u32[]{:S(2)}, u32[]{:S(2)}) collective-permute-start(f32[256,768]{1,0:T(8,128)S(1)} %get-tuple-element.35.own), channel_id=1, source_target_pairs={{0,128},{1,129},{2,130},{3,131},{4,132},{5,133},{6,134},{7,135},{8... | collective-permute-start | bytes 2359304 | tf_op jit(solution)/shard_map/ppermute | solution.py:306
  15.9 0.4 step_second.1
  16.3 1.7 %collective-permute-start.2 = (f32[8,512]{1,0:T(8,128)S(1)}, f32[8,512]{1,0:T(8,128)S(1)}, u32[]{:S(2)}, u32[]{:S(2)}) collective-permute-start(f32[8,512]{1,0:T(8,128)S(1)} %get-tuple-element.29.direction.old), channel_id=1, source_target_pairs={{0,16},{1,17},{2,18},{3,19},{4,20},{5,21},{6,22},{7,23},{8,24},{9,... | collective-permute-start | bytes 49160 | tf_op jit(solution)/shard_map/ppermute | solution.py:306
  18.0 1.3 %shadow_third.1 = (f32[8,512]{1,0:T(8,128)S(1)}, f32[128,256]{1,0:T(8,128)S(1)}, bf16[512,1024]{1,0:T(8,128)(2,1)S(1)}) custom-call(s32[2,27]{1,0:T(2,128)S(1)} %copy-done.6, s32[8,27]{1,0:T(8,128)S(1)} %copy-done.4, s32[8]{0:T(128)S(1)} %copy-done.8, f32[2,27,64,64]{3,2,1,0:T(8,128)S(1)} %copy-done.1, f32[8,64,64]{2,1,0:T(8,128)S(1)} %copy-done.2, ...), custom_call_target="tpu_custom_call" | custom-call | flops 200000000 | tf_op jit(solution)/shard_map/shadow_third/pallas_call | solution.py:391
  19.3 0.7 %collective-permute-start.7 = (f32[128,256]{1,0:T(8,128)S(1)}, f32[128,256]{1,0:T(8,128)S(1)}, u32[]{:S(2)}, u32[]{:S(2)}) collective-permute-start(f32[128,256]{1,0:T(8,128)S(1)} %get-tuple-element.39.own), channel_id=1, source_target_pairs={{0,8},{1,9},{2,10},{3,11},{4,12},{5,13},{6,14},{7,15},{8,0},{9,1},... | collective-permute-start | bytes 393224 | tf_op jit(solution)/shard_map/ppermute | solution.py:306
  20.0 1.6 %collective-permute-done.2.other = f32[8,512]{1,0:T(8,128)S(1)} collective-permute-done((f32[8,512]{1,0:T(8,128)S(1)}, f32[8,512]{1,0:T(8,128)S(1)}, u32[]{:S(2)}, u32[]{:S(2)}) %collective-permute-start.2) | collective-permute-done | bytes 16416 | tf_op jit(solution)/shard_map/ppermute | solution.py:306
  21.6 0.6 %step_third.1 = (f32[8,512]{1,0:T(8,128)S(1)}, f32[8,256]{1,0:T(8,128)S(1)}, f32[8,256]{1,0:T(8,128)S(1)}) custom-call(f32[8,512]{1,0:T(8,128)S(1)} %get-tuple-element.29.direction.old, f32[8,512]{1,0:T(8,128)S(1)} %get-tuple-element.30.residual, f32[8,512]{1,0:T(8,128)S(1)} %get-tuple-element.31.product, f32[8,512]{1,0:T(8,128)S(1)} %collective-permute-done.2.other, ...), custom_call_target="tpu_custom_call" | custom-call | flops 6000000000 | tf_op jit(solution)/shard_map/step_third/pallas_call | solution.py:37
  22.2 1.8 %collective-permute-start.3 = (f32[8,256]{1,0:T(8,128)S(1)}, f32[8,256]{1,0:T(8,128)S(1)}, u32[]{:S(2)}, u32[]{:S(2)}) collective-permute-start(f32[8,256]{1,0:T(8,128)S(1)} %get-tuple-element.34), channel_id=1, source_target_pairs={{0,16},{1,17},{2,18},{3,19},{4,20},{5,21},{6,22},{7,23},{8,24},{9,... | collective-permute-start | bytes 24584 | tf_op jit(solution)/shard_map/ppermute | solution.py:306
  24.1 0.6 %copy.14 = f32[8,8,64]{2,1,0:T(8,128)} copy(f32[8,8,64]{2,1,0:T(8,128)S(1)} %write_smoothed.1) | data formatting | bytes 32768
  24.7 1.5 %collective-permute-start.8 = (f32[256,256]{1,0:T(8,128)S(1)}, f32[256,256]{1,0:T(8,128)S(1)}, u32[]{:S(2)}, u32[]{:S(2)}) collective-permute-start(f32[256,256]{1,0:T(8,128)S(1)} %join_low.1.own), channel_id=1, source_target_pairs={{0,128},{1,129},{2,130},{3,131},{4,132},{5,133},{6,134},{7,135},{8... | collective-permute-start | bytes 786440 | tf_op jit(solution)/shard_map/ppermute | solution.py:306
  26.2 1.2 %collective-permute-done.3.b = f32[8,256]{1,0:T(8,128)S(1)} collective-permute-done((f32[8,256]{1,0:T(8,128)S(1)}, f32[8,256]{1,0:T(8,128)S(1)}, u32[]{:S(2)}, u32[]{:S(2)}) %collective-permute-start.3) | collective-permute-done | bytes 8224 | tf_op jit(solution)/shard_map/ppermute | solution.py:306
  27.4 1.3 %collective-permute-start.5 = (f32[8,256]{1,0:T(8,128)S(1)}, f32[8,256]{1,0:T(8,128)S(1)}, u32[]{:S(2)}, u32[]{:S(2)}) collective-permute-start(f32[8,256]{1,0:T(8,128)S(1)} %add_mid.1.vector.own), channel_id=1, source_target_pairs={{0,128},{1,129},{2,130},{3,131},{4,132},{5,133},{6,134},{7,135},{8... | collective-permute-start | bytes 24584 | tf_op jit(solution)/shard_map/ppermute | solution.py:306
  28.7 5.9 %collective-permute-done.4.other = f32[256,768]{1,0:T(8,128)S(1)} collective-permute-done((f32[256,768]{1,0:T(8,128)S(1)}, f32[256,768]{1,0:T(8,128)S(1)}, u32[]{:S(2)}, u32[]{:S(2)}) %collective-permute-start.4) | collective-permute-done | bytes 786464 | tf_op jit(solution)/shard_map/ppermute | solution.py:306
  34.6 0.3 join_mid.1
  34.9 0.2 own_mid.1.product
  35.2 3.8 %collective-permute-done.5.other = f32[8,256]{1,0:T(8,128)S(1)} collective-permute-done((f32[8,256]{1,0:T(8,128)S(1)}, f32[8,256]{1,0:T(8,128)S(1)}, u32[]{:S(2)}, u32[]{:S(2)}) %collective-permute-start.5) | collective-permute-done | bytes 8224 | tf_op jit(solution)/shard_map/ppermute | solution.py:306
  39.0 1.1 %solve_mid.1 = (f32[8,256]{1,0:T(8,128)S(1)}, f32[8,256]{1,0:T(8,128)S(1)}) custom-call(f32[8,512]{1,0:T(8,128)S(1)} %own_mid.1.product, f32[8,256]{1,0:T(8,128)S(1)} %add_mid.1.vector.own, f32[8,256]{1,0:T(8,128)S(1)} %collective-permute-done.5.other, bf16[512,1024]{1,0:T(8,128)(2,1)S(1)} %get-tuple-element.36.matrix, ...), custom_call_target="tpu_custom_call" | custom-call | flops 200000000 | tf_op jit(solution)/shard_map/solve_mid/pallas_call | solution.py:37
  40.0 0.6 %collective-permute-start.6 = (f32[8,256]{1,0:T(8,128)S(1)}, f32[8,256]{1,0:T(8,128)S(1)}, u32[]{:S(2)}, u32[]{:S(2)}) collective-permute-start(f32[8,256]{1,0:T(8,128)S(1)} %get-tuple-element.38.own), channel_id=1, source_target_pairs={{0,8},{1,9},{2,10},{3,11},{4,12},{5,13},{6,14},{7,15},{8,0},{9,1},... | collective-permute-start | bytes 24584 | tf_op jit(solution)/shard_map/ppermute | solution.py:306
  40.6 0.1 split_low.1
  40.7 3.0 %collective-permute-done.6.other = f32[8,256]{1,0:T(8,128)S(1)} collective-permute-done((f32[8,256]{1,0:T(8,128)S(1)}, f32[8,256]{1,0:T(8,128)S(1)}, u32[]{:S(2)}, u32[]{:S(2)}) %collective-permute-start.6) | collective-permute-done | bytes 8224 | tf_op jit(solution)/shard_map/ppermute | solution.py:306
  43.7 0.7 %solve_low.1.fixed = f32[8,256]{1,0:T(8,128)S(1)} custom-call(f32[8,256]{1,0:T(8,128)S(1)} %get-tuple-element.38.own, f32[8,256]{1,0:T(8,128)S(1)} %collective-permute-done.6.other, bf16[256,512]{1,0:T(8,128)(2,1)S(1)} %get-tuple-element.40.matrix_own, bf16[256,512]{1,0:T(8,128)(2,1)S(1)} %get-tuple-element.41.matrix_other, ...), custom_call_target="tpu_custom_call" | custom-call | flops 200000000 | tf_op jit(solution)/shard_map/solve_low/pallas_call | solution.py:37
  44.4 1.4 %collective-permute-start.9 = (f32[8,256]{1,0:T(8,128)S(1)}, f32[8,256]{1,0:T(8,128)S(1)}, u32[]{:S(2)}, u32[]{:S(2)}) collective-permute-start(f32[8,256]{1,0:T(8,128)S(1)} %solve_low.1.fixed), channel_id=1, source_target_pairs={{0,16},{1,17},{2,18},{3,19},{4,20},{5,21},{6,22},{7,23},{8,24},{9,... | collective-permute-start | bytes 24584 | tf_op jit(solution)/shard_map/ppermute | solution.py:306
  45.7 0.2 start_correction.1.partial
  46.0 3.6 %collective-permute-done.9.other = f32[8,256]{1,0:T(8,128)S(1)} collective-permute-done((f32[8,256]{1,0:T(8,128)S(1)}, f32[8,256]{1,0:T(8,128)S(1)}, u32[]{:S(2)}, u32[]{:S(2)}) %collective-permute-start.9) | collective-permute-done | bytes 8224 | tf_op jit(solution)/shard_map/ppermute | solution.py:306
  49.6 0.3 end_correction.1
  49.9 0.6 %copy.13 = f32[8,8,64]{2,1,0:T(8,128)} copy(f32[8,8,64]{2,1,0:T(8,128)S(1)} %end_correction.1) | data formatting | bytes 32768
  (29 shorter events, 0.2 us)
Async XLA Ops:
  0.6 4.1 %copy-start.4 = (s32[8,27]{1,0:T(8,128)S(1)}, s32[8,27]{1,0:T(8,128)}, u32[]{:S(2)}) copy-start(s32[8,27]{1,0:T(8,128)} %cols_top.1) | copy-start | bytes 2596
  0.6 4.1 %copy-start.9 = (f32[8,27,64,64]{3,2,1,0:T(8,128)S(1)}, f32[8,27,64,64]{3,2,1,0:T(8,128)}, u32[]{:S(2)}) copy-start(f32[8,27,64,64]{3,2,1,0:T(8,128)} %blocks.3) | copy-start | bytes 10616836
  0.6 0.9 %copy-start.10 = (f32[8,8,64]{2,1,0:T(8,128)S(1)}, f32[8,8,64]{2,1,0:T(8,128)}, u32[]{:S(2)}) copy-start(f32[8,8,64]{2,1,0:T(8,128)} %side.1) | copy-start | bytes 49156
  1.6 8.9 %copy-start.3 = (f32[4,64,64]{2,1,0:T(8,128)S(1)}, f32[4,64,64]{2,1,0:T(8,128)}, u32[]{:S(2)}) copy-start(f32[4,64,64]{2,1,0:T(8,128)} %prolong.1) | copy-start | bytes 196612
  1.6 8.9 %copy-start.5 = (s32[4,27]{1,0:T(4,128)S(1)}, s32[4,27]{1,0:T(4,128)}, u32[]{:S(2)}) copy-start(s32[4,27]{1,0:T(4,128)} %cols.4) | copy-start | bytes 1300
  1.6 8.9 %copy-start.7 = (s32[4]{0:T(128)S(1)}, s32[4]{0:T(128)}, u32[]{:S(2)}) copy-start(s32[4]{0:T(128)} %agg.1) | copy-start | bytes 52
  1.6 6.4 %collective-permute-start = (f32[8,512]{1,0:T(8,128)S(1)}, f32[8,512]{1,0:T(8,128)S(1)}, u32[]{:S(2)}, u32[]{:S(2)}) collective-permute-start(f32[8,512]{1,0:T(8,128)S(1)} %pack_side.1.first), channel_id=1, source_target_pairs={{0,16},{1,17},{2,18},{3,19},{4,20},{5,21},{6,22},{7,23},{8,24},{9,... | collective-permute-start | bytes 49160 | tf_op jit(solution)/shard_map/ppermute | solution.py:306
  4.8 5.8 %copy-start = (f32[4,27,64,64]{3,2,1,0:T(8,128)S(1)}, f32[4,27,64,64]{3,2,1,0:T(8,128)}, u32[]{:S(2)}) copy-start(f32[4,27,64,64]{3,2,1,0:T(8,128)} %blocks.4) | copy-start | bytes 5308420
  8.5 7.4 %collective-permute-start.1 = (f32[8,512]{1,0:T(8,128)S(1)}, f32[8,512]{1,0:T(8,128)S(1)}, u32[]{:S(2)}, u32[]{:S(2)}) collective-permute-start(f32[8,512]{1,0:T(8,128)S(1)} %get-tuple-element.25.direction.old), channel_id=1, source_target_pairs={{0,16},{1,17},{2,18},{3,19},{4,20},{5,21},{6,22},{7,23},{8,24},{9,... | collective-permute-start | bytes 49160 | tf_op jit(solution)/shard_map/ppermute | solution.py:306
  12.6 22.1 %collective-permute-start.4 = (f32[256,768]{1,0:T(8,128)S(1)}, f32[256,768]{1,0:T(8,128)S(1)}, u32[]{:S(2)}, u32[]{:S(2)}) collective-permute-start(f32[256,768]{1,0:T(8,128)S(1)} %get-tuple-element.35.own), channel_id=1, source_target_pairs={{0,128},{1,129},{2,130},{3,131},{4,132},{5,133},{6,134},{7,135},{8... | collective-permute-start | bytes 2359304 | tf_op jit(solution)/shard_map/ppermute | solution.py:306
  15.9 2.1 %copy-start.1 = (f32[2,27,64,64]{3,2,1,0:T(8,128)S(1)}, f32[2,27,64,64]{3,2,1,0:T(8,128)}, u32[]{:S(2)}) copy-start(f32[2,27,64,64]{3,2,1,0:T(8,128)} %blocks.5) | copy-start | bytes 2654212
  15.9 2.1 %copy-start.2 = (f32[8,64,64]{2,1,0:T(8,128)S(1)}, f32[8,64,64]{2,1,0:T(8,128)}, u32[]{:S(2)}) copy-start(f32[8,64,64]{2,1,0:T(8,128)} %prolong_top.1) | copy-start | bytes 393220
  15.9 2.1 %copy-start.6 = (s32[2,27]{1,0:T(2,128)S(1)}, s32[2,27]{1,0:T(2,128)}, u32[]{:S(2)}) copy-start(s32[2,27]{1,0:T(2,128)} %cols.5) | copy-start | bytes 652
  15.9 2.1 %copy-start.8 = (s32[8]{0:T(128)S(1)}, s32[8]{0:T(128)}, u32[]{:S(2)}) copy-start(s32[8]{0:T(128)} %agg_top.1) | copy-start | bytes 100
  16.3 5.3 %collective-permute-start.2 = (f32[8,512]{1,0:T(8,128)S(1)}, f32[8,512]{1,0:T(8,128)S(1)}, u32[]{:S(2)}, u32[]{:S(2)}) collective-permute-start(f32[8,512]{1,0:T(8,128)S(1)} %get-tuple-element.29.direction.old), channel_id=1, source_target_pairs={{0,16},{1,17},{2,18},{3,19},{4,20},{5,21},{6,22},{7,23},{8,24},{9,... | collective-permute-start | bytes 49160 | tf_op jit(solution)/shard_map/ppermute | solution.py:306
  19.3 5.4 %collective-permute-start.7 = (f32[128,256]{1,0:T(8,128)S(1)}, f32[128,256]{1,0:T(8,128)S(1)}, u32[]{:S(2)}, u32[]{:S(2)}) collective-permute-start(f32[128,256]{1,0:T(8,128)S(1)} %get-tuple-element.39.own), channel_id=1, source_target_pairs={{0,8},{1,9},{2,10},{3,11},{4,12},{5,13},{6,14},{7,15},{8,0},{9,1},... | collective-permute-start | bytes 393224 | tf_op jit(solution)/shard_map/ppermute | solution.py:306
  22.2 5.2 %collective-permute-start.3 = (f32[8,256]{1,0:T(8,128)S(1)}, f32[8,256]{1,0:T(8,128)S(1)}, u32[]{:S(2)}, u32[]{:S(2)}) collective-permute-start(f32[8,256]{1,0:T(8,128)S(1)} %get-tuple-element.34), channel_id=1, source_target_pairs={{0,16},{1,17},{2,18},{3,19},{4,20},{5,21},{6,22},{7,23},{8,24},{9,... | collective-permute-start | bytes 24584 | tf_op jit(solution)/shard_map/ppermute | solution.py:306
  24.7 15.9 %collective-permute-start.8 = (f32[256,256]{1,0:T(8,128)S(1)}, f32[256,256]{1,0:T(8,128)S(1)}, u32[]{:S(2)}, u32[]{:S(2)}) collective-permute-start(f32[256,256]{1,0:T(8,128)S(1)} %join_low.1.own), channel_id=1, source_target_pairs={{0,128},{1,129},{2,130},{3,131},{4,132},{5,133},{6,134},{7,135},{8... | collective-permute-start | bytes 786440 | tf_op jit(solution)/shard_map/ppermute | solution.py:306
  27.4 11.5 %collective-permute-start.5 = (f32[8,256]{1,0:T(8,128)S(1)}, f32[8,256]{1,0:T(8,128)S(1)}, u32[]{:S(2)}, u32[]{:S(2)}) collective-permute-start(f32[8,256]{1,0:T(8,128)S(1)} %add_mid.1.vector.own), channel_id=1, source_target_pairs={{0,128},{1,129},{2,130},{3,131},{4,132},{5,133},{6,134},{7,135},{8... | collective-permute-start | bytes 24584 | tf_op jit(solution)/shard_map/ppermute | solution.py:306
  40.0 3.7 %collective-permute-start.6 = (f32[8,256]{1,0:T(8,128)S(1)}, f32[8,256]{1,0:T(8,128)S(1)}, u32[]{:S(2)}, u32[]{:S(2)}) collective-permute-start(f32[8,256]{1,0:T(8,128)S(1)} %get-tuple-element.38.own), channel_id=1, source_target_pairs={{0,8},{1,9},{2,10},{3,11},{4,12},{5,13},{6,14},{7,15},{8,0},{9,1},... | collective-permute-start | bytes 24584 | tf_op jit(solution)/shard_map/ppermute | solution.py:306
  44.4 5.2 %collective-permute-start.9 = (f32[8,256]{1,0:T(8,128)S(1)}, f32[8,256]{1,0:T(8,128)S(1)}, u32[]{:S(2)}, u32[]{:S(2)}) collective-permute-start(f32[8,256]{1,0:T(8,128)S(1)} %solve_low.1.fixed), channel_id=1, source_target_pairs={{0,16},{1,17},{2,18},{3,19},{4,20},{5,21},{6,22},{7,23},{8,24},{9,... | collective-permute-start | bytes 24584 | tf_op jit(solution)/shard_map/ppermute | solution.py:306

commit v2 on v1

v2 whole, which is shorter than its diff:
```python
import functools

import jax
import jax.numpy as jnp
from jax import lax
from jax.experimental import pallas as pl
from jax.experimental.pallas import tpu as pltpu
from jax.sharding import PartitionSpec as P

center = 1.0
half_width = 0.6
F32 = jnp.float32
BF16 = jnp.bfloat16
N = 64
S = 8
J = 27


def chebyshev_weights():
    sigma = center / half_width
    rho = half_width / center
    weights = []
    for step in range(3):
        rho_next = 1.0 / (2.0 * sigma - rho)
        weights.append((rho_next * rho, 2.0 * rho_next / half_width))
        rho = rho_next
    return weights


W = chebyshev_weights()
COST = {"prepare_top": 4000, "step_first": 4000, "step_second": 100000, "step_third": 6000, "solve_mid": 20000}


def call(name, body, outs, *args, remote=(), scratch=(), aliases=None, limit=8):
    spaces = [pltpu.HBM if at in remote else pltpu.VMEM for at in range(len(args))]
    args = [pltpu.with_memory_space_constraint(a, m) for a, m in zip(args, spaces)]
    return pl.pallas_call(
        body,
        name=name,
        out_shape=[pltpu.VMEM(shape, dtype) for shape, dtype in outs],
        in_specs=[pl.BlockSpec(memory_space=m) for m in spaces],
        out_specs=[pl.BlockSpec(memory_space=pltpu.VMEM)] * len(outs),
        scratch_shapes=scratch,
        input_output_aliases=aliases or {},
        cost_estimate=pl.CostEstimate(flops=COST.get(name, 200) * 1000000, bytes_accessed=0, transcendentals=0),
        compiler_params=pltpu.CompilerParams(vmem_limit_bytes=limit * 1024 * 1024),
    )(*args)


def copies(sources, targets, sems):
    moves = [pltpu.make_async_copy(s, t, sems.at[n]) for n, (s, t) in enumerate(zip(sources, targets))]
    for move in moves:
        move.start()

    def wait():
        for move in moves:
            move.wait()

    return wait


def index_scratch(*arrays):
    return [pltpu.SemaphoreType.DMA((len(arrays),))] + [pltpu.SMEM(a.shape, jnp.int32) for a in arrays]


def split(value):
    high = value.astype(BF16)
    return high, (value - high.astype(F32)).astype(BF16)


def stack(value):
    return jnp.concatenate(split(value), axis=0)


def fold(value):
    return value[:S] + value[S:]


def apply_t(vector, matrix):
    both = stack(vector)
    both = jnp.concatenate([both, both], axis=1)
    out = lax.dot_general(both, matrix, (((1,), (1,)), ((), ())), preferred_element_type=F32)
    return fold(out)


def apply_n(vector, matrix):
    out = fold(lax.dot_general(stack(vector), matrix, (((1,), (0,)), ((), ())), preferred_element_type=F32))
    half = out.shape[1] // 2
    return out[:, :half] + out[:, half:]


def pack(ref):
    return jnp.concatenate([ref[b] for b in range(ref.shape[0])], axis=1)


def unpack(value, ref):
    for b in range(ref.shape[0]):
        ref[b] = value[:, b * N : (b + 1) * N]


def local(index, rows, device):
    offset = index ^ (device * rows)
    return jnp.minimum(offset, rows + (offset & (rows - 1)))


def collapse_rows(cols, b, rows, device, blocks, sums):
    for part in sums:
        part[...] = jnp.zeros(part.shape, F32)
    for j in range(J):
        for n, part in enumerate(sums):
            at = local(cols[b + n, j], rows, device)
            part[at] = part[at] + blocks[b + n, j]


def pair_of(sums, at):
    return jnp.concatenate([sums[at], sums[at + 1]], axis=1)


def spread(at, rows, block):
    twice = jnp.concatenate([block, block], axis=1)
    lane = lax.broadcasted_iota(jnp.int32, (N, 2 * N), 1) // N
    return [jnp.where(lane + 2 * piece == at, twice, 0.0) for piece in range(rows)]


def put_halves(ref, rows_at, pieces):
    half = len(pieces) // 2
    width = half * 2 * N
    for p, piece in enumerate(pieces):
        high, low = split(piece)
        base = (p // half) * 2 * width + (p % half) * 2 * N
        ref[rows_at, pl.ds(base, 2 * N)] = high
        ref[rows_at, pl.ds(base + width, 2 * N)] = low


def lanes_of(b):
    return pl.ds(pl.multiple_of(b * N, N), N)


def prepare_top(cols_in, side_in, remote, matrix, first, product, small, cols, side, held, sems, *sums):
    rows = remote.shape[0]
    wait = copies((cols_in,), (cols,), small)

    def fetch(b):
        return pltpu.make_async_copy(remote.at[b], held.at[b], sems.at[b])

    for b in range(rows):
        fetch(b).start()
    wait_side = copies((side_in,), (side,), sems.at[pl.ds(rows, 1)])
    wait()
    device = cols[0, 0] // rows

    def some(step, carry):
        b = step * len(sums)
        for n in range(len(sums)):
            fetch(b + n).wait()
        collapse_rows(cols, b, rows, device, held, sums)
        for n, part in enumerate(sums):
            put_halves(matrix, lanes_of(b + n), [pair_of(part, 2 * c) for c in range(rows)])
        return carry

    lax.fori_loop(0, rows // len(sums), some, 0)
    wait_side()
    own = pack(side)
    first[...] = own
    product[...] = apply_t(own, matrix[:, : 2 * rows * N])


def collapse_out(cols, blocks, put, sums):
    rows = blocks.shape[0]
    device = cols[0, 0] // rows
    sums = [part.at[: 2 * rows] for part in sums]

    def some(step, carry):
        b = step * len(sums)
        collapse_rows(cols, b, rows, device, blocks, sums)
        for n, part in enumerate(sums):
            for c in range(rows):
                put(b + n, c, pair_of(part, 2 * c))
        return carry

    lax.fori_loop(0, rows // len(sums), some, 0)


def prepare_mid(cols_in, agg_in, blocks, prolong, direction, matrix, product, send, small, cols, agg, *sums):
    wait = copies((cols_in, agg_in), (cols, agg), small)
    own_product(direction, matrix, product)
    rows = blocks.shape[0]
    half = rows // 2
    n_mid = rows * N
    at = rows * n_mid
    for p in range(half):
        send[at + p * N : at + (p + 1) * N] = jnp.concatenate([prolong[2 * p], prolong[2 * p + 1]], axis=1)
    at += half * N
    wait()

    def put(b, c, value):
        send[pl.ds(pl.multiple_of(c * n_mid + b * N, N), N)] = value

    collapse_out(cols, blocks, put, sums)
    device = cols[0, 0] // rows
    row = lax.broadcasted_iota(jnp.int32, (8, 2 * N), 0)
    joined = jnp.zeros((8, 2 * N), jnp.int32)
    for b in range(rows):
        joined = jnp.where(row == b, local(agg[b], half, device), joined)
    send[at : at + 8] = joined.astype(F32)


def prepare_low(
    cols_in, cols_top_in, agg_in, blocks, prolong, direction, matrix, product, send, transfer, small, cols, cols_top, agg, *sums
):
    wait = copies((cols_in, cols_top_in, agg_in), (cols, cols_top, agg), small)
    own_product(direction, matrix, product)
    n_low = blocks.shape[0] * N
    wait()

    def put(b, c, value):
        send[pl.ds(pl.multiple_of(c * n_low + b * N, N), N)] = value

    collapse_out(cols, blocks, put, sums)
    rows = prolong.shape[0]
    device = cols_top[0, 0] // rows
    for b in range(rows):
        at = local(agg[b], rows // 2, device)
        put_halves(transfer, slice(b * N, (b + 1) * N), spread(at, rows // 2, prolong[b]))


def own_product(vector, matrix, product):
    product[...] = apply_t(vector[...], matrix[:, : matrix.shape[1] // 2])


def other_product(product, other, matrix):
    return product[...] + apply_t(other, matrix[:, matrix.shape[1] // 2 :])


def step_first(first, product, other, matrix, direction, residual):
    d = first[...]
    r = d - (d + other_product(product, pack(other), matrix))
    residual[...] = r
    direction[...] = W[0][0] * d + W[0][1] * r


def step_second(first, old, residual, product, other, matrix, direction, new_residual, total):
    d = old[...]
    r = residual[...] - (d + other_product(product, other[...], matrix))
    new_residual[...] = r
    new = W[1][0] * d + W[1][1] * r
    direction[...] = new
    total[...] = first[...] + d + new


def step_third(old, residual, product, other, matrix, transfer, new_residual, other_part):
    r = residual[...] - (old[...] + other_product(product, other[...], matrix))
    new_residual[...] = r
    other_part[...] = apply_n(r, transfer[:, transfer.shape[1] // 2 :])


def restrict_own(residual, transfer_top, source, own_part, out, matrix, transfer):
    r = residual[...]
    own_part[...] = apply_n(r, transfer_top[:, : transfer_top.shape[1] // 2])
    unpack(r, out)
    join_mid(source, matrix, transfer, False)


def add_mid(a, b, after, out):
    out[...] = a[...] + b[...]


def own_mid(side, matrix, low, product, low_out):
    product[...] = apply_t(side[...], matrix[:, : matrix.shape[1] // 2])


def join_mid(source, matrix, transfer, turn):
    n_mid = matrix.shape[0]
    rows = n_mid // N
    half = rows // 2
    for c in range(rows):
        to = (c + half) % rows if turn else c
        high, low = split(source[c * n_mid : (c + 1) * n_mid])
        base = (to // half) * 2 * n_mid + (to % half) * 2 * N
        matrix[:, base : base + 2 * N] = high
        matrix[:, base + n_mid : base + n_mid + 2 * N] = low
    at = rows * n_mid
    joined = at + half * N
    for b in range(rows):
        both = source[at + (b // 2) * N : at + (b // 2 + 1) * N]
        block = both[:, (b % 2) * N : (b % 2 + 1) * N]
        to = source[joined + b : joined + b + 1].astype(jnp.int32)
        pieces = spread(to, half, block)
        for p, piece in enumerate(pieces):
            put = (p + half // 2) % half if turn else p
            high, low = split(piece)
            matrix_rows = slice(b * N, (b + 1) * N)
            transfer[matrix_rows, put * 2 * N : (put + 1) * 2 * N] = high
            transfer[matrix_rows, n_mid + put * 2 * N : n_mid + (put + 1) * 2 * N] = low


def join_other(source, side, own, matrix, transfer, product):
    join_mid(source, matrix, transfer, True)
    product[...] = jnp.concatenate([own[...], apply_t(side[...], matrix[:, : matrix.shape[1] // 2])], axis=1)


def multiply(a, b):
    (a_high, a_low), (b_high, b_low) = a, b
    out = jnp.dot(a_high, b_high, preferred_element_type=F32)
    out += jnp.dot(a_high, b_low, preferred_element_type=F32)
    return out + jnp.dot(a_low, b_high, preferred_element_type=F32)


def compose_low(own, other, out):
    half = own.shape[0] // 2
    top = jnp.concatenate([own[:half], own[half:]], axis=1)
    low = jnp.concatenate([other[half:], other[:half]], axis=1)
    pair = jnp.concatenate([top, low], axis=0)
    (a0, b0), (a1, b1) = W[0], W[1]
    square = multiply(split(top), split(pair))
    row = lax.broadcasted_iota(jnp.int32, top.shape, 0)
    column = lax.broadcasted_iota(jnp.int32, top.shape, 1)
    value = jnp.where(row == column, 1.0 + (1.0 + a1 - b1) * a0, 0.0)
    value += (b1 * (b0 - 1.0 - a0) - (1.0 + a1) * b0) * top + (b1 * b0) * square
    out[:half] = value[:, :half]
    out[half:] = value[:, half:]


def compose_fixed(own, other, transfer, pair, fine, partial, matrix):
    half = own.shape[0] // 2
    width = 2 * half
    near, far = [], []
    for at, source in ((0, own), (1, other)):
        solve = jnp.concatenate([source[:half], source[half:]], axis=1)
        here = transfer[:, at * half : (at + 1) * half], transfer[:, width + at * half : width + (at + 1) * half]
        product = multiply(here, split(solve))
        near.append(product[:, :half])
        far.append(product[:, half:])
    partial[...] = fine[...] + apply_t(pair[...], jnp.concatenate(split(jnp.concatenate(near, axis=1)), axis=1))
    high, low = split(jnp.concatenate(far, axis=1))
    matrix[:, :width] = high
    matrix[:, width:] = low


def solve_mid(product, own, other, matrix_own, matrix_other, transfer_own, transfer_other, low_pair, solution):
    half = own.shape[1]
    mid = matrix_own.shape[1] // 2

    def pair_product(value, columns):
        return jnp.concatenate(
            [apply_t(value, matrix_own[:, columns]), apply_t(value, matrix_other[:, columns])], axis=1
        )

    d = jnp.concatenate([own[...], other[...]], axis=1)
    r = d - (d + product[...] + pair_product(other[...], slice(mid, 2 * mid)))
    x = d[:, :half]
    for step in range(2):
        d = W[step][0] * d + W[step][1] * r
        x = x + d[:, :half]
        r = r - (d + pair_product(d[:, :half], slice(0, mid)) + pair_product(d[:, half:], slice(mid, 2 * mid)))
    solution[...] = x
    low_pair[...] = apply_n(r[:, :half], transfer_own[...]) + apply_n(r[:, half:], transfer_other[...])


def end_fixed(partial, other, matrix, fixed):
    fixed[...] = partial[...] + apply_t(other[...], matrix[...])


def start_correction(total, fixed, transfer, out):
    out[...] = total[...] + apply_t(fixed[...], transfer[:, : transfer.shape[1] // 2])


def end_correction(partial, other, transfer, out):
    unpack(other_product(partial, other[...], transfer), out)


def per_device(
    flips,
    right_side,
    operator_top,
    columns_top,
    aggregate_top,
    prolong_top,
    operator_mid,
    columns_mid,
    aggregate_mid,
    prolong_mid,
    operator_low,
    columns_low,
):
    def flip(value, level):
        return lax.ppermute(value, ("gx", "gy"), flips[level])

    rows = operator_top.shape[0]
    n_top = rows * N
    n_mid = n_top // 2
    n_low = n_mid // 2
    vec_top = ((S, n_top), F32)
    vec_mid = ((S, n_mid), F32)
    sums = [pltpu.VMEM((2 * rows, N, N), F32)] * 2
    mid_pieces = ((rows // 2 * n_mid + rows // 4 * N + 8, 2 * N), F32)
    low_pieces = ((rows // 4 * n_low, 2 * N), F32)

    other = flip(right_side, 0)
    matrix, first, product = call(
        "prepare_top",
        prepare_top,
        [((n_top, 4 * n_top), BF16), vec_top, vec_top],
        columns_top,
        right_side,
        operator_top,
        remote=range(3),
        scratch=[
            pltpu.SemaphoreType.DMA((1,)),
            pltpu.SMEM(columns_top.shape, jnp.int32),
            pltpu.VMEM(right_side.shape, F32),
            pltpu.VMEM(operator_top.shape, F32),
            pltpu.SemaphoreType.DMA((rows + 1,)),
        ]
        + sums,
        limit=14,
    )
    d1, r1 = call("step_first", step_first, [vec_top, vec_top], first, product, other, matrix)
    other = flip(d1, 0)
    product, send_mid = call(
        "prepare_mid",
        prepare_mid,
        [vec_top, mid_pieces],
        columns_mid,
        aggregate_mid,
        operator_mid,
        prolong_mid,
        d1,
        matrix,
        scratch=index_scratch(columns_mid, aggregate_mid) + sums,
    )
    mid_arrived = flip(send_mid, 1)
    d2, r2, total = call("step_second", step_second, [vec_top] * 3, first, d1, r1, product, other, matrix)
    other = flip(d2, 0)
    product, send_low, transfer = call(
        "prepare_low",
        prepare_low,
        [vec_top, low_pieces, ((n_top, 4 * n_mid), BF16)],
        columns_low,
        columns_top,
        aggregate_top,
        operator_low,
        prolong_top,
        d2,
        matrix,
        scratch=index_scratch(columns_low, columns_top, aggregate_top) + sums,
    )
    low_arrived = flip(send_low, 2)
    smoothed, other_part = call("step_third", step_third, [vec_top, vec_mid], d2, r2, product, other, matrix, transfer)
    arrived = flip(other_part, 0)
    own_part, smoothed_blocks, mid_own, transfer_own = call(
        "restrict_own",
        restrict_own,
        [vec_mid, ((rows, S, N), F32), ((n_mid, 4 * n_mid), BF16), ((n_mid, 4 * n_low), BF16)],
        smoothed,
        transfer,
        send_mid,
    )
    (solve_own,) = call("compose_low", compose_low, [low_pieces], send_low, low_arrived)
    (mid_side,) = call("add_mid", add_mid, [vec_mid], own_part, arrived, solve_own)
    other = flip(mid_side, 1)
    product, solve_own = call("own_mid", own_mid, [vec_mid, low_pieces], mid_side, mid_own, solve_own, aliases={2: 1})
    solve_other = flip(solve_own, 1)
    mid_other, transfer_other, product = call(
        "join_other",
        join_other,
        [((n_mid, 4 * n_mid), BF16), ((n_mid, 4 * n_low), BF16), vec_top],
        mid_arrived,
        mid_side,
        product,
    )
    low_pair, x_mid = call(
        "solve_mid",
        solve_mid,
        [((S, 2 * n_low), F32), vec_mid],
        product,
        mid_side,
        other,
        mid_own,
        mid_other,
        transfer_own,
        transfer_other,
    )
    other = flip(low_pair, 2)
    partial, fixing = call(
        "compose_fixed",
        compose_fixed,
        [vec_mid, ((n_mid, 4 * n_low), BF16)],
        solve_own,
        solve_other,
        transfer_own,
        low_pair,
        x_mid,
    )
    (mid_fixed,) = call("end_fixed", end_fixed, [vec_mid], partial, other, fixing)
    other = flip(mid_fixed, 0)
    (partial,) = call("start_correction", start_correction, [vec_top], total, mid_fixed, transfer)
    (correction,) = call("end_correction", end_correction, [((rows, S, N), F32)], partial, other, transfer)
    return correction, smoothed_blocks


def solution(mesh):
    n_gx, n_gy = mesh.shape["gx"], mesh.shape["gy"]
    masks = (n_gy // 2, n_gx // 2 * n_gy, n_gy // 4)
    flips = [[(source, source ^ mask) for source in range(n_gx * n_gy)] for mask in masks]
    lead = ("gx", "gy")
    in_specs = (
        P(lead, None, None),
        P(lead, None, None, None),
        P(lead, None),
        P(lead),
        P(lead, None, None),
        P(lead, None, None, None),
        P(lead, None),
        P(lead),
        P(lead, None, None),
        P(lead, None, None, None),
        P(lead, None),
    )
    out_specs = (P(lead, None, None), P(lead, None, None))
    return jax.shard_map(
        functools.partial(per_device, flips), mesh=mesh, in_specs=in_specs, out_specs=out_specs, check_vma=False
    )
```

time: 50.6 us -> 42.5 us (0.84)
  waiting for transfers between devices: 19.1 us -> 9.77 us
  starting transfers between devices: 17.3 us -> 19.3 us
  local copies, waits for them, and re-layouts: 2.19 us -> 1.3 us
    ppermute x10, waiting for transfers between devices: 19.1 us -> 9.77 us  [flip(): return lax.ppermute(value, ('gx', 'gy'), flips[level])]
    pallas_call x14 -> x16, Pallas kernels: 4.44 us -> 11.3 us  [call(): pl.pallas_call(body, name=name, out_shape=[pltpu.VMEM(shape, dtype) for s...]
    pallas_call x3 -> x0, Pallas kernels: 6.7 us -> none  [prepare(): pl.pallas_call(body, name=name, out_shape=[pltpu.VMEM(shape, dtype) for s...]
    ppermute x10, starting transfers between devices: 17.3 us -> 19.3 us  [flip(): return lax.ppermute(value, ('gx', 'gy'), flips[level])]
    unnamed x24 -> x20, local copies, waits for them, and re-layouts: 2.19 us -> 1.3 us
  transfers between devices with their start and end apart: 10 -> 10, of which waited for: 6 -> 6; matrix products, arithmetic and copies ran while one was open for 1% -> 1% of each run, Pallas kernels for 19% -> 25%
where the time goes in v2:
time: 42.5 us; the launch traced here: 42.4 us
  starting transfers between devices  19.3 us (45%)
  Pallas kernels  11.3 us (27%)
  waiting for transfers between devices  9.77 us (23%)
  local copies, waits for them, and re-layouts  1.3 us (3%)
  between operations  0.79 us (2%)
    ppermute x10, starting transfers between devices, flip(): return lax.ppermute(value, ('gx', 'gy'), flips[level])  19.3 us
    pallas_call x16, Pallas kernels, call(): pl.pallas_call(body, name=name, out_shape=[pltpu.VMEM(shape, dtype) for s...  11.3 us
    ppermute x10, waiting for transfers between devices, flip(): return lax.ppermute(value, ('gx', 'gy'), flips[level])  9.77 us
    unnamed x20, local copies, waits for them, and re-layouts  1.3 us
  transfers between devices with their start and end apart: 10, of which 6 were waited for; matrix products, arithmetic and copies ran while one was open for 1% of the time, Pallas kernels for 25%

profile of v2, /device:TPU:128, one launch (start us, length us, event | category | flops | bytes accessed | tf_op | source)
XLA Modules:
  0.0 42.4 jit_solution(17463633862269587784)
XLA Ops:
  0.6 3.1 %collective-permute-start = (f32[8,8,64]{2,1,0:T(8,128)}, f32[8,8,64]{2,1,0:T(8,128)S(1)}, u32[]{:S(2)}, u32[]{:S(2)}) collective-permute-start(f32[8,8,64]{2,1,0:T(8,128)} %side_in.1), channel_id=1, source_target_pairs={{0,16},{1,17},{2,18},{3,19},{4,20},{5,21},{6,22},{7,23},{8,24},{9,... | collective-permute-start | bytes 49160 | tf_op jit(solution)/shard_map/ppermute | solution.py:387
  3.7 4.0 %prepare_top.1 = (bf16[512,2048]{1,0:T(8,128)(2,1)S(1)}, f32[8,512]{1,0:T(8,128)S(1)}, f32[8,512]{1,0:T(8,128)S(1)}) custom-call(s32[8,27]{1,0:T(8,128)} %cols_top_in.1, f32[8,8,64]{2,1,0:T(8,128)} %side_in.1, f32[8,27,64,64]{3,2,1,0:T(8,128)} %remote.1), custom_call_target="tpu_custom_call" | custom-call | flops 4000000000 | tf_op jit(solution)/shard_map/prepare_top/pallas_call | solution.py:37
  7.8 0.4 step_first.1
  8.2 1.7 %collective-permute-start.1 = (f32[8,512]{1,0:T(8,128)S(1)}, f32[8,512]{1,0:T(8,128)S(1)}, u32[]{:S(2)}, u32[]{:S(2)}) collective-permute-start(f32[8,512]{1,0:T(8,128)S(1)} %get-tuple-element.33.direction.old), channel_id=1, source_target_pairs={{0,16},{1,17},{2,18},{3,19},{4,20},{5,21},{6,22},{7,23},{8,24},{9,... | collective-permute-start | bytes 49160 | tf_op jit(solution)/shard_map/ppermute | solution.py:387
  9.9 1.6 %prepare_mid.1 = (f32[8,512]{1,0:T(8,128)S(1)}, f32[1160,128]{1,0:T(8,128)S(1)}) custom-call(s32[4,27]{1,0:T(4,128)S(1)} %copy-done.5, s32[4]{0:T(128)S(1)} %copy-done.7, f32[4,27,64,64]{3,2,1,0:T(8,128)S(1)} %copy-done, f32[4,64,64]{2,1,0:T(8,128)S(1)} %copy-done.3, f32[8,512]{1,0:T(8,128)S(1)} %get-tuple-element.33.direction.old, ...), custom_call_target="tpu_custom_call" | custom-call | flops 200000000 | tf_op jit(solution)/shard_map/prepare_mid/pallas_call | solution.py:37
  11.5 3.3 %collective-permute-start.6 = (f32[1160,128]{1,0:T(8,128)S(1)}, f32[1160,128]{1,0:T(8,128)S(1)}, u32[]{:S(2)}, u32[]{:S(2)}) collective-permute-start(f32[1160,128]{1,0:T(8,128)S(1)} %get-tuple-element.42.source), channel_id=1, source_target_pairs={{0,128},{1,129},{2,130},{3,131},{4,132},{5,133},{6,134},{7,135},{8... | collective-permute-start | bytes 1781768 | tf_op jit(solution)/shard_map/ppermute | solution.py:387
  14.8 0.4 step_second.1
  15.2 2.0 %collective-permute-start.2 = (f32[8,512]{1,0:T(8,128)S(1)}, f32[8,512]{1,0:T(8,128)S(1)}, u32[]{:S(2)}, u32[]{:S(2)}) collective-permute-start(f32[8,512]{1,0:T(8,128)S(1)} %get-tuple-element.37.direction.old), channel_id=1, source_target_pairs={{0,16},{1,17},{2,18},{3,19},{4,20},{5,21},{6,22},{7,23},{8,24},{9,... | collective-permute-start | bytes 49160 | tf_op jit(solution)/shard_map/ppermute | solution.py:387
  17.2 1.3 %prepare_low.1 = (f32[8,512]{1,0:T(8,128)S(1)}, f32[256,128]{1,0:T(8,128)S(1)}, bf16[512,1024]{1,0:T(8,128)(2,1)S(1)}) custom-call(s32[2,27]{1,0:T(2,128)S(1)} %copy-done.6, s32[8,27]{1,0:T(8,128)S(1)} %copy-done.4, s32[8]{0:T(128)S(1)} %copy-done.8, f32[2,27,64,64]{3,2,1,0:T(8,128)S(1)} %copy-done.1, f32[8,64,64]{2,1,0:T(8,128)S(1)} %copy-done.2, ...), custom_call_target="tpu_custom_call" | custom-call | flops 200000000 | tf_op jit(solution)/shard_map/prepare_low/pallas_call | solution.py:37
  18.5 0.7 %collective-permute-start.4 = (f32[256,128]{1,0:T(8,128)S(1)}, f32[256,128]{1,0:T(8,128)S(1)}, u32[]{:S(2)}, u32[]{:S(2)}) collective-permute-start(f32[256,128]{1,0:T(8,128)S(1)} %get-tuple-element.45.own), channel_id=1, source_target_pairs={{0,8},{1,9},{2,10},{3,11},{4,12},{5,13},{6,14},{7,15},{8,0},{9,1},... | collective-permute-start | bytes 393224 | tf_op jit(solution)/shard_map/ppermute | solution.py:387
  19.2 1.3 %collective-permute-done.2.other = f32[8,512]{1,0:T(8,128)S(1)} collective-permute-done((f32[8,512]{1,0:T(8,128)S(1)}, f32[8,512]{1,0:T(8,128)S(1)}, u32[]{:S(2)}, u32[]{:S(2)}) %collective-permute-start.2) | collective-permute-done | bytes 16416 | tf_op jit(solution)/shard_map/ppermute | solution.py:387
  20.5 0.5 %step_third.1 = (f32[8,512]{1,0:T(8,128)S(1)}, f32[8,256]{1,0:T(8,128)S(1)}) custom-call(f32[8,512]{1,0:T(8,128)S(1)} %get-tuple-element.37.direction.old, f32[8,512]{1,0:T(8,128)S(1)} %get-tuple-element.38.residual, f32[8,512]{1,0:T(8,128)S(1)} %get-tuple-element.39.product, f32[8,512]{1,0:T(8,128)S(1)} %collective-permute-done.2.other, ...), custom_call_target="tpu_custom_call" | custom-call | flops 6000000000 | tf_op jit(solution)/shard_map/step_third/pallas_call | solution.py:37
  21.1 2.1 %collective-permute-start.3 = (f32[8,256]{1,0:T(8,128)S(1)}, f32[8,256]{1,0:T(8,128)S(1)}, u32[]{:S(2)}, u32[]{:S(2)}) collective-permute-start(f32[8,256]{1,0:T(8,128)S(1)} %get-tuple-element.44), channel_id=1, source_target_pairs={{0,16},{1,17},{2,18},{3,19},{4,20},{5,21},{6,22},{7,23},{8,24},{9,... | collective-permute-start | bytes 24584 | tf_op jit(solution)/shard_map/ppermute | solution.py:387
  23.1 0.3 restrict_own.1
  23.4 0.6 %copy.16 = f32[8,8,64]{2,1,0:T(8,128)} copy(f32[8,8,64]{2,1,0:T(8,128)S(1)} %get-tuple-element.59) | data formatting | bytes 32768
  24.1 0.2 compose_low.1.after.low
  24.3 1.9 %collective-permute-done.3.b = f32[8,256]{1,0:T(8,128)S(1)} collective-permute-done((f32[8,256]{1,0:T(8,128)S(1)}, f32[8,256]{1,0:T(8,128)S(1)}, u32[]{:S(2)}, u32[]{:S(2)}) %collective-permute-start.3) | collective-permute-done | bytes 8224 | tf_op jit(solution)/shard_map/ppermute | solution.py:387
  26.2 2.1 %collective-permute-start.7 = (f32[8,256]{1,0:T(8,128)S(1)}, f32[8,256]{1,0:T(8,128)S(1)}, u32[]{:S(2)}, u32[]{:S(2)}) collective-permute-start(f32[8,256]{1,0:T(8,128)S(1)} %add_mid.1.side.own), channel_id=1, source_target_pairs={{0,128},{1,129},{2,130},{3,131},{4,132},{5,133},{6,134},{7,135},{8... | collective-permute-start | bytes 24584 | tf_op jit(solution)/shard_map/ppermute | solution.py:387
  28.3 0.2 own_mid.1
  28.5 1.5 %collective-permute-start.5 = (f32[256,128]{1,0:T(8,128)S(1)}, f32[256,128]{1,0:T(8,128)S(1)}, u32[]{:S(2)}, u32[]{:S(2)}) collective-permute-start(f32[256,128]{1,0:T(8,128)S(1)} %get-tuple-element.47.own), channel_id=1, source_target_pairs={{0,128},{1,129},{2,130},{3,131},{4,132},{5,133},{6,134},{7,135},{8... | collective-permute-start | bytes 393224 | tf_op jit(solution)/shard_map/ppermute | solution.py:387
  29.9 0.3 join_other.1
  30.2 1.1 %collective-permute-done.7.other = f32[8,256]{1,0:T(8,128)S(1)} collective-permute-done((f32[8,256]{1,0:T(8,128)S(1)}, f32[8,256]{1,0:T(8,128)S(1)}, u32[]{:S(2)}, u32[]{:S(2)}) %collective-permute-start.7) | collective-permute-done | bytes 8224 | tf_op jit(solution)/shard_map/ppermute | solution.py:387
  31.4 1.1 %solve_mid.1 = (f32[8,256]{1,0:T(8,128)S(1)}, f32[8,256]{1,0:T(8,128)S(1)}) custom-call(f32[8,512]{1,0:T(8,128)S(1)} %get-tuple-element.50.product, f32[8,256]{1,0:T(8,128)S(1)} %add_mid.1.side.own, f32[8,256]{1,0:T(8,128)S(1)} %collective-permute-done.7.other, bf16[256,1024]{1,0:T(8,128)(2,1)S(1)} %get-tuple-element.46.matrix.matrix_own, ...), custom_call_target="tpu_custom_call" | custom-call | flops 20000000000 | tf_op jit(solution)/shard_map/solve_mid/pallas_call | solution.py:37
  32.4 0.7 %collective-permute-start.8 = (f32[8,256]{1,0:T(8,128)S(1)}, f32[8,256]{1,0:T(8,128)S(1)}, u32[]{:S(2)}, u32[]{:S(2)}) collective-permute-start(f32[8,256]{1,0:T(8,128)S(1)} %get-tuple-element.53.pair), channel_id=1, source_target_pairs={{0,8},{1,9},{2,10},{3,11},{4,12},{5,13},{6,14},{7,15},{8,0},{9,1},... | collective-permute-start | bytes 24584 | tf_op jit(solution)/shard_map/ppermute | solution.py:387
  33.2 1.8 %collective-permute-done.5.other = f32[256,128]{1,0:T(8,128)S(1)} collective-permute-done((f32[256,128]{1,0:T(8,128)S(1)}, f32[256,128]{1,0:T(8,128)S(1)}, u32[]{:S(2)}, u32[]{:S(2)}) %collective-permute-start.5) | collective-permute-done | bytes 131104 | tf_op jit(solution)/shard_map/ppermute | solution.py:387
  35.0 0.5 %compose_fixed.1 = (f32[8,256]{1,0:T(8,128)S(1)}, bf16[256,512]{1,0:T(8,128)(2,1)S(1)}) custom-call(f32[256,128]{1,0:T(8,128)S(1)} %get-tuple-element.47.own, f32[256,128]{1,0:T(8,128)S(1)} %collective-permute-done.5.other, bf16[256,512]{1,0:T(8,128)(2,1)S(1)} %get-tuple-element.48.transfer_own.transfer, f32[8,256]{1,0:T(8,128)S(1)} %get-tuple-element.53.pair, ...), custom_call_target="tpu_custom_call" | custom-call | flops 200000000 | tf_op jit(solution)/shard_map/compose_fixed/pallas_call | solution.py:37
  35.5 0.7 %collective-permute-done.8.other = f32[8,256]{1,0:T(8,128)S(1)} collective-permute-done((f32[8,256]{1,0:T(8,128)S(1)}, f32[8,256]{1,0:T(8,128)S(1)}, u32[]{:S(2)}, u32[]{:S(2)}) %collective-permute-start.8) | collective-permute-done | bytes 8224 | tf_op jit(solution)/shard_map/ppermute | solution.py:387
  36.3 2.1 %collective-permute-start.9 = (f32[8,256]{1,0:T(8,128)S(1)}, f32[8,256]{1,0:T(8,128)S(1)}, u32[]{:S(2)}, u32[]{:S(2)}) collective-permute-start(f32[8,256]{1,0:T(8,128)S(1)} %end_fixed.1.fixed), channel_id=1, source_target_pairs={{0,16},{1,17},{2,18},{3,19},{4,20},{5,21},{6,22},{7,23},{8,24},{9,... | collective-permute-start | bytes 24584 | tf_op jit(solution)/shard_map/ppermute | solution.py:387
  38.4 0.2 start_correction.1.partial
  38.7 2.8 %collective-permute-done.9.other = f32[8,256]{1,0:T(8,128)S(1)} collective-permute-done((f32[8,256]{1,0:T(8,128)S(1)}, f32[8,256]{1,0:T(8,128)S(1)}, u32[]{:S(2)}, u32[]{:S(2)}) %collective-permute-start.9) | collective-permute-done | bytes 8224 | tf_op jit(solution)/shard_map/ppermute | solution.py:387
  41.5 0.3 end_correction.1
  41.8 0.6 %copy.15 = f32[8,8,64]{2,1,0:T(8,128)} copy(f32[8,8,64]{2,1,0:T(8,128)S(1)} %end_correction.1) | data formatting | bytes 32768
  (24 shorter events, 0.2 us)
Async XLA Ops:
  0.6 7.1 %collective-permute-start = (f32[8,8,64]{2,1,0:T(8,128)}, f32[8,8,64]{2,1,0:T(8,128)S(1)}, u32[]{:S(2)}, u32[]{:S(2)}) collective-permute-start(f32[8,8,64]{2,1,0:T(8,128)} %side_in.1), channel_id=1, source_target_pairs={{0,16},{1,17},{2,18},{3,19},{4,20},{5,21},{6,22},{7,23},{8,24},{9,... | collective-permute-start | bytes 49160 | tf_op jit(solution)/shard_map/ppermute | solution.py:387
  7.7 2.2 %copy-start = (f32[4,27,64,64]{3,2,1,0:T(8,128)S(1)}, f32[4,27,64,64]{3,2,1,0:T(8,128)}, u32[]{:S(2)}) copy-start(f32[4,27,64,64]{3,2,1,0:T(8,128)} %blocks.2) | copy-start | bytes 5308420
  7.7 2.1 %copy-start.3 = (f32[4,64,64]{2,1,0:T(8,128)S(1)}, f32[4,64,64]{2,1,0:T(8,128)}, u32[]{:S(2)}) copy-start(f32[4,64,64]{2,1,0:T(8,128)} %prolong.2) | copy-start | bytes 196612
  7.7 2.1 %copy-start.5 = (s32[4,27]{1,0:T(4,128)S(1)}, s32[4,27]{1,0:T(4,128)}, u32[]{:S(2)}) copy-start(s32[4,27]{1,0:T(4,128)} %cols_in.4) | copy-start | bytes 1300
  7.7 2.1 %copy-start.7 = (s32[4]{0:T(128)S(1)}, s32[4]{0:T(128)}, u32[]{:S(2)}) copy-start(s32[4]{0:T(128)} %agg_in.2) | copy-start | bytes 52
  8.2 6.6 %collective-permute-start.1 = (f32[8,512]{1,0:T(8,128)S(1)}, f32[8,512]{1,0:T(8,128)S(1)}, u32[]{:S(2)}, u32[]{:S(2)}) collective-permute-start(f32[8,512]{1,0:T(8,128)S(1)} %get-tuple-element.33.direction.old), channel_id=1, source_target_pairs={{0,16},{1,17},{2,18},{3,19},{4,20},{5,21},{6,22},{7,23},{8,24},{9,... | collective-permute-start | bytes 49160 | tf_op jit(solution)/shard_map/ppermute | solution.py:387
  11.5 18.5 %collective-permute-start.6 = (f32[1160,128]{1,0:T(8,128)S(1)}, f32[1160,128]{1,0:T(8,128)S(1)}, u32[]{:S(2)}, u32[]{:S(2)}) collective-permute-start(f32[1160,128]{1,0:T(8,128)S(1)} %get-tuple-element.42.source), channel_id=1, source_target_pairs={{0,128},{1,129},{2,130},{3,131},{4,132},{5,133},{6,134},{7,135},{8... | collective-permute-start | bytes 1781768 | tf_op jit(solution)/shard_map/ppermute | solution.py:387
  14.7 2.4 %copy-start.1 = (f32[2,27,64,64]{3,2,1,0:T(8,128)S(1)}, f32[2,27,64,64]{3,2,1,0:T(8,128)}, u32[]{:S(2)}) copy-start(f32[2,27,64,64]{3,2,1,0:T(8,128)} %blocks.3) | copy-start | bytes 2654212
  14.8 2.4 %copy-start.2 = (f32[8,64,64]{2,1,0:T(8,128)S(1)}, f32[8,64,64]{2,1,0:T(8,128)}, u32[]{:S(2)}) copy-start(f32[8,64,64]{2,1,0:T(8,128)} %prolong.3) | copy-start | bytes 393220
  14.8 2.4 %copy-start.4 = (s32[8,27]{1,0:T(8,128)S(1)}, s32[8,27]{1,0:T(8,128)}, u32[]{:S(2)}) copy-start(s32[8,27]{1,0:T(8,128)} %cols_top_in.1) | copy-start | bytes 2596
  14.8 2.4 %copy-start.6 = (s32[2,27]{1,0:T(2,128)S(1)}, s32[2,27]{1,0:T(2,128)}, u32[]{:S(2)}) copy-start(s32[2,27]{1,0:T(2,128)} %cols_in.5) | copy-start | bytes 652
  14.8 2.4 %copy-start.8 = (s32[8]{0:T(128)S(1)}, s32[8]{0:T(128)}, u32[]{:S(2)}) copy-start(s32[8]{0:T(128)} %agg_in.3) | copy-start | bytes 100
  15.2 5.3 %collective-permute-start.2 = (f32[8,512]{1,0:T(8,128)S(1)}, f32[8,512]{1,0:T(8,128)S(1)}, u32[]{:S(2)}, u32[]{:S(2)}) collective-permute-start(f32[8,512]{1,0:T(8,128)S(1)} %get-tuple-element.37.direction.old), channel_id=1, source_target_pairs={{0,16},{1,17},{2,18},{3,19},{4,20},{5,21},{6,22},{7,23},{8,24},{9,... | collective-permute-start | bytes 49160 | tf_op jit(solution)/shard_map/ppermute | solution.py:387
  18.5 5.6 %collective-permute-start.4 = (f32[256,128]{1,0:T(8,128)S(1)}, f32[256,128]{1,0:T(8,128)S(1)}, u32[]{:S(2)}, u32[]{:S(2)}) collective-permute-start(f32[256,128]{1,0:T(8,128)S(1)} %get-tuple-element.45.own), channel_id=1, source_target_pairs={{0,8},{1,9},{2,10},{3,11},{4,12},{5,13},{6,14},{7,15},{8,0},{9,1},... | collective-permute-start | bytes 393224 | tf_op jit(solution)/shard_map/ppermute | solution.py:387
  21.1 5.2 %collective-permute-start.3 = (f32[8,256]{1,0:T(8,128)S(1)}, f32[8,256]{1,0:T(8,128)S(1)}, u32[]{:S(2)}, u32[]{:S(2)}) collective-permute-start(f32[8,256]{1,0:T(8,128)S(1)} %get-tuple-element.44), channel_id=1, source_target_pairs={{0,16},{1,17},{2,18},{3,19},{4,20},{5,21},{6,22},{7,23},{8,24},{9,... | collective-permute-start | bytes 24584 | tf_op jit(solution)/shard_map/ppermute | solution.py:387
  26.2 5.2 %collective-permute-start.7 = (f32[8,256]{1,0:T(8,128)S(1)}, f32[8,256]{1,0:T(8,128)S(1)}, u32[]{:S(2)}, u32[]{:S(2)}) collective-permute-start(f32[8,256]{1,0:T(8,128)S(1)} %add_mid.1.side.own), channel_id=1, source_target_pairs={{0,128},{1,129},{2,130},{3,131},{4,132},{5,133},{6,134},{7,135},{8... | collective-permute-start | bytes 24584 | tf_op jit(solution)/shard_map/ppermute | solution.py:387
  28.5 6.5 %collective-permute-start.5 = (f32[256,128]{1,0:T(8,128)S(1)}, f32[256,128]{1,0:T(8,128)S(1)}, u32[]{:S(2)}, u32[]{:S(2)}) collective-permute-start(f32[256,128]{1,0:T(8,128)S(1)} %get-tuple-element.47.own), channel_id=1, source_target_pairs={{0,128},{1,129},{2,130},{3,131},{4,132},{5,133},{6,134},{7,135},{8... | collective-permute-start | bytes 393224 | tf_op jit(solution)/shard_map/ppermute | solution.py:387
  32.4 3.7 %collective-permute-start.8 = (f32[8,256]{1,0:T(8,128)S(1)}, f32[8,256]{1,0:T(8,128)S(1)}, u32[]{:S(2)}, u32[]{:S(2)}) collective-permute-start(f32[8,256]{1,0:T(8,128)S(1)} %get-tuple-element.53.pair), channel_id=1, source_target_pairs={{0,8},{1,9},{2,10},{3,11},{4,12},{5,13},{6,14},{7,15},{8,0},{9,1},... | collective-permute-start | bytes 24584 | tf_op jit(solution)/shard_map/ppermute | solution.py:387
  36.3 5.2 %collective-permute-start.9 = (f32[8,256]{1,0:T(8,128)S(1)}, f32[8,256]{1,0:T(8,128)S(1)}, u32[]{:S(2)}, u32[]{:S(2)}) collective-permute-start(f32[8,256]{1,0:T(8,128)S(1)} %end_fixed.1.fixed), channel_id=1, source_target_pairs={{0,16},{1,17},{2,18},{3,19},{4,20},{5,21},{6,22},{7,23},{8,24},{9,... | collective-permute-start | bytes 24584 | tf_op jit(solution)/shard_map/ppermute | solution.py:387

commit v3 on v2

--- a/solution.py
+++ b/solution.py
@@ -31,15 +31,18 @@
 COST = {"prepare_top": 4000, "step_first": 4000, "step_second": 100000, "step_third": 6000, "solve_mid": 20000}
 
 
-def call(name, body, outs, *args, remote=(), scratch=(), aliases=None, limit=8):
-    spaces = [pltpu.HBM if at in remote else pltpu.VMEM for at in range(len(args))]
+def call(name, body, outs, *args, remote=(), scalars=(), scratch=(), aliases=None, limit=8):
+    spaces = [
+        pltpu.HBM if at in remote else pltpu.SMEM if at in scalars else pltpu.VMEM for at in range(len(args))
+    ]
     args = [pltpu.with_memory_space_constraint(a, m) for a, m in zip(args, spaces)]
+    places = [pltpu.SMEM if dtype == jnp.int32 else pltpu.VMEM for _, dtype in outs]
     return pl.pallas_call(
         body,
         name=name,
-        out_shape=[pltpu.VMEM(shape, dtype) for shape, dtype in outs],
+        out_shape=[place(shape, dtype) for place, (shape, dtype) in zip(places, outs)],
         in_specs=[pl.BlockSpec(memory_space=m) for m in spaces],
-        out_specs=[pl.BlockSpec(memory_space=pltpu.VMEM)] * len(outs),
+        out_specs=[pl.BlockSpec(memory_space=m) for m in places],
         scratch_shapes=scratch,
         input_output_aliases=aliases or {},
         cost_estimate=pl.CostEstimate(flops=COST.get(name, 200) * 1000000, bytes_accessed=0, transcendentals=0),
@@ -59,10 +62,6 @@
     return wait
 
 
-def index_scratch(*arrays):
-    return [pltpu.SemaphoreType.DMA((len(arrays),))] + [pltpu.SMEM(a.shape, jnp.int32) for a in arrays]
-
-
 def split(value):
     high = value.astype(BF16)
     return high, (value - high.astype(F32)).astype(BF16)
@@ -81,6 +80,12 @@
     both = jnp.concatenate([both, both], axis=1)
     out = lax.dot_general(both, matrix, (((1,), (1,)), ((), ())), preferred_element_type=F32)
     return fold(out)
+
+
+def apply_turned(vector, matrix):
+    both = stack(vector)
+    both = jnp.concatenate([both, both], axis=1)
+    return fold(jnp.dot(both, matrix, preferred_element_type=F32))
 
 
 def apply_n(vector, matrix):
@@ -136,7 +141,11 @@
     return pl.ds(pl.multiple_of(b * N, N), N)
 
 
-def prepare_top(cols_in, side_in, remote, matrix, first, product, small, cols, side, held, sems, *sums):
+def prepare_top(
+    cols_in, side_in, remote, agg_in, cols_mid_in, agg_mid_in, cols_low_in,
+    matrix, first, product, agg, cols_mid, agg_mid, cols_low,
+    small, cols, side, held, sems, *sums
+):
     rows = remote.shape[0]
     wait = copies((cols_in,), (cols,), small)
 
@@ -145,7 +154,11 @@
 
     for b in range(rows):
         fetch(b).start()
-    wait_side = copies((side_in,), (side,), sems.at[pl.ds(rows, 1)])
+    wait_more = copies(
+        (side_in, agg_in, cols_mid_in, agg_mid_in, cols_low_in),
+        (side, agg, cols_mid, agg_mid, cols_low),
+        sems.at[pl.ds(rows, 5)],
+    )
     wait()
     device = cols[0, 0] // rows
 
@@ -159,7 +172,7 @@
         return carry
 
     lax.fori_loop(0, rows // len(sums), some, 0)
-    wait_side()
+    wait_more()
     own = pack(side)
     first[...] = own
     product[...] = apply_t(own, matrix[:, : 2 * rows * N])
@@ -181,22 +194,19 @@
     lax.fori_loop(0, rows // len(sums), some, 0)
 
 
-def prepare_mid(cols_in, agg_in, blocks, prolong, direction, matrix, product, send, small, cols, agg, *sums):
-    wait = copies((cols_in, agg_in), (cols, agg), small)
-    own_product(direction, matrix, product)
+def prepare_mid(cols, agg, blocks, prolong, after, send, *sums):
     rows = blocks.shape[0]
     half = rows // 2
     n_mid = rows * N
+
+    def put(b, c, value):
+        send[pl.ds(pl.multiple_of(c * n_mid + b * N, N), N)] = value
+
+    collapse_out(cols, blocks, put, sums)
     at = rows * n_mid
     for p in range(half):
         send[at + p * N : at + (p + 1) * N] = jnp.concatenate([prolong[2 * p], prolong[2 * p + 1]], axis=1)
     at += half * N
-    wait()
-
-    def put(b, c, value):
-        send[pl.ds(pl.multiple_of(c * n_mid + b * N, N), N)] = value
-
-    collapse_out(cols, blocks, put, sums)
     device = cols[0, 0] // rows
     row = lax.broadcasted_iota(jnp.int32, (8, 2 * N), 0)
     joined = jnp.zeros((8, 2 * N), jnp.int32)
@@ -206,25 +216,34 @@
 
 
 def prepare_low(
-    cols_in, cols_top_in, agg_in, blocks, prolong, direction, matrix, product, send, transfer, small, cols, cols_top, agg, *sums
+    cols, agg, blocks, prolong, direction, residual, matrix, send, transfer, turned, known, part, restrict, *sums
 ):
-    wait = copies((cols_in, cols_top_in, agg_in), (cols, cols_top, agg), small)
-    own_product(direction, matrix, product)
+    turned[...] = matrix[:, matrix.shape[1] // 2 :].T
+    known[...] = residual[...] - (direction[...] + apply_t(direction[...], matrix[:, : matrix.shape[1] // 2]))
     n_low = blocks.shape[0] * N
-    wait()
 
     def put(b, c, value):
         send[pl.ds(pl.multiple_of(c * n_low + b * N, N), N)] = value
 
     collapse_out(cols, blocks, put, sums)
     rows = prolong.shape[0]
-    device = cols_top[0, 0] // rows
+    device = cols[0, 0] // blocks.shape[0]
     for b in range(rows):
         at = local(agg[b], rows // 2, device)
         put_halves(transfer, slice(b * N, (b + 1) * N), spread(at, rows // 2, prolong[b]))
-
-
-def own_product(vector, matrix, product):
+    half = transfer.shape[1] // 2
+    part[...] = apply_n(known[...], transfer[:, half:])
+    depth = turned.shape[0] // 2
+    high, low = split(
+        multiply(
+            (turned[:depth], turned[depth:]), (transfer[:, half : half + half // 2], transfer[:, half + half // 2 :])
+        )
+    )
+    restrict[:depth] = high
+    restrict[depth:] = low
+
+
+def own_product(vector, matrix, after, product):
     product[...] = apply_t(vector[...], matrix[:, : matrix.shape[1] // 2])
 
 
@@ -248,14 +267,12 @@
     total[...] = first[...] + d + new
 
 
-def step_third(old, residual, product, other, matrix, transfer, new_residual, other_part):
-    r = residual[...] - (old[...] + other_product(product, other[...], matrix))
-    new_residual[...] = r
-    other_part[...] = apply_n(r, transfer[:, transfer.shape[1] // 2 :])
-
-
-def restrict_own(residual, transfer_top, source, own_part, out, matrix, transfer):
-    r = residual[...]
+def step_third(part, other, restrict, other_part):
+    other_part[...] = part[...] - apply_turned(other[...], restrict[...])
+
+
+def restrict_own(known, other, turned, transfer_top, source, own_part, out, matrix, transfer):
+    r = known[...] - apply_turned(other[...], turned[...])
     own_part[...] = apply_n(r, transfer_top[:, : transfer_top.shape[1] // 2])
     unpack(r, out)
     join_mid(source, matrix, transfer, False)
@@ -266,19 +283,19 @@
 
 
 def own_mid(side, matrix, low, product, low_out):
-    product[...] = apply_t(side[...], matrix[:, : matrix.shape[1] // 2])
+    product[...] = apply_turned(side[...], matrix[: matrix.shape[0] // 2])
 
 
 def join_mid(source, matrix, transfer, turn):
-    n_mid = matrix.shape[0]
+    n_mid = matrix.shape[1]
     rows = n_mid // N
     half = rows // 2
     for c in range(rows):
         to = (c + half) % rows if turn else c
-        high, low = split(source[c * n_mid : (c + 1) * n_mid])
+        high, low = split(source[c * n_mid : (c + 1) * n_mid].T)
         base = (to // half) * 2 * n_mid + (to % half) * 2 * N
-        matrix[:, base : base + 2 * N] = high
-        matrix[:, base + n_mid : base + n_mid + 2 * N] = low
+        matrix[base : base + 2 * N] = high
+        matrix[base + n_mid : base + n_mid + 2 * N] = low
     at = rows * n_mid
     joined = at + half * N
     for b in range(rows):
@@ -296,7 +313,8 @@
 
 def join_other(source, side, own, matrix, transfer, product):
     join_mid(source, matrix, transfer, True)
-    product[...] = jnp.concatenate([own[...], apply_t(side[...], matrix[:, : matrix.shape[1] // 2])], axis=1)
+    other = apply_turned(side[...], matrix[: matrix.shape[0] // 2])
+    product[...] = jnp.concatenate([own[...], other], axis=1)
 
 
 def multiply(a, b):
@@ -332,18 +350,18 @@
         near.append(product[:, :half])
         far.append(product[:, half:])
     partial[...] = fine[...] + apply_t(pair[...], jnp.concatenate(split(jnp.concatenate(near, axis=1)), axis=1))
-    high, low = split(jnp.concatenate(far, axis=1))
-    matrix[:, :width] = high
-    matrix[:, width:] = low
+    high, low = split(jnp.concatenate(far, axis=1).T)
+    matrix[:width] = high
+    matrix[width:] = low
 
 
 def solve_mid(product, own, other, matrix_own, matrix_other, transfer_own, transfer_other, low_pair, solution):
     half = own.shape[1]
-    mid = matrix_own.shape[1] // 2
+    mid = matrix_own.shape[0] // 2
 
     def pair_product(value, columns):
         return jnp.concatenate(
-            [apply_t(value, matrix_own[:, columns]), apply_t(value, matrix_other[:, columns])], axis=1
+            [apply_turned(value, matrix_own[columns]), apply_turned(value, matrix_other[columns])], axis=1
         )
 
     d = jnp.concatenate([own[...], other[...]], axis=1)
@@ -358,15 +376,17 @@
 
 
 def end_fixed(partial, other, matrix, fixed):
-    fixed[...] = partial[...] + apply_t(other[...], matrix[...])
-
-
-def start_correction(total, fixed, transfer, out):
-    out[...] = total[...] + apply_t(fixed[...], transfer[:, : transfer.shape[1] // 2])
-
-
-def end_correction(partial, other, transfer, out):
-    unpack(other_product(partial, other[...], transfer), out)
+    fixed[...] = partial[...] + apply_turned(other[...], matrix[...])
+
+
+def start_correction(total, fixed, transfer, out, turned):
+    half = transfer.shape[1] // 2
+    turned[...] = transfer[:, half:].T
+    out[...] = total[...] + apply_t(fixed[...], transfer[:, :half])
+
+
+def end_correction(partial, other, turned, out):
+    unpack(partial[...] + apply_turned(other[...], turned[...]), out)
 
 
 def per_device(
@@ -397,62 +417,68 @@
     low_pieces = ((rows // 4 * n_low, 2 * N), F32)
 
     other = flip(right_side, 0)
-    matrix, first, product = call(
+    indices = (aggregate_top, columns_mid, aggregate_mid, columns_low)
+    matrix, first, product, agg_top, cols_mid, agg_mid, cols_low = call(
         "prepare_top",
         prepare_top,
-        [((n_top, 4 * n_top), BF16), vec_top, vec_top],
+        [((n_top, 4 * n_top), BF16), vec_top, vec_top] + [(a.shape, jnp.int32) for a in indices],
         columns_top,
         right_side,
         operator_top,
-        remote=range(3),
+        *indices,
+        remote=range(7),
         scratch=[
             pltpu.SemaphoreType.DMA((1,)),
             pltpu.SMEM(columns_top.shape, jnp.int32),
             pltpu.VMEM(right_side.shape, F32),
             pltpu.VMEM(operator_top.shape, F32),
-            pltpu.SemaphoreType.DMA((rows + 1,)),
+            pltpu.SemaphoreType.DMA((rows + 5,)),
         ]
         + sums,
         limit=14,
     )
     d1, r1 = call("step_first", step_first, [vec_top, vec_top], first, product, other, matrix)
     other = flip(d1, 0)
-    product, send_mid = call(
+    (send_mid,) = call(
         "prepare_mid",
         prepare_mid,
-        [vec_top, mid_pieces],
-        columns_mid,
-        aggregate_mid,
+        [mid_pieces],
+        cols_mid,
+        agg_mid,
         operator_mid,
         prolong_mid,
         d1,
-        matrix,
-        scratch=index_scratch(columns_mid, aggregate_mid) + sums,
+        scalars=(0, 1),
+        scratch=sums,
     )
     mid_arrived = flip(send_mid, 1)
+    (product,) = call("own_top", own_product, [vec_top], d1, matrix, send_mid)
     d2, r2, total = call("step_second", step_second, [vec_top] * 3, first, d1, r1, product, other, matrix)
     other = flip(d2, 0)
-    product, send_low, transfer = call(
+    send_low, transfer, turned, known, part, restrict = call(
         "prepare_low",
         prepare_low,
-        [vec_top, low_pieces, ((n_top, 4 * n_mid), BF16)],
-        columns_low,
-        columns_top,
-        aggregate_top,
+        [low_pieces, ((n_top, 4 * n_mid), BF16), ((2 * n_top, n_top), BF16), vec_top, vec_mid, ((2 * n_top, n_mid), BF16)],
+        cols_low,
+        agg_top,
         operator_low,
         prolong_top,
         d2,
+        r2,
         matrix,
-        scratch=index_scratch(columns_low, columns_top, aggregate_top) + sums,
+        scalars=(0, 1),
+        scratch=sums,
     )
     low_arrived = flip(send_low, 2)
-    smoothed, other_part = call("step_third", step_third, [vec_top, vec_mid], d2, r2, product, other, matrix, transfer)
+    (other_part,) = call("step_third", step_third, [vec_mid], part, other, restrict)
     arrived = flip(other_part, 0)
     own_part, smoothed_blocks, mid_own, transfer_own = call(
         "restrict_own",
         restrict_own,
-        [vec_mid, ((rows, S, N), F32), ((n_mid, 4 * n_mid), BF16), ((n_mid, 4 * n_low), BF16)],
-        smoothed,
+        [vec_mid, ((rows, S, N), F32), ((4 * n_mid, n_mid), BF16), ((n_mid, 4 * n_low), BF16)],
+        known,
+        other,
+        turned,
         transfer,
         send_mid,
     )
@@ -464,7 +490,7 @@
     mid_other, transfer_other, product = call(
         "join_other",
         join_other,
-        [((n_mid, 4 * n_mid), BF16), ((n_mid, 4 * n_low), BF16), vec_top],
+        [((4 * n_mid, n_mid), BF16), ((n_mid, 4 * n_low), BF16), vec_top],
         mid_arrived,
         mid_side,
         product,
@@ -485,7 +511,7 @@
     partial, fixing = call(
         "compose_fixed",
         compose_fixed,
-        [vec_mid, ((n_mid, 4 * n_low), BF16)],
+        [vec_mid, ((4 * n_low, n_mid), BF16)],
         solve_own,
         solve_other,
         transfer_own,
@@ -494,8 +520,10 @@
     )
     (mid_fixed,) = call("end_fixed", end_fixed, [vec_mid], partial, other, fixing)
     other = flip(mid_fixed, 0)
-    (partial,) = call("start_correction", start_correction, [vec_top], total, mid_fixed, transfer)
-    (correction,) = call("end_correction", end_correction, [((rows, S, N), F32)], partial, other, transfer)
+    partial, turned = call(
+        "start_correction", start_correction, [vec_top, ((2 * n_mid, n_top), BF16)], total, mid_fixed, transfer
+    )
+    (correction,) = call("end_correction", end_correction, [((rows, S, N), F32)], partial, other, turned)
     return correction, smoothed_blocks
 
 

time: 42.5 us -> 41.4 us (0.974)
  Pallas kernels: 11.3 us -> 10.3 us
    pallas_call x16 -> x17, Pallas kernels: 11.3 us -> 10.3 us  [call(): pl.pallas_call(body, name=name, out_shape=[place(shape, dtype) for place,...]
    unnamed x20 -> x10, local copies, waits for them, and re-layouts: 1.3 us -> 1.29 us
  transfers between devices with their start and end apart: 10 -> 10, of which waited for: 6 -> 5; matrix products, arithmetic and copies ran while one was open for 1% -> 2% of each run, Pallas kernels for 25% -> 23%
where the time goes in v3:
time: 41.4 us; the launch traced here: 41.3 us
  starting transfers between devices  19.1 us (46%)
  Pallas kernels  10.3 us (25%)
  waiting for transfers between devices  9.79 us (24%)
  local copies, waits for them, and re-layouts  1.29 us (3%)
  between operations  0.75 us (2%)
    ppermute x10, starting transfers between devices, flip(): return lax.ppermute(value, ('gx', 'gy'), flips[level])  19.1 us
    pallas_call x17, Pallas kernels, call(): pl.pallas_call(body, name=name, out_shape=[place(shape, dtype) for place,...  10.3 us
    ppermute x10, waiting for transfers between devices, flip(): return lax.ppermute(value, ('gx', 'gy'), flips[level])  9.79 us
    unnamed x10, local copies, waits for them, and re-layouts  1.29 us
  transfers between devices with their start and end apart: 10, of which 5 were waited for; matrix products, arithmetic and copies ran while one was open for 2% of the time, Pallas kernels for 23%

profile of v3, /device:TPU:128, one launch (start us, length us, event | category | flops | bytes accessed | tf_op | source)
XLA Modules:
  0.0 41.3 jit_solution(1271676897656520479)
XLA Ops:
  0.6 3.1 %collective-permute-start = (f32[8,8,64]{2,1,0:T(8,128)}, f32[8,8,64]{2,1,0:T(8,128)S(1)}, u32[]{:S(2)}, u32[]{:S(2)}) collective-permute-start(f32[8,8,64]{2,1,0:T(8,128)} %side_in.1), channel_id=1, source_target_pairs={{0,16},{1,17},{2,18},{3,19},{4,20},{5,21},{6,22},{7,23},{8,24},{9,... | collective-permute-start | bytes 49160 | tf_op jit(solution)/shard_map/ppermute | solution.py:407
  3.7 4.0 %prepare_top.1 = (bf16[512,2048]{1,0:T(8,128)(2,1)S(1)}, f32[8,512]{1,0:T(8,128)S(1)}, f32[8,512]{1,0:T(8,128)S(1)}, s32[8]{0:T(128)S(4)}, s32[4,27]{1,0:T(4,128...) custom-call(s32[8,27]{1,0:T(8,128)} %cols_in.1, f32[8,8,64]{2,1,0:T(8,128)} %side_in.1, f32[8,27,64,64]{3,2,1,0:T(8,128)} %remote.1, ...), custom_call_target="tpu_custom_call" | custom-call | flops 4000000000 | tf_op jit(solution)/shard_map/prepare_top/pallas_call | solution.py:40
  7.8 0.4 step_first.1
  8.2 1.7 %collective-permute-start.1 = (f32[8,512]{1,0:T(8,128)S(1)}, f32[8,512]{1,0:T(8,128)S(1)}, u32[]{:S(2)}, u32[]{:S(2)}) collective-permute-start(f32[8,512]{1,0:T(8,128)S(1)} %get-tuple-element.38.after.vector.old), channel_id=1, source_target_pairs={{0,16},{1,17},{2,18},{3,19},{4,20},{5,21},{6,22},{7,23},{8,24},{9,... | collective-permute-start | bytes 49160 | tf_op jit(solution)/shard_map/ppermute | solution.py:407
  9.9 0.8 %prepare_mid.1.after.source = f32[1160,128]{1,0:T(8,128)S(1)} custom-call(s32[4,27]{1,0:T(4,128)S(4)} %get-tuple-element.40.cols, s32[4]{0:T(128)S(4)} %get-tuple-element.41.agg, f32[4,27,64,64]{3,2,1,0:T(8,128)S(1)} %copy-done, f32[4,64,64]{2,1,0:T(8,128)S(1)} %copy-done.3, f32[8,512]{1,0:T(8,128)S(1)} %get-tuple-element.38.after.vector.old), custom_call_target="tpu_custom_call" | custom-call | flops 200000000 | tf_op jit(solution)/shard_map/prepare_mid/pallas_call | solution.py:40
  10.7 3.3 %collective-permute-start.6 = (f32[1160,128]{1,0:T(8,128)S(1)}, f32[1160,128]{1,0:T(8,128)S(1)}, u32[]{:S(2)}, u32[]{:S(2)}) collective-permute-start(f32[1160,128]{1,0:T(8,128)S(1)} %prepare_mid.1.after.source), channel_id=1, source_target_pairs={{0,128},{1,129},{2,130},{3,131},{4,132},{5,133},{6,134},{7,135},{8... | collective-permute-start | bytes 1781768 | tf_op jit(solution)/shard_map/ppermute | solution.py:407
  13.9 0.4 own_top.1.product
  14.3 0.4 step_second.1
  14.7 2.1 %collective-permute-start.2 = (f32[8,512]{1,0:T(8,128)S(1)}, f32[8,512]{1,0:T(8,128)S(1)}, u32[]{:S(2)}, u32[]{:S(2)}) collective-permute-start(f32[8,512]{1,0:T(8,128)S(1)} %get-tuple-element.45.direction), channel_id=1, source_target_pairs={{0,16},{1,17},{2,18},{3,19},{4,20},{5,21},{6,22},{7,23},{8,24},{9,... | collective-permute-start | bytes 49160 | tf_op jit(solution)/shard_map/ppermute | solution.py:407
  16.8 1.2 %prepare_low.1 = (f32[256,128]{1,0:T(8,128)S(1)}, bf16[512,1024]{1,0:T(8,128)(2,1)S(1)}, bf16[1024,512]{1,0:T(8,128)(2,1)S(1)}, f32[8,512]{1,0:T(8,128)S(1)}, f3...) custom-call(s32[2,27]{1,0:T(2,128)S(4)} %get-tuple-element.43.cols, s32[8]{0:T(128)S(4)} %get-tuple-element.44.agg, ...), custom_call_target="tpu_custom_call" | custom-call | flops 200000000 | tf_op jit(solution)/shard_map/prepare_low/pallas_call | solution.py:40
  18.0 0.7 %collective-permute-start.4 = (f32[256,128]{1,0:T(8,128)S(1)}, f32[256,128]{1,0:T(8,128)S(1)}, u32[]{:S(2)}, u32[]{:S(2)}) collective-permute-start(f32[256,128]{1,0:T(8,128)S(1)} %get-tuple-element.53.own), channel_id=1, source_target_pairs={{0,8},{1,9},{2,10},{3,11},{4,12},{5,13},{6,14},{7,15},{8,0},{9,1},... | collective-permute-start | bytes 393224 | tf_op jit(solution)/shard_map/ppermute | solution.py:407
  18.7 1.4 %collective-permute-done.2.other = f32[8,512]{1,0:T(8,128)S(1)} collective-permute-done((f32[8,512]{1,0:T(8,128)S(1)}, f32[8,512]{1,0:T(8,128)S(1)}, u32[]{:S(2)}, u32[]{:S(2)}) %collective-permute-start.2) | collective-permute-done | bytes 16416 | tf_op jit(solution)/shard_map/ppermute | solution.py:407
  20.1 0.2 step_third.1
  20.3 2.1 %collective-permute-start.3 = (f32[8,256]{1,0:T(8,128)S(1)}, f32[8,256]{1,0:T(8,128)S(1)}, u32[]{:S(2)}, u32[]{:S(2)}) collective-permute-start(f32[8,256]{1,0:T(8,128)S(1)} %step_third.1), channel_id=1, source_target_pairs={{0,16},{1,17},{2,18},{3,19},{4,20},{5,21},{6,22},{7,23},{8,24},{9,... | collective-permute-start | bytes 24584 | tf_op jit(solution)/shard_map/ppermute | solution.py:407
  22.3 0.4 %restrict_own.1 = (f32[8,256]{1,0:T(8,128)S(1)}, f32[8,8,64]{2,1,0:T(8,128)S(1)}, bf16[1024,256]{1,0:T(8,128)(2,1)S(1)}, bf16[256,512]{1,0:T(8,128)(2,1)S(1)}) custom-call(f32[8,512]{1,0:T(8,128)S(1)} %get-tuple-element.47.known, f32[8,512]{1,0:T(8,128)S(1)} %collective-permute-done.2.other, bf16[1024,512]{1,0:T(8,128)(2,1)S(1)} %get-tuple-element.48.turned, ...), custom_call_target="tpu_custom_call" | custom-call | flops 200000000 | tf_op jit(solution)/shard_map/restrict_own/pallas_call | solution.py:40
  22.7 0.6 %copy.16 = f32[8,8,64]{2,1,0:T(8,128)} copy(f32[8,8,64]{2,1,0:T(8,128)S(1)} %get-tuple-element.69) | data formatting | bytes 32768
  23.3 0.2 compose_low.1.after.low
  23.6 1.8 %collective-permute-done.3.b = f32[8,256]{1,0:T(8,128)S(1)} collective-permute-done((f32[8,256]{1,0:T(8,128)S(1)}, f32[8,256]{1,0:T(8,128)S(1)}, u32[]{:S(2)}, u32[]{:S(2)}) %collective-permute-start.3) | collective-permute-done | bytes 8224 | tf_op jit(solution)/shard_map/ppermute | solution.py:407
  25.4 2.6 %collective-permute-start.7 = (f32[8,256]{1,0:T(8,128)S(1)}, f32[8,256]{1,0:T(8,128)S(1)}, u32[]{:S(2)}, u32[]{:S(2)}) collective-permute-start(f32[8,256]{1,0:T(8,128)S(1)} %add_mid.1.side.own), channel_id=1, source_target_pairs={{0,128},{1,129},{2,130},{3,131},{4,132},{5,133},{6,134},{7,135},{8... | collective-permute-start | bytes 24584 | tf_op jit(solution)/shard_map/ppermute | solution.py:407
  28.1 1.0 %collective-permute-start.5 = (f32[256,128]{1,0:T(8,128)S(1)}, f32[256,128]{1,0:T(8,128)S(1)}, u32[]{:S(2)}, u32[]{:S(2)}) collective-permute-start(f32[256,128]{1,0:T(8,128)S(1)} %get-tuple-element.55.own), channel_id=1, source_target_pairs={{0,128},{1,129},{2,130},{3,131},{4,132},{5,133},{6,134},{7,135},{8... | collective-permute-start | bytes 393224 | tf_op jit(solution)/shard_map/ppermute | solution.py:407
  29.1 0.3 join_other.1
  29.4 1.2 %collective-permute-done.7.other = f32[8,256]{1,0:T(8,128)S(1)} collective-permute-done((f32[8,256]{1,0:T(8,128)S(1)}, f32[8,256]{1,0:T(8,128)S(1)}, u32[]{:S(2)}, u32[]{:S(2)}) %collective-permute-start.7) | collective-permute-done | bytes 8224 | tf_op jit(solution)/shard_map/ppermute | solution.py:407
  30.6 0.8 %solve_mid.1 = (f32[8,256]{1,0:T(8,128)S(1)}, f32[8,256]{1,0:T(8,128)S(1)}) custom-call(f32[8,512]{1,0:T(8,128)S(1)} %get-tuple-element.58.product, f32[8,256]{1,0:T(8,128)S(1)} %add_mid.1.side.own, f32[8,256]{1,0:T(8,128)S(1)} %collective-permute-done.7.other, bf16[1024,256]{1,0:T(8,128)(2,1)S(1)} %get-tuple-element.54.matrix.matrix_own, ...), custom_call_target="tpu_custom_call" | custom-call | flops 20000000000 | tf_op jit(solution)/shard_map/solve_mid/pallas_call | solution.py:40
  31.4 0.7 %collective-permute-start.8 = (f32[8,256]{1,0:T(8,128)S(1)}, f32[8,256]{1,0:T(8,128)S(1)}, u32[]{:S(2)}, u32[]{:S(2)}) collective-permute-start(f32[8,256]{1,0:T(8,128)S(1)} %get-tuple-element.61.pair), channel_id=1, source_target_pairs={{0,8},{1,9},{2,10},{3,11},{4,12},{5,13},{6,14},{7,15},{8,0},{9,1},... | collective-permute-start | bytes 24584 | tf_op jit(solution)/shard_map/ppermute | solution.py:407
  32.1 2.5 %collective-permute-done.5.other = f32[256,128]{1,0:T(8,128)S(1)} collective-permute-done((f32[256,128]{1,0:T(8,128)S(1)}, f32[256,128]{1,0:T(8,128)S(1)}, u32[]{:S(2)}, u32[]{:S(2)}) %collective-permute-start.5) | collective-permute-done | bytes 131104 | tf_op jit(solution)/shard_map/ppermute | solution.py:407
  34.6 0.5 %compose_fixed.1 = (f32[8,256]{1,0:T(8,128)S(1)}, bf16[512,256]{1,0:T(8,128)(2,1)S(1)}) custom-call(f32[256,128]{1,0:T(8,128)S(1)} %get-tuple-element.55.own, f32[256,128]{1,0:T(8,128)S(1)} %collective-permute-done.5.other, bf16[256,512]{1,0:T(8,128)(2,1)S(1)} %get-tuple-element.56.transfer_own.transfer, f32[8,256]{1,0:T(8,128)S(1)} %get-tuple-element.61.pair, ...), custom_call_target="tpu_custom_call" | custom-call | flops 200000000 | tf_op jit(solution)/shard_map/compose_fixed/pallas_call | solution.py:40
  35.1 0.1 end_fixed.1.fixed
  35.3 2.0 %collective-permute-start.9 = (f32[8,256]{1,0:T(8,128)S(1)}, f32[8,256]{1,0:T(8,128)S(1)}, u32[]{:S(2)}, u32[]{:S(2)}) collective-permute-start(f32[8,256]{1,0:T(8,128)S(1)} %end_fixed.1.fixed), channel_id=1, source_target_pairs={{0,16},{1,17},{2,18},{3,19},{4,20},{5,21},{6,22},{7,23},{8,24},{9,... | collective-permute-start | bytes 24584 | tf_op jit(solution)/shard_map/ppermute | solution.py:407
  37.3 0.3 start_correction.1
  37.5 2.9 %collective-permute-done.9.other = f32[8,256]{1,0:T(8,128)S(1)} collective-permute-done((f32[8,256]{1,0:T(8,128)S(1)}, f32[8,256]{1,0:T(8,128)S(1)}, u32[]{:S(2)}, u32[]{:S(2)}) %collective-permute-start.9) | collective-permute-done | bytes 8224 | tf_op jit(solution)/shard_map/ppermute | solution.py:407
  40.4 0.2 end_correction.1
  40.7 0.6 %copy.15 = f32[8,8,64]{2,1,0:T(8,128)} copy(f32[8,8,64]{2,1,0:T(8,128)S(1)} %end_correction.1) | data formatting | bytes 32768
  (15 shorter events, 0.2 us)
Async XLA Ops:
  0.6 7.1 %collective-permute-start = (f32[8,8,64]{2,1,0:T(8,128)}, f32[8,8,64]{2,1,0:T(8,128)S(1)}, u32[]{:S(2)}, u32[]{:S(2)}) collective-permute-start(f32[8,8,64]{2,1,0:T(8,128)} %side_in.1), channel_id=1, source_target_pairs={{0,16},{1,17},{2,18},{3,19},{4,20},{5,21},{6,22},{7,23},{8,24},{9,... | collective-permute-start | bytes 49160 | tf_op jit(solution)/shard_map/ppermute | solution.py:407
  7.8 2.1 %copy-start = (f32[4,27,64,64]{3,2,1,0:T(8,128)S(1)}, f32[4,27,64,64]{3,2,1,0:T(8,128)}, u32[]{:S(2)}) copy-start(f32[4,27,64,64]{3,2,1,0:T(8,128)} %blocks.2) | copy-start | bytes 5308420
  7.8 2.1 %copy-start.3 = (f32[4,64,64]{2,1,0:T(8,128)S(1)}, f32[4,64,64]{2,1,0:T(8,128)}, u32[]{:S(2)}) copy-start(f32[4,64,64]{2,1,0:T(8,128)} %prolong.2) | copy-start | bytes 196612
  8.2 6.1 %collective-permute-start.1 = (f32[8,512]{1,0:T(8,128)S(1)}, f32[8,512]{1,0:T(8,128)S(1)}, u32[]{:S(2)}, u32[]{:S(2)}) collective-permute-start(f32[8,512]{1,0:T(8,128)S(1)} %get-tuple-element.38.after.vector.old), channel_id=1, source_target_pairs={{0,16},{1,17},{2,18},{3,19},{4,20},{5,21},{6,22},{7,23},{8,24},{9,... | collective-permute-start | bytes 49160 | tf_op jit(solution)/shard_map/ppermute | solution.py:407
  10.7 18.5 %collective-permute-start.6 = (f32[1160,128]{1,0:T(8,128)S(1)}, f32[1160,128]{1,0:T(8,128)S(1)}, u32[]{:S(2)}, u32[]{:S(2)}) collective-permute-start(f32[1160,128]{1,0:T(8,128)S(1)} %prepare_mid.1.after.source), channel_id=1, source_target_pairs={{0,128},{1,129},{2,130},{3,131},{4,132},{5,133},{6,134},{7,135},{8... | collective-permute-start | bytes 1781768 | tf_op jit(solution)/shard_map/ppermute | solution.py:407
  14.3 2.5 %copy-start.1 = (f32[2,27,64,64]{3,2,1,0:T(8,128)S(1)}, f32[2,27,64,64]{3,2,1,0:T(8,128)}, u32[]{:S(2)}) copy-start(f32[2,27,64,64]{3,2,1,0:T(8,128)} %blocks.3) | copy-start | bytes 2654212
  14.3 2.5 %copy-start.2 = (f32[8,64,64]{2,1,0:T(8,128)S(1)}, f32[8,64,64]{2,1,0:T(8,128)}, u32[]{:S(2)}) copy-start(f32[8,64,64]{2,1,0:T(8,128)} %prolong.3) | copy-start | bytes 393220
  14.7 5.3 %collective-permute-start.2 = (f32[8,512]{1,0:T(8,128)S(1)}, f32[8,512]{1,0:T(8,128)S(1)}, u32[]{:S(2)}, u32[]{:S(2)}) collective-permute-start(f32[8,512]{1,0:T(8,128)S(1)} %get-tuple-element.45.direction), channel_id=1, source_target_pairs={{0,16},{1,17},{2,18},{3,19},{4,20},{5,21},{6,22},{7,23},{8,24},{9,... | collective-permute-start | bytes 49160 | tf_op jit(solution)/shard_map/ppermute | solution.py:407
  18.0 5.3 %collective-permute-start.4 = (f32[256,128]{1,0:T(8,128)S(1)}, f32[256,128]{1,0:T(8,128)S(1)}, u32[]{:S(2)}, u32[]{:S(2)}) collective-permute-start(f32[256,128]{1,0:T(8,128)S(1)} %get-tuple-element.53.own), channel_id=1, source_target_pairs={{0,8},{1,9},{2,10},{3,11},{4,12},{5,13},{6,14},{7,15},{8,0},{9,1},... | collective-permute-start | bytes 393224 | tf_op jit(solution)/shard_map/ppermute | solution.py:407
  20.3 5.2 %collective-permute-start.3 = (f32[8,256]{1,0:T(8,128)S(1)}, f32[8,256]{1,0:T(8,128)S(1)}, u32[]{:S(2)}, u32[]{:S(2)}) collective-permute-start(f32[8,256]{1,0:T(8,128)S(1)} %step_third.1), channel_id=1, source_target_pairs={{0,16},{1,17},{2,18},{3,19},{4,20},{5,21},{6,22},{7,23},{8,24},{9,... | collective-permute-start | bytes 24584 | tf_op jit(solution)/shard_map/ppermute | solution.py:407
  25.4 5.2 %collective-permute-start.7 = (f32[8,256]{1,0:T(8,128)S(1)}, f32[8,256]{1,0:T(8,128)S(1)}, u32[]{:S(2)}, u32[]{:S(2)}) collective-permute-start(f32[8,256]{1,0:T(8,128)S(1)} %add_mid.1.side.own), channel_id=1, source_target_pairs={{0,128},{1,129},{2,130},{3,131},{4,132},{5,133},{6,134},{7,135},{8... | collective-permute-start | bytes 24584 | tf_op jit(solution)/shard_map/ppermute | solution.py:407
  28.1 6.5 %collective-permute-start.5 = (f32[256,128]{1,0:T(8,128)S(1)}, f32[256,128]{1,0:T(8,128)S(1)}, u32[]{:S(2)}, u32[]{:S(2)}) collective-permute-start(f32[256,128]{1,0:T(8,128)S(1)} %get-tuple-element.55.own), channel_id=1, source_target_pairs={{0,128},{1,129},{2,130},{3,131},{4,132},{5,133},{6,134},{7,135},{8... | collective-permute-start | bytes 393224 | tf_op jit(solution)/shard_map/ppermute | solution.py:407
  31.4 3.7 %collective-permute-start.8 = (f32[8,256]{1,0:T(8,128)S(1)}, f32[8,256]{1,0:T(8,128)S(1)}, u32[]{:S(2)}, u32[]{:S(2)}) collective-permute-start(f32[8,256]{1,0:T(8,128)S(1)} %get-tuple-element.61.pair), channel_id=1, source_target_pairs={{0,8},{1,9},{2,10},{3,11},{4,12},{5,13},{6,14},{7,15},{8,0},{9,1},... | collective-permute-start | bytes 24584 | tf_op jit(solution)/shard_map/ppermute | solution.py:407
  35.3 5.2 %collective-permute-start.9 = (f32[8,256]{1,0:T(8,128)S(1)}, f32[8,256]{1,0:T(8,128)S(1)}, u32[]{:S(2)}, u32[]{:S(2)}) collective-permute-start(f32[8,256]{1,0:T(8,128)S(1)} %end_fixed.1.fixed), channel_id=1, source_target_pairs={{0,16},{1,17},{2,18},{3,19},{4,20},{5,21},{6,22},{7,23},{8,24},{9,... | collective-permute-start | bytes 24584 | tf_op jit(solution)/shard_map/ppermute | solution.py:407

commit v4 on v3

--- a/solution.py
+++ b/solution.py
@@ -137,10 +137,6 @@
         ref[rows_at, pl.ds(base + width, 2 * N)] = low
 
 
-def lanes_of(b):
-    return pl.ds(pl.multiple_of(b * N, N), N)
-
-
 def prepare_top(
     cols_in, side_in, remote, agg_in, cols_mid_in, agg_mid_in, cols_low_in,
     matrix, first, product, agg, cols_mid, agg_mid, cols_low,
@@ -148,6 +144,7 @@
 ):
     rows = remote.shape[0]
     wait = copies((cols_in,), (cols,), small)
+    wait_side = copies((side_in,), (side,), sems.at[pl.ds(rows, 1)])
 
     def fetch(b):
         return pltpu.make_async_copy(remote.at[b], held.at[b], sems.at[b])
@@ -155,52 +152,50 @@
     for b in range(rows):
         fetch(b).start()
     wait_more = copies(
-        (side_in, agg_in, cols_mid_in, agg_mid_in, cols_low_in),
-        (side, agg, cols_mid, agg_mid, cols_low),
-        sems.at[pl.ds(rows, 5)],
+        (agg_in, cols_mid_in, agg_mid_in, cols_low_in), (agg, cols_mid, agg_mid, cols_low), sems.at[pl.ds(rows + 1, 4)]
     )
     wait()
     device = cols[0, 0] // rows
-
-    def some(step, carry):
-        b = step * len(sums)
-        for n in range(len(sums)):
-            fetch(b + n).wait()
-        collapse_rows(cols, b, rows, device, held, sums)
-        for n, part in enumerate(sums):
-            put_halves(matrix, lanes_of(b + n), [pair_of(part, 2 * c) for c in range(rows)])
-        return carry
-
-    lax.fori_loop(0, rows // len(sums), some, 0)
+    half = 2 * rows * N
+    done = 0
+    for b in range(0, rows, 2):
+        fetch(b).wait()
+        fetch(b + 1).wait()
+        parts = sums[b % 4 : b % 4 + 2]
+        collapse_rows(cols, b, rows, device, held, parts)
+        for n, part in enumerate(parts):
+            put_halves(matrix, slice((b + n) * N, (b + n + 1) * N), [pair_of(part, 2 * c) for c in range(rows)])
+        if b + 2 == rows // 2:
+            wait_side()
+            first[...] = pack(side)
+        if b + 2 > rows // 2:
+            product[:, done : b * N] = apply_t(first[...], matrix[done : b * N, :half])
+            done = b * N
+    product[:, done:] = apply_t(first[...], matrix[done:, :half])
     wait_more()
-    own = pack(side)
-    first[...] = own
-    product[...] = apply_t(own, matrix[:, : 2 * rows * N])
 
 
 def collapse_out(cols, blocks, put, sums):
     rows = blocks.shape[0]
     device = cols[0, 0] // rows
     sums = [part.at[: 2 * rows] for part in sums]
-
-    def some(step, carry):
-        b = step * len(sums)
-        collapse_rows(cols, b, rows, device, blocks, sums)
-        for n, part in enumerate(sums):
+    for b in range(0, rows, 2):
+        parts = sums[b % 4 : b % 4 + 2]
+        collapse_rows(cols, b, rows, device, blocks, parts)
+        for n, part in enumerate(parts):
             for c in range(rows):
                 put(b + n, c, pair_of(part, 2 * c))
-        return carry
-
-    lax.fori_loop(0, rows // len(sums), some, 0)
-
-
-def prepare_mid(cols, agg, blocks, prolong, after, send, *sums):
+
+
+def prepare_mid(cols, agg, blocks, prolong, direction, matrix, product, send, turned, *sums):
+    turned[...] = matrix[:, matrix.shape[1] // 2 :].T
+    product[...] = apply_t(direction[...], matrix[:, : matrix.shape[1] // 2])
     rows = blocks.shape[0]
     half = rows // 2
     n_mid = rows * N
 
     def put(b, c, value):
-        send[pl.ds(pl.multiple_of(c * n_mid + b * N, N), N)] = value
+        send[c * n_mid + b * N : c * n_mid + (b + 1) * N] = value
 
     collapse_out(cols, blocks, put, sums)
     at = rows * n_mid
@@ -216,14 +211,13 @@
 
 
 def prepare_low(
-    cols, agg, blocks, prolong, direction, residual, matrix, send, transfer, turned, known, part, restrict, *sums
+    cols, agg, blocks, prolong, direction, residual, matrix, turned, send, transfer, known, part, restrict, *sums
 ):
-    turned[...] = matrix[:, matrix.shape[1] // 2 :].T
     known[...] = residual[...] - (direction[...] + apply_t(direction[...], matrix[:, : matrix.shape[1] // 2]))
     n_low = blocks.shape[0] * N
 
     def put(b, c, value):
-        send[pl.ds(pl.multiple_of(c * n_low + b * N, N), N)] = value
+        send[c * n_low + b * N : c * n_low + (b + 1) * N] = value
 
     collapse_out(cols, blocks, put, sums)
     rows = prolong.shape[0]
@@ -243,10 +237,6 @@
     restrict[depth:] = low
 
 
-def own_product(vector, matrix, after, product):
-    product[...] = apply_t(vector[...], matrix[:, : matrix.shape[1] // 2])
-
-
 def other_product(product, other, matrix):
     return product[...] + apply_t(other, matrix[:, matrix.shape[1] // 2 :])
 
@@ -258,9 +248,9 @@
     direction[...] = W[0][0] * d + W[0][1] * r
 
 
-def step_second(first, old, residual, product, other, matrix, direction, new_residual, total):
+def step_second(first, old, residual, product, other, turned, direction, new_residual, total):
     d = old[...]
-    r = residual[...] - (d + other_product(product, other[...], matrix))
+    r = residual[...] - (d + product[...] + apply_turned(other[...], turned[...]))
     new_residual[...] = r
     new = W[1][0] * d + W[1][1] * r
     direction[...] = new
@@ -412,7 +402,7 @@
     n_low = n_mid // 2
     vec_top = ((S, n_top), F32)
     vec_mid = ((S, n_mid), F32)
-    sums = [pltpu.VMEM((2 * rows, N, N), F32)] * 2
+    sums = [pltpu.VMEM((2 * rows, N, N), F32)] * 4
     mid_pieces = ((rows // 2 * n_mid + rows // 4 * N + 8, 2 * N), F32)
     low_pieces = ((rows // 4 * n_low, 2 * N), F32)
 
@@ -439,26 +429,26 @@
     )
     d1, r1 = call("step_first", step_first, [vec_top, vec_top], first, product, other, matrix)
     other = flip(d1, 0)
-    (send_mid,) = call(
+    product, send_mid, turned = call(
         "prepare_mid",
         prepare_mid,
-        [mid_pieces],
+        [vec_top, mid_pieces, ((2 * n_top, n_top), BF16)],
         cols_mid,
         agg_mid,
         operator_mid,
         prolong_mid,
         d1,
+        matrix,
         scalars=(0, 1),
         scratch=sums,
     )
     mid_arrived = flip(send_mid, 1)
-    (product,) = call("own_top", own_product, [vec_top], d1, matrix, send_mid)
-    d2, r2, total = call("step_second", step_second, [vec_top] * 3, first, d1, r1, product, other, matrix)
+    d2, r2, total = call("step_second", step_second, [vec_top] * 3, first, d1, r1, product, other, turned)
     other = flip(d2, 0)
-    send_low, transfer, turned, known, part, restrict = call(
+    send_low, transfer, known, part, restrict = call(
         "prepare_low",
         prepare_low,
-        [low_pieces, ((n_top, 4 * n_mid), BF16), ((2 * n_top, n_top), BF16), vec_top, vec_mid, ((2 * n_top, n_mid), BF16)],
+        [low_pieces, ((n_top, 4 * n_mid), BF16), vec_top, vec_mid, ((2 * n_top, n_mid), BF16)],
         cols_low,
         agg_top,
         operator_low,
@@ -466,6 +456,7 @@
         d2,
         r2,
         matrix,
+        turned,
         scalars=(0, 1),
         scratch=sums,
     )

time: 41.4 us -> 40.9 us (0.988)
  Pallas kernels: 10.3 us -> 9.54 us
  waiting for transfers between devices: 9.79 us -> 10.5 us
    pallas_call x17 -> x16, Pallas kernels: 10.3 us -> 9.54 us  [call(): pl.pallas_call(body, name=name, out_shape=[place(shape, dtype) for place,...]
    ppermute x10, waiting for transfers between devices: 9.79 us -> 10.5 us  [flip(): return lax.ppermute(value, ('gx', 'gy'), flips[level])]
  transfers between devices with their start and end apart: 10 -> 10, of which waited for: 5 -> 5; matrix products, arithmetic and copies ran while one was open for 2% -> 2% of each run, Pallas kernels for 23% -> 22%
where the time goes in v4:
time: 40.9 us; the launch traced here: 40.8 us
  starting transfers between devices  18.8 us (46%)
  waiting for transfers between devices  10.5 us (26%)
  Pallas kernels  9.54 us (23%)
  local copies, waits for them, and re-layouts  1.27 us (3%)
  between operations  0.74 us (2%)
    ppermute x10, starting transfers between devices, flip(): return lax.ppermute(value, ('gx', 'gy'), flips[level])  18.8 us
    ppermute x10, waiting for transfers between devices, flip(): return lax.ppermute(value, ('gx', 'gy'), flips[level])  10.5 us
    pallas_call x16, Pallas kernels, call(): pl.pallas_call(body, name=name, out_shape=[place(shape, dtype) for place,...  9.54 us
    unnamed x10, local copies, waits for them, and re-layouts  1.27 us
  transfers between devices with their start and end apart: 10, of which 5 were waited for; matrix products, arithmetic and copies ran while one was open for 2% of the time, Pallas kernels for 22%

profile of v4, /device:TPU:128, one launch (start us, length us, event | category | flops | bytes accessed | tf_op | source)
XLA Modules:
  0.0 40.8 jit_solution(5861096631025248261)
XLA Ops:
  0.6 3.1 %collective-permute-start = (f32[8,8,64]{2,1,0:T(8,128)}, f32[8,8,64]{2,1,0:T(8,128)S(1)}, u32[]{:S(2)}, u32[]{:S(2)}) collective-permute-start(f32[8,8,64]{2,1,0:T(8,128)} %side_in.1), channel_id=1, source_target_pairs={{0,16},{1,17},{2,18},{3,19},{4,20},{5,21},{6,22},{7,23},{8,24},{9,... | collective-permute-start | bytes 49160 | tf_op jit(solution)/shard_map/ppermute | solution.py:397
  3.7 3.8 %prepare_top.1 = (bf16[512,2048]{1,0:T(8,128)(2,1)S(1)}, f32[8,512]{1,0:T(8,128)S(1)}, f32[8,512]{1,0:T(8,128)S(1)}, s32[8]{0:T(128)S(4)}, s32[4,27]{1,0:T(4,128...) custom-call(s32[8,27]{1,0:T(8,128)} %cols_in.1, f32[8,8,64]{2,1,0:T(8,128)} %side_in.1, f32[8,27,64,64]{3,2,1,0:T(8,128)} %remote.1, ...), custom_call_target="tpu_custom_call" | custom-call | flops 4000000000 | tf_op jit(solution)/shard_map/prepare_top/pallas_call | solution.py:40
  7.6 0.4 step_first.1
  8.0 1.9 %collective-permute-start.1 = (f32[8,512]{1,0:T(8,128)S(1)}, f32[8,512]{1,0:T(8,128)S(1)}, u32[]{:S(2)}, u32[]{:S(2)}) collective-permute-start(f32[8,512]{1,0:T(8,128)S(1)} %get-tuple-element.40.direction.old), channel_id=1, source_target_pairs={{0,16},{1,17},{2,18},{3,19},{4,20},{5,21},{6,22},{7,23},{8,24},{9,... | collective-permute-start | bytes 49160 | tf_op jit(solution)/shard_map/ppermute | solution.py:397
  9.9 0.8 %prepare_mid.1 = (f32[8,512]{1,0:T(8,128)S(1)}, f32[1160,128]{1,0:T(8,128)S(1)}, bf16[1024,512]{1,0:T(8,128)(2,1)S(1)}) custom-call(s32[4,27]{1,0:T(4,128)S(4)} %get-tuple-element.42.cols, s32[4]{0:T(128)S(4)} %get-tuple-element.43.agg, f32[4,27,64,64]{3,2,1,0:T(8,128)S(1)} %copy-done, f32[4,64,64]{2,1,0:T(8,128)S(1)} %copy-done.3, ...), custom_call_target="tpu_custom_call" | custom-call | flops 200000000 | tf_op jit(solution)/shard_map/prepare_mid/pallas_call | solution.py:40
  10.6 3.3 %collective-permute-start.6 = (f32[1160,128]{1,0:T(8,128)S(1)}, f32[1160,128]{1,0:T(8,128)S(1)}, u32[]{:S(2)}, u32[]{:S(2)}) collective-permute-start(f32[1160,128]{1,0:T(8,128)S(1)} %get-tuple-element.53.source), channel_id=1, source_target_pairs={{0,128},{1,129},{2,130},{3,131},{4,132},{5,133},{6,134},{7,135},{8... | collective-permute-start | bytes 1781768 | tf_op jit(solution)/shard_map/ppermute | solution.py:397
  13.9 0.2 step_second.1
  14.2 1.8 %collective-permute-start.2 = (f32[8,512]{1,0:T(8,128)S(1)}, f32[8,512]{1,0:T(8,128)S(1)}, u32[]{:S(2)}, u32[]{:S(2)}) collective-permute-start(f32[8,512]{1,0:T(8,128)S(1)} %get-tuple-element.49.direction), channel_id=1, source_target_pairs={{0,16},{1,17},{2,18},{3,19},{4,20},{5,21},{6,22},{7,23},{8,24},{9,... | collective-permute-start | bytes 49160 | tf_op jit(solution)/shard_map/ppermute | solution.py:397
  16.0 1.2 %prepare_low.1 = (f32[256,128]{1,0:T(8,128)S(1)}, bf16[512,1024]{1,0:T(8,128)(2,1)S(1)}, f32[8,512]{1,0:T(8,128)S(1)}, f32[8,256]{1,0:T(8,128)S(1)}, bf16[1024,256]{1,0:T(8,128)(2,1)S(1)}) custom-call(s32[2,27]{1,0:T(2,128)S(4)} %get-tuple-element.47.cols, s32[8]{0:T(128)S(4)} %get-tuple-element.48.agg, f32[2,27,64,64]{3,2,1,0:T(8,128)S(1)} %copy-done.1, ...), custom_call_target="tpu_custom_call" | custom-call | flops 200000000 | tf_op jit(solution)/shard_map/prepare_low/pallas_call | solution.py:40
  17.2 0.7 %collective-permute-start.4 = (f32[256,128]{1,0:T(8,128)S(1)}, f32[256,128]{1,0:T(8,128)S(1)}, u32[]{:S(2)}, u32[]{:S(2)}) collective-permute-start(f32[256,128]{1,0:T(8,128)S(1)} %get-tuple-element.57.own), channel_id=1, source_target_pairs={{0,8},{1,9},{2,10},{3,11},{4,12},{5,13},{6,14},{7,15},{8,0},{9,1},... | collective-permute-start | bytes 393224 | tf_op jit(solution)/shard_map/ppermute | solution.py:397
  17.9 1.6 %collective-permute-done.2.other = f32[8,512]{1,0:T(8,128)S(1)} collective-permute-done((f32[8,512]{1,0:T(8,128)S(1)}, f32[8,512]{1,0:T(8,128)S(1)}, u32[]{:S(2)}, u32[]{:S(2)}) %collective-permute-start.2) | collective-permute-done | bytes 16416 | tf_op jit(solution)/shard_map/ppermute | solution.py:397
  19.5 0.2 step_third.1
  19.7 1.9 %collective-permute-start.3 = (f32[8,256]{1,0:T(8,128)S(1)}, f32[8,256]{1,0:T(8,128)S(1)}, u32[]{:S(2)}, u32[]{:S(2)}) collective-permute-start(f32[8,256]{1,0:T(8,128)S(1)} %step_third.1), channel_id=1, source_target_pairs={{0,16},{1,17},{2,18},{3,19},{4,20},{5,21},{6,22},{7,23},{8,24},{9,... | collective-permute-start | bytes 24584 | tf_op jit(solution)/shard_map/ppermute | solution.py:397
  21.5 0.4 %restrict_own.1 = (f32[8,256]{1,0:T(8,128)S(1)}, f32[8,8,64]{2,1,0:T(8,128)S(1)}, bf16[1024,256]{1,0:T(8,128)(2,1)S(1)}, bf16[256,512]{1,0:T(8,128)(2,1)S(1)}) custom-call(f32[8,512]{1,0:T(8,128)S(1)} %get-tuple-element.51.known, f32[8,512]{1,0:T(8,128)S(1)} %collective-permute-done.2.other, bf16[1024,512]{1,0:T(8,128)(2,1)S(1)} %get-tuple-element.45.turned, ...), custom_call_target="tpu_custom_call" | custom-call | flops 200000000 | tf_op jit(solution)/shard_map/restrict_own/pallas_call | solution.py:40
  21.9 0.6 %copy.16 = f32[8,8,64]{2,1,0:T(8,128)} copy(f32[8,8,64]{2,1,0:T(8,128)S(1)} %get-tuple-element.73) | data formatting | bytes 32768
  22.6 0.2 compose_low.1.after.low
  22.8 2.0 %collective-permute-done.3.b = f32[8,256]{1,0:T(8,128)S(1)} collective-permute-done((f32[8,256]{1,0:T(8,128)S(1)}, f32[8,256]{1,0:T(8,128)S(1)}, u32[]{:S(2)}, u32[]{:S(2)}) %collective-permute-start.3) | collective-permute-done | bytes 8224 | tf_op jit(solution)/shard_map/ppermute | solution.py:397
  24.8 2.7 %collective-permute-start.7 = (f32[8,256]{1,0:T(8,128)S(1)}, f32[8,256]{1,0:T(8,128)S(1)}, u32[]{:S(2)}, u32[]{:S(2)}) collective-permute-start(f32[8,256]{1,0:T(8,128)S(1)} %add_mid.1.side.own), channel_id=1, source_target_pairs={{0,128},{1,129},{2,130},{3,131},{4,132},{5,133},{6,134},{7,135},{8... | collective-permute-start | bytes 24584 | tf_op jit(solution)/shard_map/ppermute | solution.py:397
  27.5 0.1 own_mid.1
  27.7 0.9 %collective-permute-start.5 = (f32[256,128]{1,0:T(8,128)S(1)}, f32[256,128]{1,0:T(8,128)S(1)}, u32[]{:S(2)}, u32[]{:S(2)}) collective-permute-start(f32[256,128]{1,0:T(8,128)S(1)} %get-tuple-element.59.own), channel_id=1, source_target_pairs={{0,128},{1,129},{2,130},{3,131},{4,132},{5,133},{6,134},{7,135},{8... | collective-permute-start | bytes 393224 | tf_op jit(solution)/shard_map/ppermute | solution.py:397
  28.5 0.3 join_other.1
  28.8 1.2 %collective-permute-done.7.other = f32[8,256]{1,0:T(8,128)S(1)} collective-permute-done((f32[8,256]{1,0:T(8,128)S(1)}, f32[8,256]{1,0:T(8,128)S(1)}, u32[]{:S(2)}, u32[]{:S(2)}) %collective-permute-start.7) | collective-permute-done | bytes 8224 | tf_op jit(solution)/shard_map/ppermute | solution.py:397
  30.0 0.8 %solve_mid.1 = (f32[8,256]{1,0:T(8,128)S(1)}, f32[8,256]{1,0:T(8,128)S(1)}) custom-call(f32[8,512]{1,0:T(8,128)S(1)} %get-tuple-element.62.product, f32[8,256]{1,0:T(8,128)S(1)} %add_mid.1.side.own, f32[8,256]{1,0:T(8,128)S(1)} %collective-permute-done.7.other, bf16[1024,256]{1,0:T(8,128)(2,1)S(1)} %get-tuple-element.58.matrix.matrix_own, ...), custom_call_target="tpu_custom_call" | custom-call | flops 20000000000 | tf_op jit(solution)/shard_map/solve_mid/pallas_call | solution.py:40
  30.8 0.8 %collective-permute-start.8 = (f32[8,256]{1,0:T(8,128)S(1)}, f32[8,256]{1,0:T(8,128)S(1)}, u32[]{:S(2)}, u32[]{:S(2)}) collective-permute-start(f32[8,256]{1,0:T(8,128)S(1)} %get-tuple-element.65.pair), channel_id=1, source_target_pairs={{0,8},{1,9},{2,10},{3,11},{4,12},{5,13},{6,14},{7,15},{8,0},{9,1},... | collective-permute-start | bytes 24584 | tf_op jit(solution)/shard_map/ppermute | solution.py:397
  31.6 2.5 %collective-permute-done.5.other = f32[256,128]{1,0:T(8,128)S(1)} collective-permute-done((f32[256,128]{1,0:T(8,128)S(1)}, f32[256,128]{1,0:T(8,128)S(1)}, u32[]{:S(2)}, u32[]{:S(2)}) %collective-permute-start.5) | collective-permute-done | bytes 131104 | tf_op jit(solution)/shard_map/ppermute | solution.py:397
  34.1 0.5 %compose_fixed.1 = (f32[8,256]{1,0:T(8,128)S(1)}, bf16[512,256]{1,0:T(8,128)(2,1)S(1)}) custom-call(f32[256,128]{1,0:T(8,128)S(1)} %get-tuple-element.59.own, f32[256,128]{1,0:T(8,128)S(1)} %collective-permute-done.5.other, bf16[256,512]{1,0:T(8,128)(2,1)S(1)} %get-tuple-element.60.transfer_own.transfer, f32[8,256]{1,0:T(8,128)S(1)} %get-tuple-element.65.pair, ...), custom_call_target="tpu_custom_call" | custom-call | flops 200000000 | tf_op jit(solution)/shard_map/compose_fixed/pallas_call | solution.py:40
  34.6 0.1 end_fixed.1.fixed
  34.8 1.8 %collective-permute-start.9 = (f32[8,256]{1,0:T(8,128)S(1)}, f32[8,256]{1,0:T(8,128)S(1)}, u32[]{:S(2)}, u32[]{:S(2)}) collective-permute-start(f32[8,256]{1,0:T(8,128)S(1)} %end_fixed.1.fixed), channel_id=1, source_target_pairs={{0,16},{1,17},{2,18},{3,19},{4,20},{5,21},{6,22},{7,23},{8,24},{9,... | collective-permute-start | bytes 24584 | tf_op jit(solution)/shard_map/ppermute | solution.py:397
  36.6 0.2 start_correction.1
  36.8 3.1 %collective-permute-done.9.other = f32[8,256]{1,0:T(8,128)S(1)} collective-permute-done((f32[8,256]{1,0:T(8,128)S(1)}, f32[8,256]{1,0:T(8,128)S(1)}, u32[]{:S(2)}, u32[]{:S(2)}) %collective-permute-start.9) | collective-permute-done | bytes 8224 | tf_op jit(solution)/shard_map/ppermute | solution.py:397
  40.0 0.2 end_correction.1
  40.2 0.6 %copy.15 = f32[8,8,64]{2,1,0:T(8,128)} copy(f32[8,8,64]{2,1,0:T(8,128)S(1)} %end_correction.1) | data formatting | bytes 32768
  (14 shorter events, 0.0 us)
Async XLA Ops:
  0.6 6.9 %collective-permute-start = (f32[8,8,64]{2,1,0:T(8,128)}, f32[8,8,64]{2,1,0:T(8,128)S(1)}, u32[]{:S(2)}, u32[]{:S(2)}) collective-permute-start(f32[8,8,64]{2,1,0:T(8,128)} %side_in.1), channel_id=1, source_target_pairs={{0,16},{1,17},{2,18},{3,19},{4,20},{5,21},{6,22},{7,23},{8,24},{9,... | collective-permute-start | bytes 49160 | tf_op jit(solution)/shard_map/ppermute | solution.py:397
  7.6 2.3 %copy-start = (f32[4,27,64,64]{3,2,1,0:T(8,128)S(1)}, f32[4,27,64,64]{3,2,1,0:T(8,128)}, u32[]{:S(2)}) copy-start(f32[4,27,64,64]{3,2,1,0:T(8,128)} %blocks.2) | copy-start | bytes 5308420
  7.6 2.3 %copy-start.3 = (f32[4,64,64]{2,1,0:T(8,128)S(1)}, f32[4,64,64]{2,1,0:T(8,128)}, u32[]{:S(2)}) copy-start(f32[4,64,64]{2,1,0:T(8,128)} %prolong.2) | copy-start | bytes 196612
  8.0 5.9 %collective-permute-start.1 = (f32[8,512]{1,0:T(8,128)S(1)}, f32[8,512]{1,0:T(8,128)S(1)}, u32[]{:S(2)}, u32[]{:S(2)}) collective-permute-start(f32[8,512]{1,0:T(8,128)S(1)} %get-tuple-element.40.direction.old), channel_id=1, source_target_pairs={{0,16},{1,17},{2,18},{3,19},{4,20},{5,21},{6,22},{7,23},{8,24},{9,... | collective-permute-start | bytes 49160 | tf_op jit(solution)/shard_map/ppermute | solution.py:397
  10.6 17.9 %collective-permute-start.6 = (f32[1160,128]{1,0:T(8,128)S(1)}, f32[1160,128]{1,0:T(8,128)S(1)}, u32[]{:S(2)}, u32[]{:S(2)}) collective-permute-start(f32[1160,128]{1,0:T(8,128)S(1)} %get-tuple-element.53.source), channel_id=1, source_target_pairs={{0,128},{1,129},{2,130},{3,131},{4,132},{5,133},{6,134},{7,135},{8... | collective-permute-start | bytes 1781768 | tf_op jit(solution)/shard_map/ppermute | solution.py:397
  13.9 2.1 %copy-start.1 = (f32[2,27,64,64]{3,2,1,0:T(8,128)S(1)}, f32[2,27,64,64]{3,2,1,0:T(8,128)}, u32[]{:S(2)}) copy-start(f32[2,27,64,64]{3,2,1,0:T(8,128)} %blocks.3) | copy-start | bytes 2654212
  13.9 2.1 %copy-start.2 = (f32[8,64,64]{2,1,0:T(8,128)S(1)}, f32[8,64,64]{2,1,0:T(8,128)}, u32[]{:S(2)}) copy-start(f32[8,64,64]{2,1,0:T(8,128)} %prolong.3) | copy-start | bytes 393220
  14.2 5.3 %collective-permute-start.2 = (f32[8,512]{1,0:T(8,128)S(1)}, f32[8,512]{1,0:T(8,128)S(1)}, u32[]{:S(2)}, u32[]{:S(2)}) collective-permute-start(f32[8,512]{1,0:T(8,128)S(1)} %get-tuple-element.49.direction), channel_id=1, source_target_pairs={{0,16},{1,17},{2,18},{3,19},{4,20},{5,21},{6,22},{7,23},{8,24},{9,... | collective-permute-start | bytes 49160 | tf_op jit(solution)/shard_map/ppermute | solution.py:397
  17.2 5.4 %collective-permute-start.4 = (f32[256,128]{1,0:T(8,128)S(1)}, f32[256,128]{1,0:T(8,128)S(1)}, u32[]{:S(2)}, u32[]{:S(2)}) collective-permute-start(f32[256,128]{1,0:T(8,128)S(1)} %get-tuple-element.57.own), channel_id=1, source_target_pairs={{0,8},{1,9},{2,10},{3,11},{4,12},{5,13},{6,14},{7,15},{8,0},{9,1},... | collective-permute-start | bytes 393224 | tf_op jit(solution)/shard_map/ppermute | solution.py:397
  19.7 5.2 %collective-permute-start.3 = (f32[8,256]{1,0:T(8,128)S(1)}, f32[8,256]{1,0:T(8,128)S(1)}, u32[]{:S(2)}, u32[]{:S(2)}) collective-permute-start(f32[8,256]{1,0:T(8,128)S(1)} %step_third.1), channel_id=1, source_target_pairs={{0,16},{1,17},{2,18},{3,19},{4,20},{5,21},{6,22},{7,23},{8,24},{9,... | collective-permute-start | bytes 24584 | tf_op jit(solution)/shard_map/ppermute | solution.py:397
  24.8 5.2 %collective-permute-start.7 = (f32[8,256]{1,0:T(8,128)S(1)}, f32[8,256]{1,0:T(8,128)S(1)}, u32[]{:S(2)}, u32[]{:S(2)}) collective-permute-start(f32[8,256]{1,0:T(8,128)S(1)} %add_mid.1.side.own), channel_id=1, source_target_pairs={{0,128},{1,129},{2,130},{3,131},{4,132},{5,133},{6,134},{7,135},{8... | collective-permute-start | bytes 24584 | tf_op jit(solution)/shard_map/ppermute | solution.py:397
  27.7 6.5 %collective-permute-start.5 = (f32[256,128]{1,0:T(8,128)S(1)}, f32[256,128]{1,0:T(8,128)S(1)}, u32[]{:S(2)}, u32[]{:S(2)}) collective-permute-start(f32[256,128]{1,0:T(8,128)S(1)} %get-tuple-element.59.own), channel_id=1, source_target_pairs={{0,128},{1,129},{2,130},{3,131},{4,132},{5,133},{6,134},{7,135},{8... | collective-permute-start | bytes 393224 | tf_op jit(solution)/shard_map/ppermute | solution.py:397
  30.8 3.8 %collective-permute-start.8 = (f32[8,256]{1,0:T(8,128)S(1)}, f32[8,256]{1,0:T(8,128)S(1)}, u32[]{:S(2)}, u32[]{:S(2)}) collective-permute-start(f32[8,256]{1,0:T(8,128)S(1)} %get-tuple-element.65.pair), channel_id=1, source_target_pairs={{0,8},{1,9},{2,10},{3,11},{4,12},{5,13},{6,14},{7,15},{8,0},{9,1},... | collective-permute-start | bytes 24584 | tf_op jit(solution)/shard_map/ppermute | solution.py:397
  34.8 5.2 %collective-permute-start.9 = (f32[8,256]{1,0:T(8,128)S(1)}, f32[8,256]{1,0:T(8,128)S(1)}, u32[]{:S(2)}, u32[]{:S(2)}) collective-permute-start(f32[8,256]{1,0:T(8,128)S(1)} %end_fixed.1.fixed), channel_id=1, source_target_pairs={{0,16},{1,17},{2,18},{3,19},{4,20},{5,21},{6,22},{7,23},{8,24},{9,... | collective-permute-start | bytes 24584 | tf_op jit(solution)/shard_map/ppermute | solution.py:397

commit v5 on v4

--- a/solution.py
+++ b/solution.py
@@ -28,7 +28,7 @@
 
 
 W = chebyshev_weights()
-COST = {"prepare_top": 4000, "step_first": 4000, "step_second": 100000, "step_third": 6000, "solve_mid": 20000}
+COST = {"load_indices": 20000, "prepare_top": 4000, "step_first": 4000, "step_second": 100000, "step_third": 6000, "solve_mid": 20000}
 
 
 def call(name, body, outs, *args, remote=(), scalars=(), scratch=(), aliases=None, limit=8):
@@ -137,42 +137,28 @@
         ref[rows_at, pl.ds(base + width, 2 * N)] = low
 
 
-def prepare_top(
-    cols_in, side_in, remote, agg_in, cols_mid_in, agg_mid_in, cols_low_in,
-    matrix, first, product, agg, cols_mid, agg_mid, cols_low,
-    small, cols, side, held, sems, *sums
-):
-    rows = remote.shape[0]
-    wait = copies((cols_in,), (cols,), small)
-    wait_side = copies((side_in,), (side,), sems.at[pl.ds(rows, 1)])
-
-    def fetch(b):
-        return pltpu.make_async_copy(remote.at[b], held.at[b], sems.at[b])
-
-    for b in range(rows):
-        fetch(b).start()
-    wait_more = copies(
-        (agg_in, cols_mid_in, agg_mid_in, cols_low_in), (agg, cols_mid, agg_mid, cols_low), sems.at[pl.ds(rows + 1, 4)]
-    )
-    wait()
+def load_indices(*refs):
+    count = (len(refs) - 1) // 2
+    copies(refs[:count], refs[count:-1], refs[-1])()
+
+
+def prepare_top(cols, blocks, side, matrix, turned, first, product, *sums):
+    rows = blocks.shape[0]
     device = cols[0, 0] // rows
     half = 2 * rows * N
+    first[...] = pack(side)
     done = 0
     for b in range(0, rows, 2):
-        fetch(b).wait()
-        fetch(b + 1).wait()
         parts = sums[b % 4 : b % 4 + 2]
-        collapse_rows(cols, b, rows, device, held, parts)
+        collapse_rows(cols, b, rows, device, blocks, parts)
         for n, part in enumerate(parts):
             put_halves(matrix, slice((b + n) * N, (b + n + 1) * N), [pair_of(part, 2 * c) for c in range(rows)])
-        if b + 2 == rows // 2:
-            wait_side()
-            first[...] = pack(side)
         if b + 2 > rows // 2:
             product[:, done : b * N] = apply_t(first[...], matrix[done : b * N, :half])
+            turned[:, done : b * N] = matrix[done : b * N, half:].T
             done = b * N
     product[:, done:] = apply_t(first[...], matrix[done:, :half])
-    wait_more()
+    turned[:, done:] = matrix[done:, half:].T
 
 
 def collapse_out(cols, blocks, put, sums):
@@ -187,8 +173,7 @@
                 put(b + n, c, pair_of(part, 2 * c))
 
 
-def prepare_mid(cols, agg, blocks, prolong, direction, matrix, product, send, turned, *sums):
-    turned[...] = matrix[:, matrix.shape[1] // 2 :].T
+def prepare_mid(cols, agg, blocks, prolong, direction, matrix, product, send, *sums):
     product[...] = apply_t(direction[...], matrix[:, : matrix.shape[1] // 2])
     rows = blocks.shape[0]
     half = rows // 2
@@ -237,13 +222,9 @@
     restrict[depth:] = low
 
 
-def other_product(product, other, matrix):
-    return product[...] + apply_t(other, matrix[:, matrix.shape[1] // 2 :])
-
-
-def step_first(first, product, other, matrix, direction, residual):
+def step_first(first, product, other, turned, direction, residual):
     d = first[...]
-    r = d - (d + other_product(product, pack(other), matrix))
+    r = d - (d + product[...] + apply_turned(pack(other), turned[...]))
     residual[...] = r
     direction[...] = W[0][0] * d + W[0][1] * r
 
@@ -407,32 +388,31 @@
     low_pieces = ((rows // 4 * n_low, 2 * N), F32)
 
     other = flip(right_side, 0)
-    indices = (aggregate_top, columns_mid, aggregate_mid, columns_low)
-    matrix, first, product, agg_top, cols_mid, agg_mid, cols_low = call(
+    indices = (columns_top, aggregate_top, columns_mid, aggregate_mid, columns_low)
+    cols_top, agg_top, cols_mid, agg_mid, cols_low = call(
+        "load_indices",
+        load_indices,
+        [(a.shape, jnp.int32) for a in indices],
+        *indices,
+        remote=range(5),
+        scratch=[pltpu.SemaphoreType.DMA((5,))],
+    )
+    matrix, turned, first, product = call(
         "prepare_top",
         prepare_top,
-        [((n_top, 4 * n_top), BF16), vec_top, vec_top] + [(a.shape, jnp.int32) for a in indices],
-        columns_top,
+        [((n_top, 4 * n_top), BF16), ((2 * n_top, n_top), BF16), vec_top, vec_top],
+        cols_top,
+        operator_top,
         right_side,
-        operator_top,
-        *indices,
-        remote=range(7),
-        scratch=[
-            pltpu.SemaphoreType.DMA((1,)),
-            pltpu.SMEM(columns_top.shape, jnp.int32),
-            pltpu.VMEM(right_side.shape, F32),
-            pltpu.VMEM(operator_top.shape, F32),
-            pltpu.SemaphoreType.DMA((rows + 5,)),
-        ]
-        + sums,
-        limit=14,
-    )
-    d1, r1 = call("step_first", step_first, [vec_top, vec_top], first, product, other, matrix)
+        scalars=(0,),
+        scratch=sums,
+    )
+    d1, r1 = call("step_first", step_first, [vec_top, vec_top], first, product, other, turned)
     other = flip(d1, 0)
-    product, send_mid, turned = call(
+    product, send_mid = call(
         "prepare_mid",
         prepare_mid,
-        [vec_top, mid_pieces, ((2 * n_top, n_top), BF16)],
+        [vec_top, mid_pieces],
         cols_mid,
         agg_mid,
         operator_mid,

time: 40.9 us -> 40.6 us (level)
  Pallas kernels: 9.54 us -> 8.1 us
  starting transfers between devices: 18.8 us -> 19.6 us
    pallas_call x16 -> x17, Pallas kernels: 9.54 us -> 8.1 us  [call(): pl.pallas_call(body, name=name, out_shape=[place(shape, dtype) for place,...]
    ppermute x10, starting transfers between devices: 18.8 us -> 19.6 us  [flip(): return lax.ppermute(value, ('gx', 'gy'), flips[level])]
    unnamed x10 -> x14, local copies, waits for them, and re-layouts: 1.27 us -> 1.28 us
  transfers between devices with their start and end apart: 10 -> 10, of which waited for: 5 -> 6; matrix products, arithmetic and copies ran while one was open for 2% -> 2% of each run, Pallas kernels for 22% -> 18%
where the time goes in v5:
time: 40.6 us; the launch traced here: 40.5 us
  starting transfers between devices  19.6 us (48%)
  waiting for transfers between devices  10.8 us (27%)
  Pallas kernels  8.1 us (20%)
  local copies, waits for them, and re-layouts  1.28 us (3%)
  between operations  0.74 us (2%)
    ppermute x10, starting transfers between devices, flip(): return lax.ppermute(value, ('gx', 'gy'), flips[level])  19.6 us
    ppermute x10, waiting for transfers between devices, flip(): return lax.ppermute(value, ('gx', 'gy'), flips[level])  10.8 us
    pallas_call x17, Pallas kernels, call(): pl.pallas_call(body, name=name, out_shape=[place(shape, dtype) for place,...  8.1 us
    unnamed x14, local copies, waits for them, and re-layouts  1.28 us
  transfers between devices with their start and end apart: 10, of which 6 were waited for; matrix products, arithmetic and copies ran while one was open for 2% of the time, Pallas kernels for 18%

profile of v5, /device:TPU:128, one launch (start us, length us, event | category | flops | bytes accessed | tf_op | source)
XLA Modules:
  0.0 40.5 jit_solution(2378428198095514673)
XLA Ops:
  0.7 3.1 %collective-permute-start = (f32[8,8,64]{2,1,0:T(8,128)}, f32[8,8,64]{2,1,0:T(8,128)S(1)}, u32[]{:S(2)}, u32[]{:S(2)}) collective-permute-start(f32[8,8,64]{2,1,0:T(8,128)} %side.1), channel_id=1, source_target_pairs={{0,16},{1,17},{2,18},{3,19},{4,20},{5,21},{6,22},{7,23},{8,24},{9,... | collective-permute-start | bytes 49160 | tf_op jit(solution)/shard_map/ppermute | solution.py:378
  3.8 0.8 %load_indices.1 = (s32[8,27]{1,0:T(8,128)S(4)}, s32[8]{0:T(128)S(4)}, s32[4,27]{1,0:T(4,128)S(4)}, s32[4]{0:T(128)S(4)}, s32[2,27]{1,0:T(2,128)S(4)}) custom-call(s32[8,27]{1,0:T(8,128)} %refs_0_.1, s32[8]{0:T(128)} %refs_1_.1, s32[4,27]{1,0:T(4,128)} %refs_2_.1, s32[4]{0:T(128)} %refs_3_.1, s32[2,27]{1,0:T(2,128)} %refs_4_.1), custom_call_target="tpu_custom_call" | custom-call | flops 20000000000 | tf_op jit(solution)/shard_map/load_indices/pallas_call | solution.py:40
  4.6 1.7 %prepare_top.1 = (bf16[512,2048]{1,0:T(8,128)(2,1)S(1)}, bf16[1024,512]{1,0:T(8,128)(2,1)S(1)}, f32[8,512]{1,0:T(8,128)S(1)}, f32[8,512]{1,0:T(8,128)S(1)}) custom-call(s32[8,27]{1,0:T(8,128)S(4)} %get-tuple-element.38.cols, f32[8,27,64,64]{3,2,1,0:T(8,128)S(1)} %copy-done.4, f32[8,8,64]{2,1,0:T(8,128)S(1)} %copy-done.5), custom_call_target="tpu_custom_call" | custom-call | flops 4000000000 | tf_op jit(solution)/shard_map/prepare_top/pallas_call | solution.py:40
  6.4 0.3 step_first.1
  6.7 3.0 %collective-permute-start.1 = (f32[8,512]{1,0:T(8,128)S(1)}, f32[8,512]{1,0:T(8,128)S(1)}, u32[]{:S(2)}, u32[]{:S(2)}) collective-permute-start(f32[8,512]{1,0:T(8,128)S(1)} %get-tuple-element.42.direction.old), channel_id=1, source_target_pairs={{0,16},{1,17},{2,18},{3,19},{4,20},{5,21},{6,22},{7,23},{8,24},{9,... | collective-permute-start | bytes 49160 | tf_op jit(solution)/shard_map/ppermute | solution.py:378
  9.7 0.7 %prepare_mid.1 = (f32[8,512]{1,0:T(8,128)S(1)}, f32[1160,128]{1,0:T(8,128)S(1)}) custom-call(s32[4,27]{1,0:T(4,128)S(4)} %get-tuple-element.44.cols, s32[4]{0:T(128)S(4)} %get-tuple-element.45.agg, f32[4,27,64,64]{3,2,1,0:T(8,128)S(1)} %copy-done, f32[4,64,64]{2,1,0:T(8,128)S(1)} %copy-done.3, f32[8,512]{1,0:T(8,128)S(1)} %get-tuple-element.42.direction.old, ...), custom_call_target="tpu_custom_call" | custom-call | flops 200000000 | tf_op jit(solution)/shard_map/prepare_mid/pallas_call | solution.py:40
  10.4 3.3 %collective-permute-start.6 = (f32[1160,128]{1,0:T(8,128)S(1)}, f32[1160,128]{1,0:T(8,128)S(1)}, u32[]{:S(2)}, u32[]{:S(2)}) collective-permute-start(f32[1160,128]{1,0:T(8,128)S(1)} %get-tuple-element.55.source), channel_id=1, source_target_pairs={{0,128},{1,129},{2,130},{3,131},{4,132},{5,133},{6,134},{7,135},{8... | collective-permute-start | bytes 1781768 | tf_op jit(solution)/shard_map/ppermute | solution.py:378
  13.7 0.2 step_second.1
  13.9 1.7 %collective-permute-start.2 = (f32[8,512]{1,0:T(8,128)S(1)}, f32[8,512]{1,0:T(8,128)S(1)}, u32[]{:S(2)}, u32[]{:S(2)}) collective-permute-start(f32[8,512]{1,0:T(8,128)S(1)} %get-tuple-element.51.direction), channel_id=1, source_target_pairs={{0,16},{1,17},{2,18},{3,19},{4,20},{5,21},{6,22},{7,23},{8,24},{9,... | collective-permute-start | bytes 49160 | tf_op jit(solution)/shard_map/ppermute | solution.py:378
  15.7 1.2 %prepare_low.1 = (f32[256,128]{1,0:T(8,128)S(1)}, bf16[512,1024]{1,0:T(8,128)(2,1)S(1)}, f32[8,512]{1,0:T(8,128)S(1)}, f32[8,256]{1,0:T(8,128)S(1)}, bf16[1024,256]{1,0:T(8,128)(2,1)S(1)}) custom-call(s32[2,27]{1,0:T(2,128)S(4)} %get-tuple-element.49.cols, s32[8]{0:T(128)S(4)} %get-tuple-element.50.agg, f32[2,27,64,64]{3,2,1,0:T(8,128)S(1)} %copy-done.1, ...), custom_call_target="tpu_custom_call" | custom-call | flops 200000000 | tf_op jit(solution)/shard_map/prepare_low/pallas_call | solution.py:40
  16.8 0.7 %collective-permute-start.4 = (f32[256,128]{1,0:T(8,128)S(1)}, f32[256,128]{1,0:T(8,128)S(1)}, u32[]{:S(2)}, u32[]{:S(2)}) collective-permute-start(f32[256,128]{1,0:T(8,128)S(1)} %get-tuple-element.59.own), channel_id=1, source_target_pairs={{0,8},{1,9},{2,10},{3,11},{4,12},{5,13},{6,14},{7,15},{8,0},{9,1},... | collective-permute-start | bytes 393224 | tf_op jit(solution)/shard_map/ppermute | solution.py:378
  17.5 1.8 %collective-permute-done.2.other = f32[8,512]{1,0:T(8,128)S(1)} collective-permute-done((f32[8,512]{1,0:T(8,128)S(1)}, f32[8,512]{1,0:T(8,128)S(1)}, u32[]{:S(2)}, u32[]{:S(2)}) %collective-permute-start.2) | collective-permute-done | bytes 16416 | tf_op jit(solution)/shard_map/ppermute | solution.py:378
  19.3 0.2 step_third.1
  19.5 1.7 %collective-permute-start.3 = (f32[8,256]{1,0:T(8,128)S(1)}, f32[8,256]{1,0:T(8,128)S(1)}, u32[]{:S(2)}, u32[]{:S(2)}) collective-permute-start(f32[8,256]{1,0:T(8,128)S(1)} %step_third.1), channel_id=1, source_target_pairs={{0,16},{1,17},{2,18},{3,19},{4,20},{5,21},{6,22},{7,23},{8,24},{9,... | collective-permute-start | bytes 24584 | tf_op jit(solution)/shard_map/ppermute | solution.py:378
  21.2 0.4 %restrict_own.1 = (f32[8,256]{1,0:T(8,128)S(1)}, f32[8,8,64]{2,1,0:T(8,128)S(1)}, bf16[1024,256]{1,0:T(8,128)(2,1)S(1)}, bf16[256,512]{1,0:T(8,128)(2,1)S(1)}) custom-call(f32[8,512]{1,0:T(8,128)S(1)} %get-tuple-element.53.known, f32[8,512]{1,0:T(8,128)S(1)} %collective-permute-done.2.other, bf16[1024,512]{1,0:T(8,128)(2,1)S(1)} %get-tuple-element.41.turned, ...), custom_call_target="tpu_custom_call" | custom-call | flops 200000000 | tf_op jit(solution)/shard_map/restrict_own/pallas_call | solution.py:40
  21.6 0.6 %copy.16 = f32[8,8,64]{2,1,0:T(8,128)} copy(f32[8,8,64]{2,1,0:T(8,128)S(1)} %get-tuple-element.75) | data formatting | bytes 32768
  22.3 0.2 compose_low.1.after.low
  22.5 2.2 %collective-permute-done.3.b = f32[8,256]{1,0:T(8,128)S(1)} collective-permute-done((f32[8,256]{1,0:T(8,128)S(1)}, f32[8,256]{1,0:T(8,128)S(1)}, u32[]{:S(2)}, u32[]{:S(2)}) %collective-permute-start.3) | collective-permute-done | bytes 8224 | tf_op jit(solution)/shard_map/ppermute | solution.py:378
  24.7 1.6 %collective-permute-start.7 = (f32[8,256]{1,0:T(8,128)S(1)}, f32[8,256]{1,0:T(8,128)S(1)}, u32[]{:S(2)}, u32[]{:S(2)}) collective-permute-start(f32[8,256]{1,0:T(8,128)S(1)} %add_mid.1.side.own), channel_id=1, source_target_pairs={{0,128},{1,129},{2,130},{3,131},{4,132},{5,133},{6,134},{7,135},{8... | collective-permute-start | bytes 24584 | tf_op jit(solution)/shard_map/ppermute | solution.py:378
  26.4 1.9 %collective-permute-start.5 = (f32[256,128]{1,0:T(8,128)S(1)}, f32[256,128]{1,0:T(8,128)S(1)}, u32[]{:S(2)}, u32[]{:S(2)}) collective-permute-start(f32[256,128]{1,0:T(8,128)S(1)} %get-tuple-element.61.own), channel_id=1, source_target_pairs={{0,128},{1,129},{2,130},{3,131},{4,132},{5,133},{6,134},{7,135},{8... | collective-permute-start | bytes 393224 | tf_op jit(solution)/shard_map/ppermute | solution.py:378
  28.4 0.3 join_other.1
  28.6 1.2 %collective-permute-done.7.other = f32[8,256]{1,0:T(8,128)S(1)} collective-permute-done((f32[8,256]{1,0:T(8,128)S(1)}, f32[8,256]{1,0:T(8,128)S(1)}, u32[]{:S(2)}, u32[]{:S(2)}) %collective-permute-start.7) | collective-permute-done | bytes 8224 | tf_op jit(solution)/shard_map/ppermute | solution.py:378
  29.8 0.8 %solve_mid.1 = (f32[8,256]{1,0:T(8,128)S(1)}, f32[8,256]{1,0:T(8,128)S(1)}) custom-call(f32[8,512]{1,0:T(8,128)S(1)} %get-tuple-element.64.product, f32[8,256]{1,0:T(8,128)S(1)} %add_mid.1.side.own, f32[8,256]{1,0:T(8,128)S(1)} %collective-permute-done.7.other, bf16[1024,256]{1,0:T(8,128)(2,1)S(1)} %get-tuple-element.60.matrix.matrix_own, ...), custom_call_target="tpu_custom_call" | custom-call | flops 20000000000 | tf_op jit(solution)/shard_map/solve_mid/pallas_call | solution.py:40
  30.6 0.7 %collective-permute-start.8 = (f32[8,256]{1,0:T(8,128)S(1)}, f32[8,256]{1,0:T(8,128)S(1)}, u32[]{:S(2)}, u32[]{:S(2)}) collective-permute-start(f32[8,256]{1,0:T(8,128)S(1)} %get-tuple-element.67.pair), channel_id=1, source_target_pairs={{0,8},{1,9},{2,10},{3,11},{4,12},{5,13},{6,14},{7,15},{8,0},{9,1},... | collective-permute-start | bytes 24584 | tf_op jit(solution)/shard_map/ppermute | solution.py:378
  31.3 1.6 %collective-permute-done.5.other = f32[256,128]{1,0:T(8,128)S(1)} collective-permute-done((f32[256,128]{1,0:T(8,128)S(1)}, f32[256,128]{1,0:T(8,128)S(1)}, u32[]{:S(2)}, u32[]{:S(2)}) %collective-permute-start.5) | collective-permute-done | bytes 131104 | tf_op jit(solution)/shard_map/ppermute | solution.py:378
  32.9 0.5 %compose_fixed.1 = (f32[8,256]{1,0:T(8,128)S(1)}, bf16[512,256]{1,0:T(8,128)(2,1)S(1)}) custom-call(f32[256,128]{1,0:T(8,128)S(1)} %get-tuple-element.61.own, f32[256,128]{1,0:T(8,128)S(1)} %collective-permute-done.5.other, bf16[256,512]{1,0:T(8,128)(2,1)S(1)} %get-tuple-element.62.transfer_own.transfer, f32[8,256]{1,0:T(8,128)S(1)} %get-tuple-element.67.pair, ...), custom_call_target="tpu_custom_call" | custom-call | flops 200000000 | tf_op jit(solution)/shard_map/compose_fixed/pallas_call | solution.py:40
  33.4 1.0 %collective-permute-done.8.other = f32[8,256]{1,0:T(8,128)S(1)} collective-permute-done((f32[8,256]{1,0:T(8,128)S(1)}, f32[8,256]{1,0:T(8,128)S(1)}, u32[]{:S(2)}, u32[]{:S(2)}) %collective-permute-start.8) | collective-permute-done | bytes 8224 | tf_op jit(solution)/shard_map/ppermute | solution.py:378
  34.5 1.9 %collective-permute-start.9 = (f32[8,256]{1,0:T(8,128)S(1)}, f32[8,256]{1,0:T(8,128)S(1)}, u32[]{:S(2)}, u32[]{:S(2)}) collective-permute-start(f32[8,256]{1,0:T(8,128)S(1)} %end_fixed.1.fixed), channel_id=1, source_target_pairs={{0,16},{1,17},{2,18},{3,19},{4,20},{5,21},{6,22},{7,23},{8,24},{9,... | collective-permute-start | bytes 24584 | tf_op jit(solution)/shard_map/ppermute | solution.py:378
  36.3 0.2 start_correction.1
  36.6 3.1 %collective-permute-done.9.other = f32[8,256]{1,0:T(8,128)S(1)} collective-permute-done((f32[8,256]{1,0:T(8,128)S(1)}, f32[8,256]{1,0:T(8,128)S(1)}, u32[]{:S(2)}, u32[]{:S(2)}) %collective-permute-start.9) | collective-permute-done | bytes 8224 | tf_op jit(solution)/shard_map/ppermute | solution.py:378
  39.7 0.2 end_correction.1
  39.9 0.6 %copy.15 = f32[8,8,64]{2,1,0:T(8,128)} copy(f32[8,8,64]{2,1,0:T(8,128)S(1)} %end_correction.1) | data formatting | bytes 32768
  (19 shorter events, 0.3 us)
Async XLA Ops:
  0.6 4.0 %copy-start.5 = (f32[8,8,64]{2,1,0:T(8,128)S(1)}, f32[8,8,64]{2,1,0:T(8,128)}, u32[]{:S(2)}) copy-start(f32[8,8,64]{2,1,0:T(8,128)} %side.1) | copy-start | bytes 49156
  0.6 4.0 %copy-start.4 = (f32[8,27,64,64]{3,2,1,0:T(8,128)S(1)}, f32[8,27,64,64]{3,2,1,0:T(8,128)}, u32[]{:S(2)}) copy-start(f32[8,27,64,64]{3,2,1,0:T(8,128)} %blocks.3) | copy-start | bytes 10616836
  0.7 5.7 %collective-permute-start = (f32[8,8,64]{2,1,0:T(8,128)}, f32[8,8,64]{2,1,0:T(8,128)S(1)}, u32[]{:S(2)}, u32[]{:S(2)}) collective-permute-start(f32[8,8,64]{2,1,0:T(8,128)} %side.1), channel_id=1, source_target_pairs={{0,16},{1,17},{2,18},{3,19},{4,20},{5,21},{6,22},{7,23},{8,24},{9,... | collective-permute-start | bytes 49160 | tf_op jit(solution)/shard_map/ppermute | solution.py:378
  6.4 3.3 %copy-start = (f32[4,27,64,64]{3,2,1,0:T(8,128)S(1)}, f32[4,27,64,64]{3,2,1,0:T(8,128)}, u32[]{:S(2)}) copy-start(f32[4,27,64,64]{3,2,1,0:T(8,128)} %blocks.4) | copy-start | bytes 5308420
  6.4 3.3 %copy-start.3 = (f32[4,64,64]{2,1,0:T(8,128)S(1)}, f32[4,64,64]{2,1,0:T(8,128)}, u32[]{:S(2)}) copy-start(f32[4,64,64]{2,1,0:T(8,128)} %prolong.2) | copy-start | bytes 196612
  6.7 7.0 %collective-permute-start.1 = (f32[8,512]{1,0:T(8,128)S(1)}, f32[8,512]{1,0:T(8,128)S(1)}, u32[]{:S(2)}, u32[]{:S(2)}) collective-permute-start(f32[8,512]{1,0:T(8,128)S(1)} %get-tuple-element.42.direction.old), channel_id=1, source_target_pairs={{0,16},{1,17},{2,18},{3,19},{4,20},{5,21},{6,22},{7,23},{8,24},{9,... | collective-permute-start | bytes 49160 | tf_op jit(solution)/shard_map/ppermute | solution.py:378
  10.4 18.0 %collective-permute-start.6 = (f32[1160,128]{1,0:T(8,128)S(1)}, f32[1160,128]{1,0:T(8,128)S(1)}, u32[]{:S(2)}, u32[]{:S(2)}) collective-permute-start(f32[1160,128]{1,0:T(8,128)S(1)} %get-tuple-element.55.source), channel_id=1, source_target_pairs={{0,128},{1,129},{2,130},{3,131},{4,132},{5,133},{6,134},{7,135},{8... | collective-permute-start | bytes 1781768 | tf_op jit(solution)/shard_map/ppermute | solution.py:378
  13.7 2.0 %copy-start.1 = (f32[2,27,64,64]{3,2,1,0:T(8,128)S(1)}, f32[2,27,64,64]{3,2,1,0:T(8,128)}, u32[]{:S(2)}) copy-start(f32[2,27,64,64]{3,2,1,0:T(8,128)} %blocks.5) | copy-start | bytes 2654212
  13.7 2.0 %copy-start.2 = (f32[8,64,64]{2,1,0:T(8,128)S(1)}, f32[8,64,64]{2,1,0:T(8,128)}, u32[]{:S(2)}) copy-start(f32[8,64,64]{2,1,0:T(8,128)} %prolong.3) | copy-start | bytes 393220
  13.9 5.4 %collective-permute-start.2 = (f32[8,512]{1,0:T(8,128)S(1)}, f32[8,512]{1,0:T(8,128)S(1)}, u32[]{:S(2)}, u32[]{:S(2)}) collective-permute-start(f32[8,512]{1,0:T(8,128)S(1)} %get-tuple-element.51.direction), channel_id=1, source_target_pairs={{0,16},{1,17},{2,18},{3,19},{4,20},{5,21},{6,22},{7,23},{8,24},{9,... | collective-permute-start | bytes 49160 | tf_op jit(solution)/shard_map/ppermute | solution.py:378
  16.8 5.4 %collective-permute-start.4 = (f32[256,128]{1,0:T(8,128)S(1)}, f32[256,128]{1,0:T(8,128)S(1)}, u32[]{:S(2)}, u32[]{:S(2)}) collective-permute-start(f32[256,128]{1,0:T(8,128)S(1)} %get-tuple-element.59.own), channel_id=1, source_target_pairs={{0,8},{1,9},{2,10},{3,11},{4,12},{5,13},{6,14},{7,15},{8,0},{9,1},... | collective-permute-start | bytes 393224 | tf_op jit(solution)/shard_map/ppermute | solution.py:378
  19.5 5.2 %collective-permute-start.3 = (f32[8,256]{1,0:T(8,128)S(1)}, f32[8,256]{1,0:T(8,128)S(1)}, u32[]{:S(2)}, u32[]{:S(2)}) collective-permute-start(f32[8,256]{1,0:T(8,128)S(1)} %step_third.1), channel_id=1, source_target_pairs={{0,16},{1,17},{2,18},{3,19},{4,20},{5,21},{6,22},{7,23},{8,24},{9,... | collective-permute-start | bytes 24584 | tf_op jit(solution)/shard_map/ppermute | solution.py:378
  24.7 5.2 %collective-permute-start.7 = (f32[8,256]{1,0:T(8,128)S(1)}, f32[8,256]{1,0:T(8,128)S(1)}, u32[]{:S(2)}, u32[]{:S(2)}) collective-permute-start(f32[8,256]{1,0:T(8,128)S(1)} %add_mid.1.side.own), channel_id=1, source_target_pairs={{0,128},{1,129},{2,130},{3,131},{4,132},{5,133},{6,134},{7,135},{8... | collective-permute-start | bytes 24584 | tf_op jit(solution)/shard_map/ppermute | solution.py:378
  26.4 6.5 %collective-permute-start.5 = (f32[256,128]{1,0:T(8,128)S(1)}, f32[256,128]{1,0:T(8,128)S(1)}, u32[]{:S(2)}, u32[]{:S(2)}) collective-permute-start(f32[256,128]{1,0:T(8,128)S(1)} %get-tuple-element.61.own), channel_id=1, source_target_pairs={{0,128},{1,129},{2,130},{3,131},{4,132},{5,133},{6,134},{7,135},{8... | collective-permute-start | bytes 393224 | tf_op jit(solution)/shard_map/ppermute | solution.py:378
  30.6 3.7 %collective-permute-start.8 = (f32[8,256]{1,0:T(8,128)S(1)}, f32[8,256]{1,0:T(8,128)S(1)}, u32[]{:S(2)}, u32[]{:S(2)}) collective-permute-start(f32[8,256]{1,0:T(8,128)S(1)} %get-tuple-element.67.pair), channel_id=1, source_target_pairs={{0,8},{1,9},{2,10},{3,11},{4,12},{5,13},{6,14},{7,15},{8,0},{9,1},... | collective-permute-start | bytes 24584 | tf_op jit(solution)/shard_map/ppermute | solution.py:378
  34.5 5.2 %collective-permute-start.9 = (f32[8,256]{1,0:T(8,128)S(1)}, f32[8,256]{1,0:T(8,128)S(1)}, u32[]{:S(2)}, u32[]{:S(2)}) collective-permute-start(f32[8,256]{1,0:T(8,128)S(1)} %end_fixed.1.fixed), channel_id=1, source_target_pairs={{0,16},{1,17},{2,18},{3,19},{4,20},{5,21},{6,22},{7,23},{8,24},{9,... | collective-permute-start | bytes 24584 | tf_op jit(solution)/shard_map/ppermute | solution.py:378

commit v6 on v5

--- a/solution.py
+++ b/solution.py
@@ -246,7 +246,7 @@
     r = known[...] - apply_turned(other[...], turned[...])
     own_part[...] = apply_n(r, transfer_top[:, : transfer_top.shape[1] // 2])
     unpack(r, out)
-    join_mid(source, matrix, transfer, False)
+    join_mid(source, matrix, transfer, 0)
 
 
 def add_mid(a, b, after, out):
@@ -254,19 +254,20 @@
 
 
 def own_mid(side, matrix, low, product, low_out):
-    product[...] = apply_turned(side[...], matrix[: matrix.shape[0] // 2])
+    product[...] = apply_turned(side[...], matrix[: matrix.shape[0] // 2, : matrix.shape[1] // 2])
 
 
 def join_mid(source, matrix, transfer, turn):
-    n_mid = matrix.shape[1]
+    n_mid = matrix.shape[1] // 2
     rows = n_mid // N
     half = rows // 2
+    here = slice(turn * n_mid, (turn + 1) * n_mid)
     for c in range(rows):
         to = (c + half) % rows if turn else c
         high, low = split(source[c * n_mid : (c + 1) * n_mid].T)
         base = (to // half) * 2 * n_mid + (to % half) * 2 * N
-        matrix[base : base + 2 * N] = high
-        matrix[base + n_mid : base + n_mid + 2 * N] = low
+        matrix[base : base + 2 * N, here] = high
+        matrix[base + n_mid : base + n_mid + 2 * N, here] = low
     at = rows * n_mid
     joined = at + half * N
     for b in range(rows):
@@ -277,15 +278,21 @@
         for p, piece in enumerate(pieces):
             put = (p + half // 2) % half if turn else p
             high, low = split(piece)
-            matrix_rows = slice(b * N, (b + 1) * N)
+            matrix_rows = slice(turn * n_mid + b * N, turn * n_mid + (b + 1) * N)
             transfer[matrix_rows, put * 2 * N : (put + 1) * 2 * N] = high
             transfer[matrix_rows, n_mid + put * 2 * N : n_mid + (put + 1) * 2 * N] = low
 
 
-def join_other(source, side, own, matrix, transfer, product):
-    join_mid(source, matrix, transfer, True)
-    other = apply_turned(side[...], matrix[: matrix.shape[0] // 2])
+def join_other(source, side, own, matrix_in, transfer_in, matrix, transfer, product, last):
+    join_mid(source, matrix, transfer, 1)
+    other = apply_turned(side[...], matrix[: matrix.shape[0] // 2, matrix.shape[1] // 2 :])
     product[...] = jnp.concatenate([own[...], other], axis=1)
+    n_mid = matrix.shape[1] // 2
+    for at in (0, 2 * n_mid):
+        here = matrix[at : at + n_mid], matrix[at + n_mid : at + 2 * n_mid]
+        high, low = split(multiply(here, (transfer[:, :n_mid], transfer[:, n_mid:])))
+        last[at : at + n_mid] = high
+        last[at + n_mid : at + 2 * n_mid] = low
 
 
 def multiply(a, b):
@@ -316,7 +323,8 @@
     near, far = [], []
     for at, source in ((0, own), (1, other)):
         solve = jnp.concatenate([source[:half], source[half:]], axis=1)
-        here = transfer[:, at * half : (at + 1) * half], transfer[:, width + at * half : width + (at + 1) * half]
+        rows = slice(0, fine.shape[1])
+        here = tuple(transfer[rows, low + at * half : low + (at + 1) * half] for low in (0, width))
         product = multiply(here, split(solve))
         near.append(product[:, :half])
         far.append(product[:, half:])
@@ -326,24 +334,23 @@
     matrix[width:] = low
 
 
-def solve_mid(product, own, other, matrix_own, matrix_other, transfer_own, transfer_other, low_pair, solution):
+def solve_mid(product, own, other, matrix, transfer, last, low_pair, solution):
     half = own.shape[1]
-    mid = matrix_own.shape[0] // 2
-
-    def pair_product(value, columns):
-        return jnp.concatenate(
-            [apply_turned(value, matrix_own[columns]), apply_turned(value, matrix_other[columns])], axis=1
-        )
+
+    def pair_product(value, by):
+        near, far = stack(value[:, :half]), stack(value[:, half:])
+        both = jnp.concatenate([near, near, far, far], axis=1)
+        return fold(jnp.dot(both, by[...], preferred_element_type=F32))
 
     d = jnp.concatenate([own[...], other[...]], axis=1)
-    r = d - (d + product[...] + pair_product(other[...], slice(mid, 2 * mid)))
+    r = d - (d + product[...] + apply_turned(other[...], matrix[matrix.shape[0] // 2 :]))
     x = d[:, :half]
-    for step in range(2):
-        d = W[step][0] * d + W[step][1] * r
-        x = x + d[:, :half]
-        r = r - (d + pair_product(d[:, :half], slice(0, mid)) + pair_product(d[:, half:], slice(mid, 2 * mid)))
-    solution[...] = x
-    low_pair[...] = apply_n(r[:, :half], transfer_own[...]) + apply_n(r[:, half:], transfer_other[...])
+    d = W[0][0] * d + W[0][1] * r
+    x = x + d[:, :half]
+    r = r - (d + pair_product(d, matrix))
+    d = W[1][0] * d + W[1][1] * r
+    solution[...] = x + d[:, :half]
+    low_pair[...] = apply_n(r - d, transfer[...]) - pair_product(d, last)
 
 
 def end_fixed(partial, other, matrix, fixed):
@@ -443,10 +450,10 @@
     low_arrived = flip(send_low, 2)
     (other_part,) = call("step_third", step_third, [vec_mid], part, other, restrict)
     arrived = flip(other_part, 0)
-    own_part, smoothed_blocks, mid_own, transfer_own = call(
+    own_part, smoothed_blocks, mid_matrix, mid_transfer = call(
         "restrict_own",
         restrict_own,
-        [vec_mid, ((rows, S, N), F32), ((4 * n_mid, n_mid), BF16), ((n_mid, 4 * n_low), BF16)],
+        [vec_mid, ((rows, S, N), F32), ((4 * n_mid, 2 * n_mid), BF16), ((2 * n_mid, 4 * n_low), BF16)],
         known,
         other,
         turned,
@@ -456,15 +463,18 @@
     (solve_own,) = call("compose_low", compose_low, [low_pieces], send_low, low_arrived)
     (mid_side,) = call("add_mid", add_mid, [vec_mid], own_part, arrived, solve_own)
     other = flip(mid_side, 1)
-    product, solve_own = call("own_mid", own_mid, [vec_mid, low_pieces], mid_side, mid_own, solve_own, aliases={2: 1})
+    product, solve_own = call("own_mid", own_mid, [vec_mid, low_pieces], mid_side, mid_matrix, solve_own, aliases={2: 1})
     solve_other = flip(solve_own, 1)
-    mid_other, transfer_other, product = call(
+    mid_matrix, mid_transfer, product, last = call(
         "join_other",
         join_other,
-        [((4 * n_mid, n_mid), BF16), ((n_mid, 4 * n_low), BF16), vec_top],
+        [((4 * n_mid, 2 * n_mid), BF16), ((2 * n_mid, 4 * n_low), BF16), vec_top, ((4 * n_mid, n_mid), BF16)],
         mid_arrived,
         mid_side,
         product,
+        mid_matrix,
+        mid_transfer,
+        aliases={3: 0, 4: 1},
     )
     low_pair, x_mid = call(
         "solve_mid",
@@ -473,10 +483,9 @@
         product,
         mid_side,
         other,
-        mid_own,
-        mid_other,
-        transfer_own,
-        transfer_other,
+        mid_matrix,
+        mid_transfer,
+        last,
     )
     other = flip(low_pair, 2)
     partial, fixing = call(
@@ -485,7 +494,7 @@
         [vec_mid, ((4 * n_low, n_mid), BF16)],
         solve_own,
         solve_other,
-        transfer_own,
+        mid_transfer,
         low_pair,
         x_mid,
     )

time: 40.6 us -> 40.5 us (level)
  waiting for transfers between devices: 10.8 us -> 10.2 us
    ppermute x10, waiting for transfers between devices: 10.8 us -> 10.2 us  [flip(): return lax.ppermute(value, ('gx', 'gy'), flips[level])]
  transfers between devices with their start and end apart: 10 -> 10, of which waited for: 6 -> 6; matrix products, arithmetic and copies ran while one was open for 2% -> 2% of each run, Pallas kernels for 18% -> 19%
where the time goes in v6:
time: 40.5 us; the launch traced here: 40.4 us
  starting transfers between devices  19.7 us (49%)
  waiting for transfers between devices  10.2 us (25%)
  Pallas kernels  8.48 us (21%)
  local copies, waits for them, and re-layouts  1.28 us (3%)
  between operations  0.74 us (2%)
    ppermute x10, starting transfers between devices, flip(): return lax.ppermute(value, ('gx', 'gy'), flips[level])  19.7 us
    ppermute x10, waiting for transfers between devices, flip(): return lax.ppermute(value, ('gx', 'gy'), flips[level])  10.2 us
    pallas_call x17, Pallas kernels, call(): pl.pallas_call(body, name=name, out_shape=[place(shape, dtype) for place,...  8.48 us
    unnamed x14, local copies, waits for them, and re-layouts  1.28 us
  transfers between devices with their start and end apart: 10, of which 6 were waited for; matrix products, arithmetic and copies ran while one was open for 2% of the time, Pallas kernels for 19%

profile of v6, /device:TPU:128, one launch (start us, length us, event | category | flops | bytes accessed | tf_op | source)
XLA Modules:
  0.0 40.4 jit_solution(11376790669846850816)
XLA Ops:
  0.7 3.1 %collective-permute-start = (f32[8,8,64]{2,1,0:T(8,128)}, f32[8,8,64]{2,1,0:T(8,128)S(1)}, u32[]{:S(2)}, u32[]{:S(2)}) collective-permute-start(f32[8,8,64]{2,1,0:T(8,128)} %side.1), channel_id=1, source_target_pairs={{0,16},{1,17},{2,18},{3,19},{4,20},{5,21},{6,22},{7,23},{8,24},{9,... | collective-permute-start | bytes 49160 | tf_op jit(solution)/shard_map/ppermute | solution.py:385
  3.8 0.8 %load_indices.1 = (s32[8,27]{1,0:T(8,128)S(4)}, s32[8]{0:T(128)S(4)}, s32[4,27]{1,0:T(4,128)S(4)}, s32[4]{0:T(128)S(4)}, s32[2,27]{1,0:T(2,128)S(4)}) custom-call(s32[8,27]{1,0:T(8,128)} %refs_0_.1, s32[8]{0:T(128)} %refs_1_.1, s32[4,27]{1,0:T(4,128)} %refs_2_.1, s32[4]{0:T(128)} %refs_3_.1, s32[2,27]{1,0:T(2,128)} %refs_4_.1), custom_call_target="tpu_custom_call" | custom-call | flops 20000000000 | tf_op jit(solution)/shard_map/load_indices/pallas_call | solution.py:40
  4.6 1.7 %prepare_top.1 = (bf16[512,2048]{1,0:T(8,128)(2,1)S(1)}, bf16[1024,512]{1,0:T(8,128)(2,1)S(1)}, f32[8,512]{1,0:T(8,128)S(1)}, f32[8,512]{1,0:T(8,128)S(1)}) custom-call(s32[8,27]{1,0:T(8,128)S(4)} %get-tuple-element.39.cols, f32[8,27,64,64]{3,2,1,0:T(8,128)S(1)} %copy-done.4, f32[8,8,64]{2,1,0:T(8,128)S(1)} %copy-done.5), custom_call_target="tpu_custom_call" | custom-call | flops 4000000000 | tf_op jit(solution)/shard_map/prepare_top/pallas_call | solution.py:40
  6.4 0.3 step_first.1
  6.7 3.0 %collective-permute-start.1 = (f32[8,512]{1,0:T(8,128)S(1)}, f32[8,512]{1,0:T(8,128)S(1)}, u32[]{:S(2)}, u32[]{:S(2)}) collective-permute-start(f32[8,512]{1,0:T(8,128)S(1)} %get-tuple-element.43.direction.old), channel_id=1, source_target_pairs={{0,16},{1,17},{2,18},{3,19},{4,20},{5,21},{6,22},{7,23},{8,24},{9,... | collective-permute-start | bytes 49160 | tf_op jit(solution)/shard_map/ppermute | solution.py:385
  9.7 0.7 %prepare_mid.1 = (f32[8,512]{1,0:T(8,128)S(1)}, f32[1160,128]{1,0:T(8,128)S(1)}) custom-call(s32[4,27]{1,0:T(4,128)S(4)} %get-tuple-element.45.cols, s32[4]{0:T(128)S(4)} %get-tuple-element.46.agg, f32[4,27,64,64]{3,2,1,0:T(8,128)S(1)} %copy-done, f32[4,64,64]{2,1,0:T(8,128)S(1)} %copy-done.3, f32[8,512]{1,0:T(8,128)S(1)} %get-tuple-element.43.direction.old, ...), custom_call_target="tpu_custom_call" | custom-call | flops 200000000 | tf_op jit(solution)/shard_map/prepare_mid/pallas_call | solution.py:40
  10.4 3.3 %collective-permute-start.6 = (f32[1160,128]{1,0:T(8,128)S(1)}, f32[1160,128]{1,0:T(8,128)S(1)}, u32[]{:S(2)}, u32[]{:S(2)}) collective-permute-start(f32[1160,128]{1,0:T(8,128)S(1)} %get-tuple-element.56.source), channel_id=1, source_target_pairs={{0,128},{1,129},{2,130},{3,131},{4,132},{5,133},{6,134},{7,135},{8... | collective-permute-start | bytes 1781768 | tf_op jit(solution)/shard_map/ppermute | solution.py:385
  13.7 0.2 step_second.1
  13.9 1.7 %collective-permute-start.2 = (f32[8,512]{1,0:T(8,128)S(1)}, f32[8,512]{1,0:T(8,128)S(1)}, u32[]{:S(2)}, u32[]{:S(2)}) collective-permute-start(f32[8,512]{1,0:T(8,128)S(1)} %get-tuple-element.52.direction), channel_id=1, source_target_pairs={{0,16},{1,17},{2,18},{3,19},{4,20},{5,21},{6,22},{7,23},{8,24},{9,... | collective-permute-start | bytes 49160 | tf_op jit(solution)/shard_map/ppermute | solution.py:385
  15.7 1.2 %prepare_low.1 = (f32[256,128]{1,0:T(8,128)S(1)}, bf16[512,1024]{1,0:T(8,128)(2,1)S(1)}, f32[8,512]{1,0:T(8,128)S(1)}, f32[8,256]{1,0:T(8,128)S(1)}, bf16[1024,256]{1,0:T(8,128)(2,1)S(1)}) custom-call(s32[2,27]{1,0:T(2,128)S(4)} %get-tuple-element.50.cols, s32[8]{0:T(128)S(4)} %get-tuple-element.51.agg, f32[2,27,64,64]{3,2,1,0:T(8,128)S(1)} %copy-done.1, ...), custom_call_target="tpu_custom_call" | custom-call | flops 200000000 | tf_op jit(solution)/shard_map/prepare_low/pallas_call | solution.py:40
  16.8 0.7 %collective-permute-start.4 = (f32[256,128]{1,0:T(8,128)S(1)}, f32[256,128]{1,0:T(8,128)S(1)}, u32[]{:S(2)}, u32[]{:S(2)}) collective-permute-start(f32[256,128]{1,0:T(8,128)S(1)} %get-tuple-element.60.own), channel_id=1, source_target_pairs={{0,8},{1,9},{2,10},{3,11},{4,12},{5,13},{6,14},{7,15},{8,0},{9,1},... | collective-permute-start | bytes 393224 | tf_op jit(solution)/shard_map/ppermute | solution.py:385
  17.5 1.8 %collective-permute-done.2.other = f32[8,512]{1,0:T(8,128)S(1)} collective-permute-done((f32[8,512]{1,0:T(8,128)S(1)}, f32[8,512]{1,0:T(8,128)S(1)}, u32[]{:S(2)}, u32[]{:S(2)}) %collective-permute-start.2) | collective-permute-done | bytes 16416 | tf_op jit(solution)/shard_map/ppermute | solution.py:385
  19.3 0.2 step_third.1
  19.5 1.7 %collective-permute-start.3 = (f32[8,256]{1,0:T(8,128)S(1)}, f32[8,256]{1,0:T(8,128)S(1)}, u32[]{:S(2)}, u32[]{:S(2)}) collective-permute-start(f32[8,256]{1,0:T(8,128)S(1)} %step_third.1), channel_id=1, source_target_pairs={{0,16},{1,17},{2,18},{3,19},{4,20},{5,21},{6,22},{7,23},{8,24},{9,... | collective-permute-start | bytes 24584 | tf_op jit(solution)/shard_map/ppermute | solution.py:385
  21.2 0.4 %restrict_own.1 = (f32[8,256]{1,0:T(8,128)S(1)}, f32[8,8,64]{2,1,0:T(8,128)S(1)}, bf16[1024,512]{1,0:T(8,128)(2,1)S(1)}, bf16[512,512]{1,0:T(8,128)(2,1)S(1)}) custom-call(f32[8,512]{1,0:T(8,128)S(1)} %get-tuple-element.54.known, f32[8,512]{1,0:T(8,128)S(1)} %collective-permute-done.2.other, bf16[1024,512]{1,0:T(8,128)(2,1)S(1)} %get-tuple-element.42.turned, ...), custom_call_target="tpu_custom_call" | custom-call | flops 200000000 | tf_op jit(solution)/shard_map/restrict_own/pallas_call | solution.py:40
  21.7 0.6 %copy.20 = f32[8,8,64]{2,1,0:T(8,128)} copy(f32[8,8,64]{2,1,0:T(8,128)S(1)} %get-tuple-element.77) | data formatting | bytes 32768
  22.3 0.2 compose_low.1.after.low
  22.5 2.2 %collective-permute-done.3.b = f32[8,256]{1,0:T(8,128)S(1)} collective-permute-done((f32[8,256]{1,0:T(8,128)S(1)}, f32[8,256]{1,0:T(8,128)S(1)}, u32[]{:S(2)}, u32[]{:S(2)}) %collective-permute-start.3) | collective-permute-done | bytes 8224 | tf_op jit(solution)/shard_map/ppermute | solution.py:385
  24.7 1.6 %collective-permute-start.7 = (f32[8,256]{1,0:T(8,128)S(1)}, f32[8,256]{1,0:T(8,128)S(1)}, u32[]{:S(2)}, u32[]{:S(2)}) collective-permute-start(f32[8,256]{1,0:T(8,128)S(1)} %add_mid.1.side.own), channel_id=1, source_target_pairs={{0,128},{1,129},{2,130},{3,131},{4,132},{5,133},{6,134},{7,135},{8... | collective-permute-start | bytes 24584 | tf_op jit(solution)/shard_map/ppermute | solution.py:385
  26.4 1.9 %collective-permute-start.5 = (f32[256,128]{1,0:T(8,128)S(1)}, f32[256,128]{1,0:T(8,128)S(1)}, u32[]{:S(2)}, u32[]{:S(2)}) collective-permute-start(f32[256,128]{1,0:T(8,128)S(1)} %get-tuple-element.62.own), channel_id=1, source_target_pairs={{0,128},{1,129},{2,130},{3,131},{4,132},{5,133},{6,134},{7,135},{8... | collective-permute-start | bytes 393224 | tf_op jit(solution)/shard_map/ppermute | solution.py:385
  28.4 0.7 %join_other.1 = (bf16[1024,512]{1,0:T(8,128)(2,1)S(1)}, bf16[512,512]{1,0:T(8,128)(2,1)S(1)}, f32[8,512]{1,0:T(8,128)S(1)}, bf16[1024,256]{1,0:T(8,128)(2,1)S(1)}) custom-call(f32[1160,128]{1,0:T(8,128)S(1)} %collective-permute-done.6.source, f32[8,256]{1,0:T(8,128)S(1)} %add_mid.1.side.own, ...), custom_call_target="tpu_custom_call", output_to_operand_aliasing={{0}: (3, {}), {1}: (4, {})} | custom-call | flops 200000000 | tf_op jit(solution)/shard_map/join_other/pallas_call | solution.py:40
  29.1 0.7 %collective-permute-done.7.other = f32[8,256]{1,0:T(8,128)S(1)} collective-permute-done((f32[8,256]{1,0:T(8,128)S(1)}, f32[8,256]{1,0:T(8,128)S(1)}, u32[]{:S(2)}, u32[]{:S(2)}) %collective-permute-start.7) | collective-permute-done | bytes 8224 | tf_op jit(solution)/shard_map/ppermute | solution.py:385
  29.8 0.7 %solve_mid.1 = (f32[8,256]{1,0:T(8,128)S(1)}, f32[8,256]{1,0:T(8,128)S(1)}) custom-call(f32[8,512]{1,0:T(8,128)S(1)} %get-tuple-element.66.product, f32[8,256]{1,0:T(8,128)S(1)} %add_mid.1.side.own, f32[8,256]{1,0:T(8,128)S(1)} %collective-permute-done.7.other, bf16[1024,512]{1,0:T(8,128)(2,1)S(1)} %get-tuple-element.67.matrix, ...), custom_call_target="tpu_custom_call" | custom-call | flops 20000000000 | tf_op jit(solution)/shard_map/solve_mid/pallas_call | solution.py:40
  30.5 0.7 %collective-permute-start.8 = (f32[8,256]{1,0:T(8,128)S(1)}, f32[8,256]{1,0:T(8,128)S(1)}, u32[]{:S(2)}, u32[]{:S(2)}) collective-permute-start(f32[8,256]{1,0:T(8,128)S(1)} %get-tuple-element.69.pair), channel_id=1, source_target_pairs={{0,8},{1,9},{2,10},{3,11},{4,12},{5,13},{6,14},{7,15},{8,0},{9,1},... | collective-permute-start | bytes 24584 | tf_op jit(solution)/shard_map/ppermute | solution.py:385
  31.2 1.7 %collective-permute-done.5.other = f32[256,128]{1,0:T(8,128)S(1)} collective-permute-done((f32[256,128]{1,0:T(8,128)S(1)}, f32[256,128]{1,0:T(8,128)S(1)}, u32[]{:S(2)}, u32[]{:S(2)}) %collective-permute-start.5) | collective-permute-done | bytes 131104 | tf_op jit(solution)/shard_map/ppermute | solution.py:385
  32.9 0.5 %compose_fixed.1 = (f32[8,256]{1,0:T(8,128)S(1)}, bf16[512,256]{1,0:T(8,128)(2,1)S(1)}) custom-call(f32[256,128]{1,0:T(8,128)S(1)} %get-tuple-element.62.own, f32[256,128]{1,0:T(8,128)S(1)} %collective-permute-done.5.other, bf16[512,512]{1,0:T(8,128)(2,1)S(1)} %get-tuple-element.65.transfer, f32[8,256]{1,0:T(8,128)S(1)} %get-tuple-element.69.pair, ...), custom_call_target="tpu_custom_call" | custom-call | flops 200000000 | tf_op jit(solution)/shard_map/compose_fixed/pallas_call | solution.py:40
  33.4 0.8 %collective-permute-done.8.other = f32[8,256]{1,0:T(8,128)S(1)} collective-permute-done((f32[8,256]{1,0:T(8,128)S(1)}, f32[8,256]{1,0:T(8,128)S(1)}, u32[]{:S(2)}, u32[]{:S(2)}) %collective-permute-start.8) | collective-permute-done | bytes 8224 | tf_op jit(solution)/shard_map/ppermute | solution.py:385
  34.3 2.0 %collective-permute-start.9 = (f32[8,256]{1,0:T(8,128)S(1)}, f32[8,256]{1,0:T(8,128)S(1)}, u32[]{:S(2)}, u32[]{:S(2)}) collective-permute-start(f32[8,256]{1,0:T(8,128)S(1)} %end_fixed.1.fixed), channel_id=1, source_target_pairs={{0,16},{1,17},{2,18},{3,19},{4,20},{5,21},{6,22},{7,23},{8,24},{9,... | collective-permute-start | bytes 24584 | tf_op jit(solution)/shard_map/ppermute | solution.py:385
  36.3 0.2 start_correction.1
  36.6 2.9 %collective-permute-done.9.other = f32[8,256]{1,0:T(8,128)S(1)} collective-permute-done((f32[8,256]{1,0:T(8,128)S(1)}, f32[8,256]{1,0:T(8,128)S(1)}, u32[]{:S(2)}, u32[]{:S(2)}) %collective-permute-start.9) | collective-permute-done | bytes 8224 | tf_op jit(solution)/shard_map/ppermute | solution.py:385
  39.5 0.2 end_correction.1
  39.7 0.6 %copy.19 = f32[8,8,64]{2,1,0:T(8,128)} copy(f32[8,8,64]{2,1,0:T(8,128)S(1)} %end_correction.1) | data formatting | bytes 32768
  (19 shorter events, 0.3 us)
Async XLA Ops:
  0.6 4.0 %copy-start.5 = (f32[8,8,64]{2,1,0:T(8,128)S(1)}, f32[8,8,64]{2,1,0:T(8,128)}, u32[]{:S(2)}) copy-start(f32[8,8,64]{2,1,0:T(8,128)} %side.1) | copy-start | bytes 49156
  0.6 4.0 %copy-start.4 = (f32[8,27,64,64]{3,2,1,0:T(8,128)S(1)}, f32[8,27,64,64]{3,2,1,0:T(8,128)}, u32[]{:S(2)}) copy-start(f32[8,27,64,64]{3,2,1,0:T(8,128)} %blocks.3) | copy-start | bytes 10616836
  0.7 5.7 %collective-permute-start = (f32[8,8,64]{2,1,0:T(8,128)}, f32[8,8,64]{2,1,0:T(8,128)S(1)}, u32[]{:S(2)}, u32[]{:S(2)}) collective-permute-start(f32[8,8,64]{2,1,0:T(8,128)} %side.1), channel_id=1, source_target_pairs={{0,16},{1,17},{2,18},{3,19},{4,20},{5,21},{6,22},{7,23},{8,24},{9,... | collective-permute-start | bytes 49160 | tf_op jit(solution)/shard_map/ppermute | solution.py:385
  6.4 3.3 %copy-start = (f32[4,27,64,64]{3,2,1,0:T(8,128)S(1)}, f32[4,27,64,64]{3,2,1,0:T(8,128)}, u32[]{:S(2)}) copy-start(f32[4,27,64,64]{3,2,1,0:T(8,128)} %blocks.4) | copy-start | bytes 5308420
  6.4 3.3 %copy-start.3 = (f32[4,64,64]{2,1,0:T(8,128)S(1)}, f32[4,64,64]{2,1,0:T(8,128)}, u32[]{:S(2)}) copy-start(f32[4,64,64]{2,1,0:T(8,128)} %prolong.2) | copy-start | bytes 196612
  6.7 7.0 %collective-permute-start.1 = (f32[8,512]{1,0:T(8,128)S(1)}, f32[8,512]{1,0:T(8,128)S(1)}, u32[]{:S(2)}, u32[]{:S(2)}) collective-permute-start(f32[8,512]{1,0:T(8,128)S(1)} %get-tuple-element.43.direction.old), channel_id=1, source_target_pairs={{0,16},{1,17},{2,18},{3,19},{4,20},{5,21},{6,22},{7,23},{8,24},{9,... | collective-permute-start | bytes 49160 | tf_op jit(solution)/shard_map/ppermute | solution.py:385
  10.4 18.0 %collective-permute-start.6 = (f32[1160,128]{1,0:T(8,128)S(1)}, f32[1160,128]{1,0:T(8,128)S(1)}, u32[]{:S(2)}, u32[]{:S(2)}) collective-permute-start(f32[1160,128]{1,0:T(8,128)S(1)} %get-tuple-element.56.source), channel_id=1, source_target_pairs={{0,128},{1,129},{2,130},{3,131},{4,132},{5,133},{6,134},{7,135},{8... | collective-permute-start | bytes 1781768 | tf_op jit(solution)/shard_map/ppermute | solution.py:385
  13.7 2.0 %copy-start.1 = (f32[2,27,64,64]{3,2,1,0:T(8,128)S(1)}, f32[2,27,64,64]{3,2,1,0:T(8,128)}, u32[]{:S(2)}) copy-start(f32[2,27,64,64]{3,2,1,0:T(8,128)} %blocks.5) | copy-start | bytes 2654212
  13.7 2.0 %copy-start.2 = (f32[8,64,64]{2,1,0:T(8,128)S(1)}, f32[8,64,64]{2,1,0:T(8,128)}, u32[]{:S(2)}) copy-start(f32[8,64,64]{2,1,0:T(8,128)} %prolong.3) | copy-start | bytes 393220
  13.9 5.4 %collective-permute-start.2 = (f32[8,512]{1,0:T(8,128)S(1)}, f32[8,512]{1,0:T(8,128)S(1)}, u32[]{:S(2)}, u32[]{:S(2)}) collective-permute-start(f32[8,512]{1,0:T(8,128)S(1)} %get-tuple-element.52.direction), channel_id=1, source_target_pairs={{0,16},{1,17},{2,18},{3,19},{4,20},{5,21},{6,22},{7,23},{8,24},{9,... | collective-permute-start | bytes 49160 | tf_op jit(solution)/shard_map/ppermute | solution.py:385
  16.8 5.4 %collective-permute-start.4 = (f32[256,128]{1,0:T(8,128)S(1)}, f32[256,128]{1,0:T(8,128)S(1)}, u32[]{:S(2)}, u32[]{:S(2)}) collective-permute-start(f32[256,128]{1,0:T(8,128)S(1)} %get-tuple-element.60.own), channel_id=1, source_target_pairs={{0,8},{1,9},{2,10},{3,11},{4,12},{5,13},{6,14},{7,15},{8,0},{9,1},... | collective-permute-start | bytes 393224 | tf_op jit(solution)/shard_map/ppermute | solution.py:385
  19.5 5.2 %collective-permute-start.3 = (f32[8,256]{1,0:T(8,128)S(1)}, f32[8,256]{1,0:T(8,128)S(1)}, u32[]{:S(2)}, u32[]{:S(2)}) collective-permute-start(f32[8,256]{1,0:T(8,128)S(1)} %step_third.1), channel_id=1, source_target_pairs={{0,16},{1,17},{2,18},{3,19},{4,20},{5,21},{6,22},{7,23},{8,24},{9,... | collective-permute-start | bytes 24584 | tf_op jit(solution)/shard_map/ppermute | solution.py:385
  24.7 5.2 %collective-permute-start.7 = (f32[8,256]{1,0:T(8,128)S(1)}, f32[8,256]{1,0:T(8,128)S(1)}, u32[]{:S(2)}, u32[]{:S(2)}) collective-permute-start(f32[8,256]{1,0:T(8,128)S(1)} %add_mid.1.side.own), channel_id=1, source_target_pairs={{0,128},{1,129},{2,130},{3,131},{4,132},{5,133},{6,134},{7,135},{8... | collective-permute-start | bytes 24584 | tf_op jit(solution)/shard_map/ppermute | solution.py:385
  26.4 6.5 %collective-permute-start.5 = (f32[256,128]{1,0:T(8,128)S(1)}, f32[256,128]{1,0:T(8,128)S(1)}, u32[]{:S(2)}, u32[]{:S(2)}) collective-permute-start(f32[256,128]{1,0:T(8,128)S(1)} %get-tuple-element.62.own), channel_id=1, source_target_pairs={{0,128},{1,129},{2,130},{3,131},{4,132},{5,133},{6,134},{7,135},{8... | collective-permute-start | bytes 393224 | tf_op jit(solution)/shard_map/ppermute | solution.py:385
  30.5 3.7 %collective-permute-start.8 = (f32[8,256]{1,0:T(8,128)S(1)}, f32[8,256]{1,0:T(8,128)S(1)}, u32[]{:S(2)}, u32[]{:S(2)}) collective-permute-start(f32[8,256]{1,0:T(8,128)S(1)} %get-tuple-element.69.pair), channel_id=1, source_target_pairs={{0,8},{1,9},{2,10},{3,11},{4,12},{5,13},{6,14},{7,15},{8,0},{9,1},... | collective-permute-start | bytes 24584 | tf_op jit(solution)/shard_map/ppermute | solution.py:385
  34.3 5.2 %collective-permute-start.9 = (f32[8,256]{1,0:T(8,128)S(1)}, f32[8,256]{1,0:T(8,128)S(1)}, u32[]{:S(2)}, u32[]{:S(2)}) collective-permute-start(f32[8,256]{1,0:T(8,128)S(1)} %end_fixed.1.fixed), channel_id=1, source_target_pairs={{0,16},{1,17},{2,18},{3,19},{4,20},{5,21},{6,22},{7,23},{8,24},{9,... | collective-permute-start | bytes 24584 | tf_op jit(solution)/shard_map/ppermute | solution.py:385
